TPU v7x, 256 devices: a whole 4x4x8 slice. The times are simulated.
256 devices in a mesh: dp: 64 (over y_lo, x, z), mp: 4 (over y_hi, core).
Axes of the slice: x: 4, y: 4 (y_hi: 2, y_lo: 2; y = y_hi * 2 + y_lo), z: 8, core: 2. Of those that a mesh axis runs over, the one named last changes fastest.
Arguments:
- mixer_vectors: bfloat16 [98304, 4096], P('dp', 'mp'), may hold values from -16 to 16
- upstream_adjoint: bfloat16 [98304, 2, 1792], P('dp', None, 'mp'), may hold values from -6 to 6
- relative_benefit: float32 [98304], P('dp'), may hold values from -4 to 4
- present_policy_logit: float32 [98304], P('dp'), may hold values from -1.5 to 0
- behaviour_policy_logit: float32 [98304], P('dp'), may hold values from -1.5 to 0
- retained_entries: int32 [64, 768], P('dp'), may hold values from 0 to 1535, as said below
- tallies: int32 [64], P('dp'), may hold values from 1 to 768, as said below
- keeper_slot: int32 [32], replicated, may hold values from 0 to 31, each once
Outputs:
- update: bfloat16 [64, 128, 1792], P('dp', None, 'mp')
- gradient: float32 [64, 128, 1792], P('dp', None, 'mp')
Inputs may be any that keep to these rules, and one draw needn't show every extreme that they name: `retained_entries`: the 768 slots of one shard name distinct rows of that shard. `tallies`: some shard has all 768 slots live. `keeper_slot`: every owner slot is taken by one head.
All inputs are finite; a program needn't handle non-finite values.
Results may differ from a plain program's by a relative error of at most 0.0046.
The roundings to bfloat16 on the way count: a program that leaves them out, or rounds other values in their place, can miss the bound.
Values may be sent and summed in bfloat16 or wider, within the bound.
No kernel may reach another device: no remote copies, remote signals or barrier semaphores. Data moves between devices by JAX's collectives and lax.ppermute only.
A program may use at most 192 MiB of HBM per device.

v0:
```python
import math

import jax
import jax.numpy as jnp
from jax import lax
from jax.sharding import PartitionSpec as P

DHALF = 1792


coeff_a = 3.4445
coeff_b = -4.775
coeff_c = 2.0315
norm_eps = 1e-06
highest_precision_mode = lax.Precision.HIGHEST


def partner_2(value, axis, apart):
    mask = 2**apart
    pairs = [(source, source ^ mask) for source in range(lax.axis_size(axis))]
    return lax.ppermute(value, axis, pairs)


def half_bit():
    return lax.axis_size("dp").bit_length() - 2


def total_gram(blocks):
    partial_sum = jnp.einsum("nrq,ntq->nrt", blocks, blocks, precision=highest_precision_mode)
    partner = partner_2(partial_sum.astype(jnp.bfloat16), "dp", half_bit()).astype(
        partial_sum.dtype
    )
    return lax.psum(partial_sum + partner, "mp")


def total_squares(blocks):
    partial_sum = jnp.sum(blocks * blocks, axis=(1, 2))
    partner = partner_2(partial_sum, "dp", half_bit())
    return lax.psum(partial_sum + partner, "mp")


def to_owner_order(blocks, source):
    distribute_rows = lax.all_to_all(blocks, "dp", split_axis=1, concat_axis=0, tiled=True)
    ordered = jnp.take(distribute_rows, source, axis=0)
    return lax.all_to_all(ordered, "dp", split_axis=0, concat_axis=1, tiled=True)


def to_holder_order(blocks, source):
    distribute_rows = lax.all_to_all(blocks, "dp", split_axis=1, concat_axis=0, tiled=True)
    ordered = jnp.take(distribute_rows, source, axis=0)
    return lax.all_to_all(ordered, "dp", split_axis=0, concat_axis=1, tiled=True)


def make_term(values, scaled, head_of, half_of, row_count):
    head_size = values.shape[2]
    nblocks = row_count // head_size
    block_ids = jnp.arange(nblocks, dtype=jnp.int32)
    head_ids = jnp.take(head_of, block_ids)
    half_ids = jnp.take(half_of, block_ids)
    picked_values = jnp.take(values, head_ids, axis=1)
    picked_grads = jnp.take(scaled, half_ids, axis=1)
    product = jnp.einsum(
        "cnr,cnq->nrq", picked_values, picked_grads, preferred_element_type=jnp.float32
    )
    return product.reshape(nblocks * head_size, scaled.shape[2])


def on_device(
    mixer_vectors,
    upstream_adjoint,
    relative_benefit,
    present_policy_logit,
    behaviour_policy_logit,
    retained_entries,
    tallies,
    keeper_slot,
):
    kept_samples = retained_entries[0]
    capacity = kept_samples.shape[0]
    active = jnp.arange(capacity, dtype=jnp.int32) < tallies[0]
    weight = jnp.where(
        active,
        relative_benefit[kept_samples]
        * jnp.exp(present_policy_logit[kept_samples] - behaviour_policy_logit[kept_samples]),
        0.0,
    )
    scaled = (weight[:, None, None] * upstream_adjoint[kept_samples].astype(jnp.float32)).astype(
        jnp.bfloat16
    )
    values = lax.all_gather(mixer_vectors[kept_samples], "mp", axis=1, tiled=True)
    heads_total = keeper_slot.shape[0]
    head_size = values.shape[1] // heads_total
    values = values.reshape(capacity, heads_total, head_size)
    positions = jnp.arange(2 * heads_total, dtype=jnp.int32)
    inverse = (
        jnp.zeros((heads_total,), jnp.int32)
        .at[keeper_slot]
        .set(jnp.arange(heads_total, dtype=jnp.int32))
    )
    halves = positions // heads_total
    slot_ids = positions % heads_total
    local_rows = 2 * heads_total // lax.axis_size("dp") * head_size
    summed = lax.psum_scatter(
        make_term(values, scaled, slot_ids, halves, local_rows * lax.axis_size("dp")),
        "dp",
        scatter_dimension=0,
        tiled=True,
    )
    owned_grads = to_owner_order(
        summed.reshape(-1, head_size, summed.shape[1]), halves * heads_total + inverse[slot_ids]
    )
    norm_scale = jnp.sqrt(total_squares(owned_grads)) + norm_eps
    iterate = owned_grads / norm_scale[:, None, None]
    gram_sum = total_gram(iterate)
    for sweep in range(2):
        if sweep > 0:
            gram_sum = total_gram(iterate)
        poly_mix = coeff_b * gram_sum + coeff_c * jnp.einsum(
            "nrs,nst->nrt", gram_sum, gram_sum, precision=highest_precision_mode
        )
        iterate = coeff_a * iterate + jnp.einsum(
            "nrs,nsq->nrq", poly_mix, iterate, precision=highest_precision_mode
        )
    update = (0.2 * math.sqrt(2 * DHALF) * iterate).astype(jnp.bfloat16)
    returned = to_holder_order(update, jnp.concatenate([keeper_slot, keeper_slot + heads_total]))
    return (returned, owned_grads)


def solution(mesh):
    return jax.shard_map(
        on_device,
        mesh=mesh,
        in_specs=(
            P("dp", "mp"),
            P("dp", None, "mp"),
            P("dp"),
            P("dp"),
            P("dp"),
            P("dp", None),
            P("dp"),
            P(),
        ),
        out_specs=(P("dp", None, "mp"), P("dp", None, "mp")),
        check_vma=False,
    )
```

profile of v0, /device:TPU:8, one launch (start us, length us, event | category | flops | bytes accessed | tf_op | source)
XLA Modules:
  0.0 685.7 jit_solution(6945192708124122802)
XLA Ops:
  7.2 0.8 fusion.29
  8.1 1.0 copy-done
  9.1 3.6 gather_fusion.1
  12.7 4.5 gather_fusion.3
  17.2 4.5 gather_fusion.4
  21.7 4.5 gather_fusion.5
  26.8 7.4 %copy.38 = bf16[1536,2,448]{2,1,0:T(2,128)(2,1)S(1)} copy(bf16[1536,2,448]{0,2,1:T(8,128)(2,1)} %param.11) | data formatting | bytes 5505024 | tf_op args[1]
  34.2 5.5 gather_fusion.6
  39.7 3.7 copy.39
  43.5 0.8 gather_fusion.10
  44.2 0.8 gather_fusion.11
  45.3 15.5 %gather_fusion.7 = bf16[64,768,448]{1,2,0:T(8,128)(2,1)} fusion(bf16[768,2,448]{0,2,1:T(8,128)(2,1)S(1)} %multiply_convert_fusion, s32[1024]{0:T(1024)S(1)} %pad_clamp_fusion.3), kind=kCustom, calls=%fused_computation.9 | custom fusion | bytes 88080640 | tf_op jit(solution)/shard_map/jit(_take)/gather | solution.py:61
  60.9 6.9 %all-gather.3.cloned.1.call-done = bf16[768,4096]{1,0:T(8,128)(2,1)} async-done(((bf16[768,1024]{1,0:T(8,128)(2,1)}), bf16[768,4096]{1,0:T(8,128)(2,1)}) %all-gather.3.cloned.1.call-update) | async-done | bytes 6291472 | tf_op jit(solution)/shard_map/all_gather | solution.py:90
  67.8 7.1 %copy_bitcast_fusion.1 = bf16[768,32,128]{2,0,1:T(8,128)(2,1)} fusion(bf16[768,4096]{1,0:T(8,128)(2,1)} %all-gather.3.cloned.1.call-done), kind=kLoop, calls=%fused_computation.23 | loop fusion | bytes 12582912 | tf_op jit(solution)/shard_map/reshape | solution.py:93
  74.9 9.6 %gather_fusion.2 = bf16[64,768,128]{2,1,0:T(8,128)(2,1)} fusion(bf16[768,32,128]{2,0,1:T(8,128)(2,1)} %copy_bitcast_fusion.1, s32[1024]{0:T(1024)S(1)} %pad_clamp_fusion.2), kind=kCustom, calls=%fused_computation.4 | custom fusion | bytes 25166080 | tf_op jit(solution)/shard_map/jit(_take)/gather | solution.py:60
  84.5 28.1 %fusion.8 = f32[64,56,8,128]{3,2,1,0:T(8,128)} fusion(bf16[64,768,128]{2,1,0:T(8,128)(2,1)} %gather_fusion.2, pred[64]{0:T(512)(128)(4,1)S(1)} %get-tuple-element.20, bf16[64,768,448]{1,2,0:T(8,128)(2,1)} %gather_fusion.7, pred[64]{0:T(512)(128)(4,1)S(1)} %get-tuple-element.13), kind=kOutput, calls=%fused_computation.22 | convolution fusion | flops 5665456128 | bytes 71303296 | tf_op jit(solution)/shard_map/cnr,cnq->nrq/dot_general | solution.py:62
  112.6 12.3 %copy.52 = f32[64,56,8,128]{3,2,0,1:T(8,128)} copy(f32[64,56,8,128]{3,2,1,0:T(8,128)} %fusion.8) | data formatting | bytes 29360128 | tf_op jit(solution)/shard_map/reshape | solution.py:65
  124.9 0.6 copy-done.7
  125.5 0.9 scatter_custom_fusion
  126.4 0.8 gather_fusion
  127.2 347.6 %reduce-scatter.2.cloned.1.call-done = f32[128,448]{0,1:T(8,128)} async-done(((f32[8192,448]{0,1:T(8,128)}), f32[128,448]{0,1:T(8,128)}) %reduce-scatter.2.cloned.1.call-update) | async-done | bytes 229392 | tf_op jit(solution)/shard_map/reduce_scatter | solution.py:103
  474.8 1.8 copy.41
  476.6 7.3 %all-to-all-start = ((f32[1,128,448]{2,0,1:T(1,128)}), f32[1,128,448]{2,0,1:T(1,128)S(1)}, u32[]{:S(2)}, u32[]{:S(2)}) async-start(f32[1,128,448]{2,0,1:T(1,128)} %copy.41), calls=%async_computation.1 | async-start | bytes 524288 | tf_op jit(solution)/shard_map/all_to_all | solution.py:43
  484.0 11.8 %all-to-all-done = f32[1,128,448]{2,0,1:T(1,128)S(1)} async-done(((f32[1,128,448]{2,0,1:T(1,128)}), f32[1,128,448]{2,0,1:T(1,128)S(1)}, u32[]{:S(2)}, u32[]{:S(2)}) %all-to-all-start) | async-done | bytes 229408 | tf_op jit(solution)/shard_map/all_to_all | solution.py:43
  495.9 1.4 reduce.2
  497.3 1.8 all_to_all.17
  499.1 1.8 gather_fusion.8
  501.1 16.5 %all_to_all.48 = f32[64,2,448]{2,1,0:T(2,128)S(1)} all-to-all(f32[64,2,448]{2,1,0:T(2,128)S(1)} %broadcast_select_fusion), channel_id=1, replica_groups=mesh['dp'=64,'mp'=4] {'dp'}, dimensions={0} | all-to-all | bytes 458752 | tf_op jit(solution)/shard_map/all_to_all | solution.py:45
  517.6 0.9 multiply_reduce_fusion
  518.4 0.6 collective-permute-start
  519.0 3.1 collective-permute-done
  523.4 7.7 %psum.21 = f32[1]{0:T(128)} all-reduce(f32[1]{0:T(128)S(6)} %add.174), channel_id=1, replica_groups=mesh['dp'=64,'mp'=4] {'mp'}, use_global_device_ids=true, to_apply=%region_3.5 | all-reduce | flops 1 | bytes 8 | tf_op jit(solution)/shard_map/psum | solution.py:39
  531.8 1.0 broadcast_multiply_fusion
  532.8 1.1 div.42
  533.9 0.4 fusion.41
  534.3 0.7 collective-permute-start.1
  534.9 3.3 collective-permute-done.1
  538.3 0.6 bitcast_add_fusion.1
  539.0 1.8 mul.78
  540.8 1.8 copy.42
  542.6 36.1 %all-reduce.3.cloned.1.call-done = f32[1,128,128]{2,1,0:T(8,128)} async-done(((f32[1,128,128]{2,1,0:T(8,128)}), f32[1,128,128]{2,1,0:T(8,128)}) %all-reduce.3.cloned.1.call-update) | async-done | bytes 65552 | tf_op jit(solution)/shard_map/psum | solution.py:33
  578.7 1.1 fusion.18
  579.8 1.6 convolution_add_fusion.1
  581.4 0.7 copy-done.6
  582.1 0.6 fusion.42
  582.7 1.5 collective-permute-start.2
  584.2 2.5 collective-permute-done.2
  586.7 0.6 bitcast_add_fusion
  587.4 44.5 %all-reduce.5.cloned.1.call-done = f32[1,128,128]{2,1,0:T(8,128)} async-done(((f32[1,128,128]{2,1,0:T(8,128)}), f32[1,128,128]{2,1,0:T(8,128)}) %all-reduce.5.cloned.1.call-update) | async-done | bytes 65552 | tf_op jit(solution)/shard_map/psum | solution.py:33
  631.8 1.1 fusion.17
  632.9 1.4 fusion.16
  634.6 0.5 broadcast.340
  635.1 1.4 reduce.6
  636.6 0.7 reshape.444
  637.3 11.6 %all-to-all-start.2 = ((bf16[64,2,448]{2,1,0:T(2,128)(2,1)}), bf16[64,2,448]{2,1,0:T(2,128)(2,1)S(1)}, u32[]{:S(2)}, u32[]{:S(2)}) async-start(bf16[64,2,448]{2,1,0:T(2,128)(2,1)} %reshape.444), calls=%async_computation.3 | async-start | bytes 262144 | tf_op jit(solution)/shard_map/all_to_all | solution.py:49
  649.0 10.9 %all-to-all-done.2 = bf16[64,2,448]{2,1,0:T(2,128)(2,1)S(1)} async-done(((bf16[64,2,448]{2,1,0:T(2,128)(2,1)}), bf16[64,2,448]{2,1,0:T(2,128)(2,1)S(1)}, u32[]{:S(2)}, u32[]{:S(2)}) %all-to-all-start.2) | async-done | bytes 114720 | tf_op jit(solution)/shard_map/all_to_all | solution.py:49
  660.1 0.7 bitcast_reduce_fusion
  660.9 0.8 gather_fusion.9
  661.7 0.9 broadcast_select_fusion.1
  662.6 5.1 all-to-all-start.3
  667.7 1.1 all_to_all.43
  668.8 0.8 copy.45
  669.6 8.6 %all-to-all-done.3 = bf16[64,2,448]{2,1,0:T(2,128)(2,1)S(1)} async-done(((bf16[64,2,448]{2,1,0:T(2,128)(2,1)}), bf16[64,2,448]{2,1,0:T(2,128)(2,1)S(1)}, u32[]{:S(2)}, u32[]{:S(2)}) %all-to-all-start.3) | async-done | bytes 114720 | tf_op jit(solution)/shard_map/all_to_all | solution.py:51
  678.4 0.8 copy.44
  (48 shorter events, 1.5 us)
Async XLA Ops:
  7.2 1.9 copy-start
  7.2 60.6 %all-gather.3.cloned.1.call-start = ((), (), s32[]{:S(2)}) async-start(), calls=%async_computation.8 | async-start | bytes 7864320 | tf_op jit(solution)/shard_map/all_gather | solution.py:90
  9.1 3.6 copy-start.2
  12.6 4.6 copy-start.3
  12.6 9.0 %copy-start.4 = (f32[1536]{0:T(1024)S(1)}, f32[1536]{0:T(1024)}, u32[]{:S(2)}) copy-start(f32[1536]{0:T(1024)} %param.14) | copy-start | bytes 18436
  12.7 462.2 %reduce-scatter.2.cloned.1.call-start = ((), (), s32[]{:S(2)}) async-start(), calls=%async_computation.5 | async-start | bytes 14909440 | tf_op jit(solution)/shard_map/reduce_scatter | solution.py:103
  124.9 0.7 copy-start.7
  476.6 19.3 %all-to-all-start = ((f32[1,128,448]{2,0,1:T(1,128)}), f32[1,128,448]{2,0,1:T(1,128)S(1)}, u32[]{:S(2)}, u32[]{:S(2)}) async-start(f32[1,128,448]{2,0,1:T(1,128)} %copy.41), calls=%async_computation.1 | async-start | bytes 524288 | tf_op jit(solution)/shard_map/all_to_all | solution.py:43
  484.0 94.8 %all-reduce.3.cloned.1.call-start = ((), (), s32[]{:S(2)}) async-start(), calls=%async_computation.6 | async-start | bytes 131072 | tf_op jit(solution)/shard_map/psum | solution.py:33
  495.9 183.3 %copy-start.1 = (bf16[1536,1024]{1,0:T(8,128)(2,1)S(1)}, bf16[1536,1024]{1,0:T(8,128)(2,1)}, u32[]{:S(2)}) copy-start(bf16[1536,1024]{1,0:T(8,128)(2,1)} %param.10) | copy-start | bytes 9437188
  517.6 15.2 %copy-start.5 = (f32[64,2,448]{2,1,0:T(2,128)}, f32[64,2,448]{2,1,0:T(2,128)S(1)}, u32[]{:S(2)}) copy-start(f32[64,2,448]{2,1,0:T(2,128)S(1)} %all_to_all.48) | copy-start | bytes 688132
  518.4 3.6 collective-permute-start
  534.3 4.0 collective-permute-start.1
  538.9 92.9 %all-reduce.5.cloned.1.call-start = ((), (), s32[]{:S(2)}) async-start(), calls=%async_computation.7 | async-start | bytes 131072 | tf_op jit(solution)/shard_map/psum | solution.py:33
  581.4 0.7 copy-start.6
  582.7 4.0 collective-permute-start.2
  637.3 22.6 %all-to-all-start.2 = ((bf16[64,2,448]{2,1,0:T(2,128)(2,1)}), bf16[64,2,448]{2,1,0:T(2,128)(2,1)S(1)}, u32[]{:S(2)}, u32[]{:S(2)}) async-start(bf16[64,2,448]{2,1,0:T(2,128)(2,1)} %reshape.444), calls=%async_computation.3 | async-start | bytes 262144 | tf_op jit(solution)/shard_map/all_to_all | solution.py:49
  662.6 15.7 %all-to-all-start.3 = ((bf16[64,2,448]{2,1,0:T(2,128)(2,1)}), bf16[64,2,448]{2,1,0:T(2,128)(2,1)S(1)}, u32[]{:S(2)}, u32[]{:S(2)}) async-start(bf16[64,2,448]{2,1,0:T(2,128)(2,1)} %broadcast_select_fusion.1), calls=%async_computation.4 | async-start | bytes 262144 | tf_op jit(solution)/shard_map/all_to_all | solution.py:51
Sparse Core Ops, SparseCore 0:
  12.8 54.9 all-gather.2
  125.0 349.7 reduce-scatter.1
  539.1 39.5 all-reduce.2
  587.5 44.2 all-reduce.4
where the time goes:
time: 687 us; the launch traced here: 686 us
  waiting for transfers between devices  475 us (69%)
  local copies, waits for them, and re-layouts  99.7 us (15%)
  matrix products  34.3 us (5%)
  starting transfers between devices  26.9 us (4%)
  blocking collectives  24.2 us (4%)
  between operations  16.8 us (2%)
  other arithmetic  8.35 us (1%)
    reduce_scatter x1, waiting for transfers between devices, on_device(): lax.psum_scatter(make_term(values, scaled, slot_ids, halves, local_rows *...  348 us
    psum x2, waiting for transfers between devices, total_gram(): return lax.psum(partial_sum + partner, 'mp')  80.6 us
    dot_general x1, matrix products, make_term(): jnp.einsum('cnr,cnq->nrq', picked_values, picked_grads, preferred_element...  28.1 us
    all_to_all x1, blocking collectives, to_owner_order(): lax.all_to_all(ordered, 'dp', split_axis=0, concat_axis=1, tiled=True)  16.5 us
    gather x1, local copies, waits for them, and re-layouts, make_term(): picked_grads = jnp.take(scaled, half_ids, axis=1)  15.5 us
  transfers between devices with their start and end apart: 10, of which 10 were waited for; matrix products, arithmetic and copies ran while one was open for 8% of the time, Pallas kernels for 0%

commit v1 on v0

v1 whole, which is shorter than its diff:
```python
import math

import jax
import jax.numpy as jnp
import numpy as np
from jax import lax
from jax.experimental import pallas as pl
from jax.experimental.pallas import tpu as pltpu
from jax.sharding import Mesh
from jax.sharding import PartitionSpec as P

DHALF = 1792

coeff_a = 3.4445
coeff_b = -4.775
coeff_c = 2.0315
norm_eps = 1e-06
highest_precision_mode = lax.Precision.HIGHEST

YL, X, Z, YH, C = 2, 4, 8, 2, 2
NAMES = ("yl", "x", "z", "yh", "c")
VIA_PARTNER = 256


def ring_pairs(flip):
    def index(y):
        return (y % 2) * 2 + y // 2

    return [(index(y), index(y ^ flip)) for y in range(4)]


def over_y(value, flip):
    return lax.ppermute(value, ("yl", "yh"), ring_pairs(flip))


def shift(value, axis, size, step):
    return lax.ppermute(value, axis, [(i, (i + step) % size) for i in range(size)])


def odd_to_even(value, step):
    pairs = [
        (x * 2 + c, (x + step) % X * 2 + c) for x in range(X) for c in range(C) if (x + c) % 2
    ]
    return lax.ppermute(value, ("x", "c"), pairs)


def even_to_odd_core(value):
    pairs = [(x * 2 + c, x * 2 + 1 - c) for x in range(X) for c in range(C) if not (x + c) % 2]
    return lax.ppermute(value, ("x", "c"), pairs)


def partial_kernel(plan, s_ref, own_ref, e1_ref, oa_ref, ob_ref, e3_ref, *out_refs):
    cap = own_ref.shape[0]
    first = oa_ref.shape[0]
    for slot, out_ref in enumerate(out_refs):
        chunk, side = plan[slot], plan[4 + slot]

        def term(lo, hi, v_ref, side=side):
            return jnp.dot(s_ref[side, :, lo:hi], v_ref[...], preferred_element_type=jnp.float32)

        @pl.when(chunk == 0)
        def _(out_ref=out_ref, term=term):
            out_ref[...] = (term(0, cap, own_ref) + term(cap, 2 * cap, e1_ref)).astype(
                out_ref.dtype
            )

        @pl.when(chunk == 1)
        def _(out_ref=out_ref, term=term):
            out_ref[...] = (
                term(0, first, oa_ref)
                + term(first, cap, ob_ref)
                + term(cap, 2 * cap, e3_ref)
            ).astype(out_ref.dtype)


def partials(plan, s_all, own, e1, oa, ob, e3):
    cap, cols = own.shape
    q = s_all.shape[1]
    tile = 256

    def v_spec(v):
        return pl.BlockSpec((v.shape[0], tile), lambda i, plan: (0, i))

    return pl.pallas_call(
        partial_kernel,
        grid_spec=pltpu.PrefetchScalarGridSpec(
            num_scalar_prefetch=1,
            grid=(cols // tile,),
            in_specs=[pl.BlockSpec(s_all.shape, lambda i, plan: (0, 0, 0))]
            + [v_spec(v) for v in (own, e1, oa, ob, e3)],
            out_specs=[pl.BlockSpec((q, tile), lambda i, plan: (0, i))] * 4,
        ),
        out_shape=[jax.ShapeDtypeStruct((q, cols), jnp.bfloat16)] * 4,
        compiler_params=pltpu.CompilerParams(vmem_limit_bytes=40 * 2**20),
        cost_estimate=pl.CostEstimate(
            flops=8 * q * 2 * cap * cols, bytes_accessed=12 * 2**20, transcendentals=0
        ),
    )(plan, s_all, own, e1, oa, ob, e3)


def polar_kernel(scale, g_ref, *refs):
    out_ref = refs[-1]
    gram = refs[0][...]
    for ref in refs[1:-1]:
        gram = gram + ref[...]

    def mul(a, b):
        return jnp.dot(a, b, precision=highest_precision_mode, preferred_element_type=jnp.float32)

    n = gram.shape[0]
    eye = (
        lax.broadcasted_iota(jnp.int32, (n, n), 0) == lax.broadcasted_iota(jnp.int32, (n, n), 1)
    ).astype(jnp.float32)
    norm = jnp.sqrt(jnp.sum(gram * eye, keepdims=True)) + norm_eps
    a1 = gram / norm / norm
    p1 = coeff_a * eye + coeff_b * a1 + coeff_c * mul(a1, a1)
    a2 = mul(mul(p1, a1), p1)
    p2 = coeff_a * eye + coeff_b * a2 + coeff_c * mul(a2, a2)
    mix = mul(p2, p1) * (scale / norm)
    out_ref[...] = lax.dot_general(
        mix,
        g_ref[...],
        (((1,), (1,)), ((), ())),
        precision=highest_precision_mode,
        preferred_element_type=jnp.float32,
    ).astype(out_ref.dtype)


def polar(g, grams):
    q, n = g.shape
    return pl.pallas_call(
        lambda *refs: polar_kernel(0.2 * math.sqrt(2 * DHALF), *refs),
        out_shape=jax.ShapeDtypeStruct((n, q), jnp.bfloat16),
        compiler_params=pltpu.CompilerParams(vmem_limit_bytes=16 * 2**20),
    )(g, *grams)


def on_device(
    mixer_vectors,
    upstream_adjoint,
    relative_benefit,
    present_policy_logit,
    behaviour_policy_logit,
    retained_entries,
    tallies,
    keeper_slot,
):
    bf16, f32 = jnp.bfloat16, jnp.float32
    yl, x, z = lax.axis_index("yl"), lax.axis_index("x"), lax.axis_index("z")
    yh, core = lax.axis_index("yh"), lax.axis_index("c")
    kept = retained_entries[0]
    cap = kept.shape[0]
    rows = mixer_vectors.shape[0]
    q = upstream_adjoint.shape[2]

    own = mixer_vectors.at[kept].get(mode="promise_in_bounds")
    e3 = over_y(own, 3)
    e1 = over_y(own, 1)
    oa = over_y(e3[:VIA_PARTNER], 1)
    ob = over_y(e1[VIA_PARTNER:], 3)

    pick = lax.broadcasted_iota(jnp.int32, (rows, cap), 0) == kept[None, :]
    weight_all = relative_benefit * jnp.exp(present_policy_logit - behaviour_policy_logit)
    weight = jnp.sum(jnp.where(pick, weight_all[:, None], 0.0), axis=0)
    weight = jnp.where(jnp.arange(cap, dtype=jnp.int32) < tallies[0], weight, 0.0)
    adjoint = upstream_adjoint.transpose(1, 2, 0).reshape(2 * q, rows)
    picked = jnp.dot(adjoint, pick.astype(bf16), preferred_element_type=f32)
    scaled = (weight[None, :] * picked).astype(bf16).reshape(2, q, cap)
    s_keep = lax.dynamic_index_in_dim(scaled, yl, 0, keepdims=False)
    s_send = lax.dynamic_index_in_dim(scaled, 1 - yl, 0, keepdims=False)
    s_own = jnp.concatenate([s_keep, over_y(s_send, 1)], axis=1)
    s_all = jnp.stack([s_own, shift(s_own, "c", C, 1)])

    odd = (x + core) % 2
    near = jnp.where((x + odd) % X // 2 == yh, 0, 1)
    far = 1 - near
    chunk = jnp.where(
        odd == 1, jnp.stack([near, far, near, far]), jnp.stack([far, far, near, near])
    )
    side = jnp.where(odd == 1, jnp.array([1, 0, 0, 1]), jnp.array([0, 1, 1, 0]))
    plan = jnp.concatenate([chunk, side]).astype(jnp.int32)
    t0, t1, t2, t3 = partials(plan, s_all, own, e1, oa, ob, e3)
    ra = shift(t0, "x", X, 1)
    rb = shift(t1, "x", X, -1)
    u2 = t2.astype(f32) + ra.astype(f32)
    u3 = t3.astype(f32) + rb.astype(f32)
    rp = odd_to_even(u2.astype(bf16), 1)
    rm = odd_to_even(u3.astype(bf16), -1)
    keep = (u3 + rp.astype(f32)).astype(bf16)
    cross = even_to_odd_core((u2 + rm.astype(f32)).astype(bf16))
    mine = jnp.where(odd == 1, cross, keep)

    head = mine.shape[1] // Z

    def block(step):
        return lax.dynamic_slice_in_dim(mine, (z + step) % Z * head, head, 1)

    g = block(0).astype(f32)
    for got in [shift(block(d), "z", Z, d) for d in (4, 3, 5, 2, 6, 1, 7)]:
        g = g + got.astype(f32)

    gram = lax.dot_general(
        g, g, (((0,), (0,)), ((), ())), precision=highest_precision_mode,
        preferred_element_type=f32,
    )
    grams = [gram] + [
        lax.ppermute(gram, ("yl", "yh", "c"), [(i, i ^ d) for i in range(8)]) for d in range(1, 8)
    ]
    update = polar(g, grams)

    heads_total = keeper_slot.shape[0]
    heads = jnp.arange(heads_total, dtype=jnp.int32)
    wanted = x * Z + jnp.arange(Z, dtype=jnp.int32)
    source = jnp.sum(
        jnp.where(keeper_slot[None, :] == wanted[:, None], heads[None, :], 0), axis=1
    )
    place = (x - source // Z) % X * Z + source % Z
    spread = lax.all_to_all(g.astype(bf16).reshape(Z, q // Z, head), "z", 0, 0, tiled=True)
    everyone = jnp.concatenate([spread] + [shift(spread, "x", X, d) for d in (1, 2, 3)])
    chosen = everyone.at[place].get(mode="promise_in_bounds")
    arrived = lax.all_to_all(chosen, "z", 0, 0, tiled=True).reshape(q, head)
    gradient = arrived.astype(f32).T
    return (update[None], gradient[None])


def solution(mesh):
    wide = Mesh(np.asarray(mesh.devices).reshape(YL, X, Z, YH, C), NAMES)
    dp, mp = ("yl", "x", "z"), ("yh", "c")
    return jax.shard_map(
        on_device,
        mesh=wide,
        in_specs=(
            P(dp, mp),
            P(dp, None, mp),
            P(dp),
            P(dp),
            P(dp),
            P(dp, None),
            P(dp),
            P(),
        ),
        out_specs=(P(dp, None, mp), P(dp, None, mp)),
        check_vma=False,
    )
```

time: 687 us -> 240 us (0.35)
  waiting for transfers between devices: 475 us -> 125 us
  local copies, waits for them, and re-layouts: 99.7 us -> 16.8 us
  starting transfers between devices: 26.9 us -> 56.7 us
  matrix products: 34.3 us -> 6.14 us
  blocking collectives: 24.2 us -> 0 us
  between operations: 16.8 us -> 1.58 us
  Pallas kernels: 0 us -> 12.7 us
  other arithmetic: 8.35 us -> 16.9 us
    reduce_scatter x1 -> x0, waiting for transfers between devices: 348 us -> none  [on_device(): lax.psum_scatter(make_term(values, scaled, slot_ids, halves, local_rows *...]
    ppermute x3 -> x28, waiting for transfers between devices: 8.89 us -> 116 us  [the longest x5 58 us: over_y(): return lax.ppermute(value, ('yl', 'yh'), ring_pairs(flip))]
    psum x2 -> x0, waiting for transfers between devices: 80.6 us -> none  [total_gram(): return lax.psum(partial_sum + partner, 'mp')]
    gather x13 -> x2, local copies, waits for them, and re-layouts: 56.2 us -> 5.81 us  [the longest x1 3.58 us: on_device(): own = mixer_vectors.at[kept].get(mode='promise_in_bounds')]
    ppermute x3 -> x28, starting transfers between devices: 2.74 us -> 47.6 us  [the longest x13 28.1 us: shift(): lax.ppermute(value, axis, [(i, (i + step) % size) for i in range(size)])]
    dot_general x7 -> x2, matrix products: 34.3 us -> 6.14 us  [the longest x1 5.54 us: on_device(): picked = jnp.dot(adjoint, pick.astype(bf16), preferred_element_type=f32)]
    all_to_all x3 -> x2, waiting for transfers between devices: 31.4 us -> 8.71 us  [the longest x1 8.71 us: on_device(): lax.all_to_all(g.astype(bf16).reshape(Z, q // Z, head), 'z', 0, 0, tiled=...]
    reshape x3 -> x0, local copies, waits for them, and re-layouts: 21.2 us -> none  [the longest x1 12.3 us: make_term(): return product.reshape(nblocks * head_size, scaled.shape[2])]
  transfers between devices with their start and end apart: 10 -> 30, of which waited for: 10 -> 21; matrix products, arithmetic and copies ran while one was open for 8% -> 6% of each run, Pallas kernels for 0% -> 1%
where the time goes in v1:
time: 240 us; the launch traced here: 236 us
  waiting for transfers between devices  125 us (52%)
  starting transfers between devices  56.7 us (24%)
  other arithmetic  16.9 us (7%)
  local copies, waits for them, and re-layouts  16.8 us (7%)
  Pallas kernels  12.7 us (5%)
  matrix products  6.14 us (3%)
    ppermute x5, waiting for transfers between devices, over_y(): return lax.ppermute(value, ('yl', 'yh'), ring_pairs(flip))  58 us
    ppermute x13, starting transfers between devices, shift(): lax.ppermute(value, axis, [(i, (i + step) % size) for i in range(size)])  28.1 us
    ppermute x13, waiting for transfers between devices, shift(): lax.ppermute(value, axis, [(i, (i + step) % size) for i in range(size)])  27.8 us
    ppermute x2, waiting for transfers between devices, odd_to_even(): return lax.ppermute(value, ('x', 'c'), pairs)  25.5 us
    pallas_call x1, Pallas kernels, partials(): pl.pallas_call(partial_kernel, grid_spec=pltpu.PrefetchScalarGridSpec(num...  11 us
    all_to_all x1, waiting for transfers between devices, on_device(): lax.all_to_all(g.astype(bf16).reshape(Z, q // Z, head), 'z', 0, 0, tiled=...  8.71 us
    ppermute x7, starting transfers between devices, on_device(): lax.ppermute(gram, ('yl', 'yh', 'c'), [(i, i ^ d) for i in range(8)])  7.54 us
    ppermute x5, starting transfers between devices, over_y(): return lax.ppermute(value, ('yl', 'yh'), ring_pairs(flip))  7.15 us
  transfers between devices with their start and end apart: 30, of which 21 were waited for; matrix products, arithmetic and copies ran while one was open for 6% of the time, Pallas kernels for 1%

profile of v1, /device:TPU:8, one launch (start us, length us, event | category | flops | bytes accessed | tf_op | source)
XLA Modules:
  0.0 235.6 jit_solution(3490595159460688115)
XLA Ops:
  0.6 0.8 reduce
  2.2 0.7 exponential_multiply_fusion
  3.6 5.5 %fusion.8 = bf16[896,768]{0,1:T(8,128)(2,1)} fusion(bf16[896,1536]{1,0:T(8,128)(2,1)} %bitcast.50, s32[768]{0:T(1024)S(1)} %reduce, f32[768]{0:T(1024)S(1)} %fusion.12), kind=kOutput, calls=%fused_computation.15 | convolution fusion | flops 2117664768 | bytes 4134912 | tf_op jit(solution)/shard_map/dot_general | solution.py:167
  9.1 2.5 %copy.17 = bf16[896,768]{1,0:T(8,128)(2,1)} copy(bf16[896,768]{0,1:T(8,128)(2,1)} %fusion.8) | data formatting | bytes 2752512 | tf_op jit(solution)/shard_map/convert_element_type | solution.py:168
  11.7 2.5 %dynamic-slice_bitcast_fusion.1 = (bf16[448,768]{1,0:T(8,128)(2,1)}, bf16[448,768]{1,0:T(8,128)(2,1)}) fusion(bf16[2,448,768]{2,1,0:T(8,128)(2,1)} %bitcast.49, s32[]{:T(128)S(6)} %select_n.186, s32[]{:T(128)S(6)} %select_n.187), kind=kLoop, calls=%fused_computation.19 | loop fusion | bytes 2752520 | tf_op jit(solution)/shard_map/jit(dynamic_index_in_dim)/squeeze | solution.py:169
  14.2 2.2 collective-permute-start
  16.4 3.6 %gather_fusion = bf16[768,1024]{1,0:T(8,128)(2,1)} fusion(bf16[1536,1024]{1,0:T(8,128)(2,1)S(1)} %copy-done, s32[1024]{0:T(1024)S(1)} %pad_clamp_fusion.1), kind=kCustom, calls=%fused_computation | custom fusion | bytes 3148800 | tf_op jit(solution)/shard_map/gather | solution.py:156
  20.0 1.4 collective-permute-start.3
  21.4 11.6 %collective-permute-done = bf16[448,768]{1,0:T(8,128)(2,1)} collective-permute-done((bf16[448,768]{1,0:T(8,128)(2,1)}, bf16[448,768]{1,0:T(8,128)(2,1)}, u32[]{:S(2)}, u32[]{:S(2)}) %collective-permute-start) | collective-permute-done | bytes 688160 | tf_op jit(solution)/shard_map/ppermute | solution.py:33
  33.0 3.0 %fusion.18 = (bf16[1,448,1536]{2,1,0:T(8,128)(2,1)}, bf16[448,1536]{1,0:T(8,128)(2,1)}) fusion(bf16[448,768]{1,0:T(8,128)(2,1)} %collective-permute-done, bf16[448,768]{1,0:T(8,128)(2,1)} %get-tuple-element.22), kind=kLoop, calls=%fused_computation.56 | loop fusion | flops 2752512 | bytes 4128768 | tf_op jit(solution)/shard_map/stack | solution.py:172
  36.0 29.2 %collective-permute-done.2.e1_ref = bf16[768,1024]{1,0:T(8,128)(2,1)S(1)} collective-permute-done((bf16[768,1024]{1,0:T(8,128)(2,1)}, bf16[768,1024]{1,0:T(8,128)(2,1)S(1)}, u32[]{:S(2)}, u32[]{:S(2)}) %collective-permute-start.2) | collective-permute-done | bytes 1572896 | tf_op jit(solution)/shard_map/ppermute | solution.py:33
  65.3 1.0 slice.13
  66.3 1.1 copy-done.3
  67.5 1.6 collective-permute-start.5
  69.0 1.1 slice.12
  70.1 2.0 collective-permute-start.4
  72.3 2.2 pad_maximum_fusion.s_ref
  74.4 8.4 %collective-permute-done.4.oa_ref = bf16[256,1024]{1,0:T(8,128)(2,1)S(1)} collective-permute-done((bf16[256,1024]{1,0:T(8,128)(2,1)S(1)}, bf16[256,1024]{1,0:T(8,128)(2,1)S(1)}, u32[]{:S(2)}, u32[]{:S(2)}) %collective-permute-start.4) | collective-permute-done | bytes 524320 | tf_op jit(solution)/shard_map/ppermute | solution.py:33
  82.9 8.8 %collective-permute-done.5.ob_ref = bf16[512,1024]{1,0:T(8,128)(2,1)} collective-permute-done((bf16[512,1024]{1,0:T(8,128)(2,1)}, bf16[512,1024]{1,0:T(8,128)(2,1)}, u32[]{:S(2)}, u32[]{:S(2)}) %collective-permute-start.5) | collective-permute-done | bytes 1048608 | tf_op jit(solution)/shard_map/ppermute | solution.py:33
  91.6 11.0 %shard_map.113 = (bf16[448,1024]{1,0:T(8,128)(2,1)S(1)}, bf16[448,1024]{1,0:T(8,128)(2,1)S(1)}, bf16[448,1024]{1,0:T(8,128)(2,1)S(1)}, bf16[448,1024]{1,0:T(8,128)(2,1)S(1)}) custom-call(s32[8]{0:T(128)S(1)} %pad_add_fusion.plan, bf16[2,448,1536]{2,1,0:T(8,128)(2,1)S(1)} %pad_maximum_fusion.s_ref, bf16[768,1024]{1,0:T(8,128)(2,1)S(1)} %copy-done.2, ...), custom_call_target="tpu_custom_call" | custom-call | flops 5637144576 | bytes 12582912 | tf_op jit(solution)/shard_map/pallas_call | solution.py:84
  102.7 3.0 %collective-permute-start.7 = (bf16[448,1024]{1,0:T(8,128)(2,1)S(1)}, bf16[448,1024]{1,0:T(8,128)(2,1)S(1)}, u32[]{:S(2)}, u32[]{:S(2)}) collective-permute-start(bf16[448,1024]{1,0:T(8,128)(2,1)S(1)} %get-tuple-element.9), channel_id=1, source_target_pairs={{0,96},{32,0},{64,32},{96,64},{1,97},{33,1},{65,33},{97,65},{2,98}... | collective-permute-start | bytes 2752520 | tf_op jit(solution)/shard_map/ppermute | solution.py:37
  105.7 17.8 %collective-permute-done.7 = bf16[448,1024]{1,0:T(8,128)(2,1)S(1)} collective-permute-done((bf16[448,1024]{1,0:T(8,128)(2,1)S(1)}, bf16[448,1024]{1,0:T(8,128)(2,1)S(1)}, u32[]{:S(2)}, u32[]{:S(2)}) %collective-permute-start.7) | collective-permute-done | bytes 917536 | tf_op jit(solution)/shard_map/ppermute | solution.py:37
  123.9 1.3 collective-permute-start.8
  125.2 1.8 collective-permute-done.6
  126.9 12.2 %collective-permute-done.8 = bf16[448,1024]{1,0:T(8,128)(2,1)S(1)} collective-permute-done((bf16[448,1024]{1,0:T(8,128)(2,1)S(1)}, bf16[448,1024]{1,0:T(8,128)(2,1)S(1)}, u32[]{:S(2)}, u32[]{:S(2)}) %collective-permute-start.8) | collective-permute-done | bytes 917536 | tf_op jit(solution)/shard_map/ppermute | solution.py:44
  139.1 1.9 fusion.4
  141.1 1.3 collective-permute-start.10
  142.3 2.2 collective-permute-start.9
  144.6 13.3 %collective-permute-done.10 = bf16[448,1024]{1,0:T(8,128)(2,1)} collective-permute-done((bf16[448,1024]{1,0:T(8,128)(2,1)}, bf16[448,1024]{1,0:T(8,128)(2,1)}, u32[]{:S(2)}, u32[]{:S(2)}) %collective-permute-start.10) | collective-permute-done | bytes 917536 | tf_op jit(solution)/shard_map/ppermute | solution.py:44
  157.9 2.5 %fusion.11 = bf16[448,1024]{1,0:T(8,128)(2,1)S(1)} fusion(bf16[448,1024]{1,0:T(8,128)(2,1)} %collective-permute-done.9, bf16[448,1024]{1,0:T(8,128)(2,1)} %collective-permute-done.10, bf16[448,1024]{1,0:T(8,128)(2,1)} %copy-done.6, bf16[448,1024]{1,0:T(8,128)(2,1)} %copy-done.1, pred[]{:T(512)S(6)} %eq.45), kind=kLoop, calls=%fused_computation.17 | loop fusion | flops 3211264 | bytes 4587521 | tf_op jit(solution)/shard_map/jit(_where)/select_n | solution.py:191
  160.4 0.9 copy-done.5
  161.3 0.9 constant_dynamic-slice_fusion.6
  162.2 7.2 %collective-permute-start.11 = (bf16[448,128]{1,0:T(8,128)(2,1)S(1)}, bf16[448,128]{1,0:T(8,128)(2,1)S(1)}, u32[]{:S(2)}, u32[]{:S(2)}) collective-permute-start(bf16[448,128]{1,0:T(8,128)(2,1)S(1)} %get-tuple-element.24), channel_id=1, source_target_pairs={{0,16},{4,20},{8,24},{12,28},{16,0},{20,4},{24,8},{28,12},{1,17},{... | collective-permute-start | bytes 344072 | tf_op jit(solution)/shard_map/ppermute | solution.py:37
  169.4 1.9 collective-permute-start.12
  171.3 3.1 %collective-permute-start.13 = (bf16[448,128]{1,0:T(8,128)(2,1)}, bf16[448,128]{1,0:T(8,128)(2,1)S(1)}, u32[]{:S(2)}, u32[]{:S(2)}) collective-permute-start(bf16[448,128]{1,0:T(8,128)(2,1)} %get-tuple-element.29), channel_id=1, source_target_pairs={{0,20},{4,24},{8,28},{12,0},{16,4},{20,8},{24,12},{28,16},{1,21},{... | collective-permute-start | bytes 344072 | tf_op jit(solution)/shard_map/ppermute | solution.py:37
  174.4 1.5 collective-permute-start.14
  175.9 2.6 %collective-permute-start.15 = (bf16[448,128]{1,0:T(8,128)(2,1)}, bf16[448,128]{1,0:T(8,128)(2,1)}, u32[]{:S(2)}, u32[]{:S(2)}) collective-permute-start(bf16[448,128]{1,0:T(8,128)(2,1)} %get-tuple-element.27), channel_id=1, source_target_pairs={{0,24},{4,28},{8,0},{12,4},{16,8},{20,12},{24,16},{28,20},{1,25},{... | collective-permute-start | bytes 344072 | tf_op jit(solution)/shard_map/ppermute | solution.py:37
  178.6 1.0 collective-permute-start.16
  179.6 1.4 collective-permute-done.12
  181.0 0.8 collective-permute-start.17
  181.8 0.6 collective-permute-done.14
  182.4 2.1 collective-permute-done.15
  184.9 1.2 collective-permute-done.17
  186.1 2.0 fusion.19
  188.1 5.1 %all-to-all-start = ((bf16[8,56,128]{2,1,0:T(8,128)(2,1)}), bf16[8,56,128]{2,1,0:T(8,128)(2,1)S(1)}, u32[]{:S(2)}, u32[]{:S(2)}) async-start(bf16[8,56,128]{2,1,0:T(8,128)(2,1)} %bitcast.13), calls=%async_computation | async-start | bytes 229376 | tf_op jit(solution)/shard_map/all_to_all | solution.py:218
  193.4 8.7 %all-to-all-done = bf16[8,56,128]{2,1,0:T(8,128)(2,1)S(1)} async-done(((bf16[8,56,128]{2,1,0:T(8,128)(2,1)}), bf16[8,56,128]{2,1,0:T(8,128)(2,1)S(1)}, u32[]{:S(2)}, u32[]{:S(2)}) %all-to-all-start) | async-done | bytes 114720 | tf_op jit(solution)/shard_map/all_to_all | solution.py:218
  202.1 0.8 collective-permute-start.25
  202.9 3.9 %collective-permute-start.26 = (bf16[8,56,128]{2,1,0:T(8,128)(2,1)S(1)}, bf16[8,56,128]{2,1,0:T(8,128)(2,1)S(1)}, u32[]{:S(2)}, u32[]{:S(2)}) collective-permute-start(bf16[8,56,128]{2,1,0:T(8,128)(2,1)S(1)} %all-to-all-done), channel_id=1, source_target_pairs={{0,64},{32,96},{64,0},{96,32},{1,65},{33,97},{65,1},{97,33},{2,66}... | collective-permute-start | bytes 344072 | tf_op jit(solution)/shard_map/ppermute | solution.py:37
  206.8 2.2 collective-permute-start.27
  209.0 1.7 collective-permute-done.26
  210.8 0.8 collective-permute-done.27
  211.6 0.8 pad_maximum_fusion.2
  212.4 2.2 gather_fusion.1
  214.6 4.0 %all-to-all-start.1 = ((bf16[8,56,128]{2,1,0:T(8,128)(2,1)}), bf16[8,56,128]{2,1,0:T(8,128)(2,1)}, u32[]{:S(2)}, u32[]{:S(2)}) async-start(bf16[8,56,128]{2,1,0:T(8,128)(2,1)} %gather_fusion.1), calls=%async_computation.1 | async-start | bytes 229376 | tf_op jit(solution)/shard_map/all_to_all | solution.py:221
  219.3 3.6 %collective-permute-start.19 = (f32[128,128]{1,0:T(8,128)S(1)}, f32[128,128]{1,0:T(8,128)S(1)}, u32[]{:S(2)}, u32[]{:S(2)}) collective-permute-start(f32[128,128]{1,0:T(8,128)S(1)} %fusion.20.refs_1_), channel_id=1, source_target_pairs={{0,2},{1,3},{2,0},{3,1},{128,130},{129,131},{130,128},{131,129},{4... | collective-permute-start | bytes 196616 | tf_op jit(solution)/shard_map/ppermute | solution.py:207
  223.0 1.4 collective-permute-start.21
  224.7 2.1 collective-permute-start.23
  226.8 1.8 collective-permute-done.20.refs_4_
  228.7 0.8 collective-permute-done.22.refs_6_
  229.5 0.8 collective-permute-done.23.refs_7_
  230.3 1.3 collective-permute-done.24.refs_8_
  231.6 1.7 shard_map.114
  233.3 0.8 copy.18
  234.0 1.6 convert_bitcast_fusion
  (54 shorter events, 2.9 us)
Async XLA Ops:
  0.6 15.8 %copy-start = (bf16[1536,1024]{1,0:T(8,128)(2,1)S(1)}, bf16[1536,1024]{1,0:T(8,128)(2,1)}, u32[]{:S(2)}) copy-start(bf16[1536,1024]{1,0:T(8,128)(2,1)} %param.10) | copy-start | bytes 9437188
  11.7 4.7 %copy-start.9 = (s32[1,768]{1,0:T(1,128)S(1)}, s32[1,768]{1,0:T(1,128)}, u32[]{:S(2)}) copy-start(s32[1,768]{1,0:T(1,128)} %param.15) | copy-start | bytes 9220
  14.2 18.8 %collective-permute-start = (bf16[448,768]{1,0:T(8,128)(2,1)}, bf16[448,768]{1,0:T(8,128)(2,1)}, u32[]{:S(2)}, u32[]{:S(2)}) collective-permute-start(bf16[448,768]{1,0:T(8,128)(2,1)} %get-tuple-element.23), channel_id=1, source_target_pairs={{0,128},{128,0},{2,130},{130,2},{1,129},{129,1},{3,131},{131,3},{4... | collective-permute-start | bytes 2064392 | tf_op jit(solution)/shard_map/ppermute | solution.py:33
  20.0 45.3 %collective-permute-start.2 = (bf16[768,1024]{1,0:T(8,128)(2,1)}, bf16[768,1024]{1,0:T(8,128)(2,1)S(1)}, u32[]{:S(2)}, u32[]{:S(2)}) collective-permute-start(bf16[768,1024]{1,0:T(8,128)(2,1)} %gather_fusion), channel_id=1, source_target_pairs={{0,128},{128,0},{2,130},{130,2},{1,129},{129,1},{3,131},{131,3},{4... | collective-permute-start | bytes 4718600 | tf_op jit(solution)/shard_map/ppermute | solution.py:33
  20.0 49.0 %collective-permute-start.3 = (bf16[768,1024]{1,0:T(8,128)(2,1)}, bf16[768,1024]{1,0:T(8,128)(2,1)}, u32[]{:S(2)}, u32[]{:S(2)}) collective-permute-start(bf16[768,1024]{1,0:T(8,128)(2,1)} %gather_fusion), channel_id=1, source_target_pairs={{0,130},{128,2},{2,128},{130,0},{1,131},{129,3},{3,129},{131,1},{4... | collective-permute-start | bytes 4718600 | tf_op jit(solution)/shard_map/ppermute | solution.py:33
  36.0 36.1 %copy-start.10 = (s32[4]{0:T(128)S(1)}, s32[4]{0:T(128)}, u32[]{:S(2)}) copy-start(s32[4]{0:T(128)} %constant.147.clone) | copy-start | bytes 52
  36.0 36.1 %copy-start.11 = (s32[4]{0:T(128)S(1)}, s32[4]{0:T(128)}, u32[]{:S(2)}) copy-start(s32[4]{0:T(128)} %constant.148.clone) | copy-start | bytes 52
  36.0 36.2 %collective-permute-start.1 = (bf16[448,1536]{1,0:T(8,128)(2,1)}, bf16[448,1536]{1,0:T(8,128)(2,1)}, u32[]{:S(2)}, u32[]{:S(2)}) collective-permute-start(bf16[448,1536]{1,0:T(8,128)(2,1)} %get-tuple-element.21), channel_id=1, source_target_pairs={{0,1},{1,0},{2,3},{3,2},{4,5},{5,4},{6,7},{7,6},{8,9},{9,8},{10,11... | collective-permute-start | bytes 4128776 | tf_op jit(solution)/shard_map/ppermute | solution.py:37
  66.3 1.1 copy-start.3
  67.5 24.2 %collective-permute-start.5 = (bf16[512,1024]{1,0:T(8,128)(2,1)}, bf16[512,1024]{1,0:T(8,128)(2,1)}, u32[]{:S(2)}, u32[]{:S(2)}) collective-permute-start(bf16[512,1024]{1,0:T(8,128)(2,1)} %slice.13), channel_id=1, source_target_pairs={{0,130},{128,2},{2,128},{130,0},{1,131},{129,3},{3,129},{131,1},{4... | collective-permute-start | bytes 3145736 | tf_op jit(solution)/shard_map/ppermute | solution.py:33
  70.1 12.7 %collective-permute-start.4 = (bf16[256,1024]{1,0:T(8,128)(2,1)S(1)}, bf16[256,1024]{1,0:T(8,128)(2,1)S(1)}, u32[]{:S(2)}, u32[]{:S(2)}) collective-permute-start(bf16[256,1024]{1,0:T(8,128)(2,1)S(1)} %slice.12), channel_id=1, source_target_pairs={{0,128},{128,0},{2,130},{130,2},{1,129},{129,1},{3,131},{131,3},{4... | collective-permute-start | bytes 1572872 | tf_op jit(solution)/shard_map/ppermute | solution.py:33
  72.3 19.4 %copy-start.2 = (bf16[768,1024]{1,0:T(8,128)(2,1)S(1)}, bf16[768,1024]{1,0:T(8,128)(2,1)}, u32[]{:S(2)}) copy-start(bf16[768,1024]{1,0:T(8,128)(2,1)} %gather_fusion) | copy-start | bytes 4718596
  72.3 19.4 %copy-start.4 = (bf16[768,1024]{1,0:T(8,128)(2,1)S(1)}, bf16[768,1024]{1,0:T(8,128)(2,1)}, u32[]{:S(2)}) copy-start(bf16[768,1024]{1,0:T(8,128)(2,1)} %copy-done.3) | copy-start | bytes 4718596
  102.7 38.4 %copy-start.1 = (bf16[448,1024]{1,0:T(8,128)(2,1)}, bf16[448,1024]{1,0:T(8,128)(2,1)S(1)}, u32[]{:S(2)}) copy-start(bf16[448,1024]{1,0:T(8,128)(2,1)S(1)} %get-tuple-element.8) | copy-start | bytes 2752516
  102.7 20.8 %collective-permute-start.7 = (bf16[448,1024]{1,0:T(8,128)(2,1)S(1)}, bf16[448,1024]{1,0:T(8,128)(2,1)S(1)}, u32[]{:S(2)}, u32[]{:S(2)}) collective-permute-start(bf16[448,1024]{1,0:T(8,128)(2,1)S(1)} %get-tuple-element.9), channel_id=1, source_target_pairs={{0,96},{32,0},{64,32},{96,64},{1,97},{33,1},{65,33},{97,65},{2,98}... | collective-permute-start | bytes 2752520 | tf_op jit(solution)/shard_map/ppermute | solution.py:37
  105.7 21.2 %collective-permute-start.6 = (bf16[448,1024]{1,0:T(8,128)(2,1)S(1)}, bf16[448,1024]{1,0:T(8,128)(2,1)S(1)}, u32[]{:S(2)}, u32[]{:S(2)}) collective-permute-start(bf16[448,1024]{1,0:T(8,128)(2,1)S(1)} %get-tuple-element.7), channel_id=1, source_target_pairs={{0,32},{32,64},{64,96},{96,0},{1,33},{33,65},{65,97},{97,1},{2,34}... | collective-permute-start | bytes 2752520 | tf_op jit(solution)/shard_map/ppermute | solution.py:37
  123.5 3.4 %copy-start.6 = (bf16[448,1024]{1,0:T(8,128)(2,1)}, bf16[448,1024]{1,0:T(8,128)(2,1)S(1)}, u32[]{:S(2)}) copy-start(bf16[448,1024]{1,0:T(8,128)(2,1)S(1)} %collective-permute-done.7) | copy-start | bytes 2752516
  123.9 15.3 %collective-permute-start.8 = (bf16[448,1024]{1,0:T(8,128)(2,1)S(1)}, bf16[448,1024]{1,0:T(8,128)(2,1)S(1)}, u32[]{:S(2)}, u32[]{:S(2)}) collective-permute-start(bf16[448,1024]{1,0:T(8,128)(2,1)S(1)} %fusion.5), channel_id=1, source_target_pairs={{1,97},{32,0},{65,33},{96,64},{3,99},{34,2},{67,35},{98,66},{5,101... | collective-permute-start | bytes 2752520 | tf_op jit(solution)/shard_map/ppermute | solution.py:44
  141.1 16.8 %collective-permute-start.10 = (bf16[448,1024]{1,0:T(8,128)(2,1)}, bf16[448,1024]{1,0:T(8,128)(2,1)}, u32[]{:S(2)}, u32[]{:S(2)}) collective-permute-start(bf16[448,1024]{1,0:T(8,128)(2,1)} %get-tuple-element.18), channel_id=1, source_target_pairs={{1,33},{32,64},{65,97},{96,0},{3,35},{34,66},{67,99},{98,2},{5,37}... | collective-permute-start | bytes 2752520 | tf_op jit(solution)/shard_map/ppermute | solution.py:44
  142.3 15.5 %collective-permute-start.9 = (bf16[448,1024]{1,0:T(8,128)(2,1)}, bf16[448,1024]{1,0:T(8,128)(2,1)}, u32[]{:S(2)}, u32[]{:S(2)}) collective-permute-start(bf16[448,1024]{1,0:T(8,128)(2,1)} %get-tuple-element.19), channel_id=1, source_target_pairs={{0,1},{33,32},{64,65},{97,96},{2,3},{35,34},{66,67},{99,98},{4,5},... | collective-permute-start | bytes 2752520 | tf_op jit(solution)/shard_map/ppermute | solution.py:49
  160.4 0.9 copy-start.5
  161.3 31.9 %copy-start.12 = (s32[32]{0:T(128)S(1)}, s32[32]{0:T(128)}, u32[]{:S(2)}) copy-start(s32[32]{0:T(128)} %param.17) | copy-start | bytes 388
  162.2 16.4 %collective-permute-start.11 = (bf16[448,128]{1,0:T(8,128)(2,1)S(1)}, bf16[448,128]{1,0:T(8,128)(2,1)S(1)}, u32[]{:S(2)}, u32[]{:S(2)}) collective-permute-start(bf16[448,128]{1,0:T(8,128)(2,1)S(1)} %get-tuple-element.24), channel_id=1, source_target_pairs={{0,16},{4,20},{8,24},{12,28},{16,0},{20,4},{24,8},{28,12},{1,17},{... | collective-permute-start | bytes 344072 | tf_op jit(solution)/shard_map/ppermute | solution.py:37
  169.4 11.6 %collective-permute-start.12 = (bf16[448,128]{1,0:T(8,128)(2,1)S(1)}, bf16[448,128]{1,0:T(8,128)(2,1)}, u32[]{:S(2)}, u32[]{:S(2)}) collective-permute-start(bf16[448,128]{1,0:T(8,128)(2,1)S(1)} %get-tuple-element.30), channel_id=1, source_target_pairs={{0,12},{4,16},{8,20},{12,24},{16,28},{20,0},{24,4},{28,8},{1,13},{... | collective-permute-start | bytes 344072 | tf_op jit(solution)/shard_map/ppermute | solution.py:37
  171.3 10.5 %collective-permute-start.13 = (bf16[448,128]{1,0:T(8,128)(2,1)}, bf16[448,128]{1,0:T(8,128)(2,1)S(1)}, u32[]{:S(2)}, u32[]{:S(2)}) collective-permute-start(bf16[448,128]{1,0:T(8,128)(2,1)} %get-tuple-element.29), channel_id=1, source_target_pairs={{0,20},{4,24},{8,28},{12,0},{16,4},{20,8},{24,12},{28,16},{1,21},{... | collective-permute-start | bytes 344072 | tf_op jit(solution)/shard_map/ppermute | solution.py:37
  174.4 8.0 %collective-permute-start.14 = (bf16[448,128]{1,0:T(8,128)(2,1)}, bf16[448,128]{1,0:T(8,128)(2,1)S(1)}, u32[]{:S(2)}, u32[]{:S(2)}) collective-permute-start(bf16[448,128]{1,0:T(8,128)(2,1)} %get-tuple-element.28), channel_id=1, source_target_pairs={{0,8},{4,12},{8,16},{12,20},{16,24},{20,28},{24,0},{28,4},{1,9},{5... | collective-permute-start | bytes 344072 | tf_op jit(solution)/shard_map/ppermute | solution.py:37
  175.9 8.7 %collective-permute-start.15 = (bf16[448,128]{1,0:T(8,128)(2,1)}, bf16[448,128]{1,0:T(8,128)(2,1)}, u32[]{:S(2)}, u32[]{:S(2)}) collective-permute-start(bf16[448,128]{1,0:T(8,128)(2,1)} %get-tuple-element.27), channel_id=1, source_target_pairs={{0,24},{4,28},{8,0},{12,4},{16,8},{20,12},{24,16},{28,20},{1,25},{... | collective-permute-start | bytes 344072 | tf_op jit(solution)/shard_map/ppermute | solution.py:37
  178.6 6.3 %collective-permute-start.16 = (bf16[448,128]{1,0:T(8,128)(2,1)}, bf16[448,128]{1,0:T(8,128)(2,1)}, u32[]{:S(2)}, u32[]{:S(2)}) collective-permute-start(bf16[448,128]{1,0:T(8,128)(2,1)} %get-tuple-element.26), channel_id=1, source_target_pairs={{0,4},{4,8},{8,12},{12,16},{16,20},{20,24},{24,28},{28,0},{1,5},{5... | collective-permute-start | bytes 344072 | tf_op jit(solution)/shard_map/ppermute | solution.py:37
  181.0 5.1 %collective-permute-start.17 = (bf16[448,128]{1,0:T(8,128)(2,1)}, bf16[448,128]{1,0:T(8,128)(2,1)}, u32[]{:S(2)}, u32[]{:S(2)}) collective-permute-start(bf16[448,128]{1,0:T(8,128)(2,1)} %get-tuple-element.25), channel_id=1, source_target_pairs={{0,28},{4,0},{8,4},{12,8},{16,12},{20,16},{24,20},{28,24},{1,29},{... | collective-permute-start | bytes 344072 | tf_op jit(solution)/shard_map/ppermute | solution.py:37
  181.8 3.1 %copy-start.7 = (bf16[448,128]{1,0:T(8,128)(2,1)}, bf16[448,128]{1,0:T(8,128)(2,1)S(1)}, u32[]{:S(2)}) copy-start(bf16[448,128]{1,0:T(8,128)(2,1)S(1)} %collective-permute-done.13) | copy-start | bytes 344068
  182.4 2.5 %copy-start.8 = (bf16[448,128]{1,0:T(8,128)(2,1)}, bf16[448,128]{1,0:T(8,128)(2,1)S(1)}, u32[]{:S(2)}) copy-start(bf16[448,128]{1,0:T(8,128)(2,1)S(1)} %collective-permute-done.14) | copy-start | bytes 344068
  188.1 14.0 %all-to-all-start = ((bf16[8,56,128]{2,1,0:T(8,128)(2,1)}), bf16[8,56,128]{2,1,0:T(8,128)(2,1)S(1)}, u32[]{:S(2)}, u32[]{:S(2)}) async-start(bf16[8,56,128]{2,1,0:T(8,128)(2,1)} %bitcast.13), calls=%async_computation | async-start | bytes 229376 | tf_op jit(solution)/shard_map/all_to_all | solution.py:218
  202.1 6.9 %collective-permute-start.25 = (bf16[8,56,128]{2,1,0:T(8,128)(2,1)S(1)}, bf16[8,56,128]{2,1,0:T(8,128)(2,1)S(1)}, u32[]{:S(2)}, u32[]{:S(2)}) collective-permute-start(bf16[8,56,128]{2,1,0:T(8,128)(2,1)S(1)} %all-to-all-done), channel_id=1, source_target_pairs={{0,32},{32,64},{64,96},{96,0},{1,33},{33,65},{65,97},{97,1},{2,34}... | collective-permute-start | bytes 344072 | tf_op jit(solution)/shard_map/ppermute | solution.py:37
  202.9 7.9 %collective-permute-start.26 = (bf16[8,56,128]{2,1,0:T(8,128)(2,1)S(1)}, bf16[8,56,128]{2,1,0:T(8,128)(2,1)S(1)}, u32[]{:S(2)}, u32[]{:S(2)}) collective-permute-start(bf16[8,56,128]{2,1,0:T(8,128)(2,1)S(1)} %all-to-all-done), channel_id=1, source_target_pairs={{0,64},{32,96},{64,0},{96,32},{1,65},{33,97},{65,1},{97,33},{2,66}... | collective-permute-start | bytes 344072 | tf_op jit(solution)/shard_map/ppermute | solution.py:37
  206.8 4.8 %collective-permute-start.27 = (bf16[8,56,128]{2,1,0:T(8,128)(2,1)S(1)}, bf16[8,56,128]{2,1,0:T(8,128)(2,1)S(1)}, u32[]{:S(2)}, u32[]{:S(2)}) collective-permute-start(bf16[8,56,128]{2,1,0:T(8,128)(2,1)S(1)} %all-to-all-done), channel_id=1, source_target_pairs={{0,96},{32,0},{64,32},{96,64},{1,97},{33,1},{65,33},{97,65},{2,98}... | collective-permute-start | bytes 344072 | tf_op jit(solution)/shard_map/ppermute | solution.py:37
  214.6 19.4 %all-to-all-start.1 = ((bf16[8,56,128]{2,1,0:T(8,128)(2,1)}), bf16[8,56,128]{2,1,0:T(8,128)(2,1)}, u32[]{:S(2)}, u32[]{:S(2)}) async-start(bf16[8,56,128]{2,1,0:T(8,128)(2,1)} %gather_fusion.1), calls=%async_computation.1 | async-start | bytes 229376 | tf_op jit(solution)/shard_map/all_to_all | solution.py:221
  219.2 5.5 %collective-permute-start.18 = (f32[128,128]{1,0:T(8,128)S(1)}, f32[128,128]{1,0:T(8,128)S(1)}, u32[]{:S(2)}, u32[]{:S(2)}) collective-permute-start(f32[128,128]{1,0:T(8,128)S(1)} %fusion.20.refs_1_), channel_id=1, source_target_pairs={{0,1},{1,0},{2,3},{3,2},{128,129},{129,128},{130,131},{131,130},{4... | collective-permute-start | bytes 196616 | tf_op jit(solution)/shard_map/ppermute | solution.py:207
  219.3 7.5 %collective-permute-start.19 = (f32[128,128]{1,0:T(8,128)S(1)}, f32[128,128]{1,0:T(8,128)S(1)}, u32[]{:S(2)}, u32[]{:S(2)}) collective-permute-start(f32[128,128]{1,0:T(8,128)S(1)} %fusion.20.refs_1_), channel_id=1, source_target_pairs={{0,2},{1,3},{2,0},{3,1},{128,130},{129,131},{130,128},{131,129},{4... | collective-permute-start | bytes 196616 | tf_op jit(solution)/shard_map/ppermute | solution.py:207
  222.9 5.6 %collective-permute-start.20 = (f32[128,128]{1,0:T(8,128)S(1)}, f32[128,128]{1,0:T(8,128)S(1)}, u32[]{:S(2)}, u32[]{:S(2)}) collective-permute-start(f32[128,128]{1,0:T(8,128)S(1)} %fusion.20.refs_1_), channel_id=1, source_target_pairs={{0,3},{1,2},{2,1},{3,0},{128,131},{129,130},{130,129},{131,128},{4... | collective-permute-start | bytes 196616 | tf_op jit(solution)/shard_map/ppermute | solution.py:207
  223.0 5.7 %collective-permute-start.21 = (f32[128,128]{1,0:T(8,128)S(1)}, f32[128,128]{1,0:T(8,128)S(1)}, u32[]{:S(2)}, u32[]{:S(2)}) collective-permute-start(f32[128,128]{1,0:T(8,128)S(1)} %fusion.20.refs_1_), channel_id=1, source_target_pairs={{0,128},{1,129},{2,130},{3,131},{128,0},{129,1},{130,2},{131,3},{4... | collective-permute-start | bytes 196616 | tf_op jit(solution)/shard_map/ppermute | solution.py:207
  224.4 5.1 %collective-permute-start.22 = (f32[128,128]{1,0:T(8,128)S(1)}, f32[128,128]{1,0:T(8,128)S(1)}, u32[]{:S(2)}, u32[]{:S(2)}) collective-permute-start(f32[128,128]{1,0:T(8,128)S(1)} %fusion.20.refs_1_), channel_id=1, source_target_pairs={{0,129},{1,128},{2,131},{3,130},{128,1},{129,0},{130,3},{131,2},{4... | collective-permute-start | bytes 196616 | tf_op jit(solution)/shard_map/ppermute | solution.py:207
  224.7 5.6 %collective-permute-start.23 = (f32[128,128]{1,0:T(8,128)S(1)}, f32[128,128]{1,0:T(8,128)S(1)}, u32[]{:S(2)}, u32[]{:S(2)}) collective-permute-start(f32[128,128]{1,0:T(8,128)S(1)} %fusion.20.refs_1_), channel_id=1, source_target_pairs={{0,130},{1,131},{2,128},{3,129},{128,2},{129,3},{130,0},{131,1},{4... | collective-permute-start | bytes 196616 | tf_op jit(solution)/shard_map/ppermute | solution.py:207
  226.8 4.8 %collective-permute-start.24 = (f32[128,128]{1,0:T(8,128)S(1)}, f32[128,128]{1,0:T(8,128)S(1)}, u32[]{:S(2)}, u32[]{:S(2)}) collective-permute-start(f32[128,128]{1,0:T(8,128)S(1)} %fusion.20.refs_1_), channel_id=1, source_target_pairs={{0,131},{1,130},{2,129},{3,128},{128,3},{129,2},{130,1},{131,0},{4... | collective-permute-start | bytes 196616 | tf_op jit(solution)/shard_map/ppermute | solution.py:207

commit v2 on v1

v2 whole, which is shorter than its diff:
```python
import math

import jax
import jax.numpy as jnp
import numpy as np
from jax import lax
from jax.experimental import pallas as pl
from jax.experimental.pallas import tpu as pltpu
from jax.sharding import Mesh
from jax.sharding import PartitionSpec as P

DHALF = 1792

coeff_a = 3.4445
coeff_b = -4.775
coeff_c = 2.0315
norm_eps = 1e-06
highest_precision_mode = lax.Precision.HIGHEST

YL, X, Z, YH, C = 2, 4, 8, 2, 2
NAMES = ("yl", "x", "z", "yh", "c")
PIECES = 2


def ring_pairs(flip):
    def index(y):
        return (y % 2) * 2 + y // 2

    return [(index(y), index(y ^ flip)) for y in range(4)]


def over_y(value, flip):
    return lax.ppermute(value, ("yl", "yh"), ring_pairs(flip))


def shift(value, axis, size, step):
    return lax.ppermute(value, axis, [(i, (i + step) % size) for i in range(size)])


def odd_to_even(value, step):
    pairs = [
        (x * 2 + c, (x + step) % X * 2 + c) for x in range(X) for c in range(C) if (x + c) % 2
    ]
    return lax.ppermute(value, ("x", "c"), pairs)


def even_to_odd_core(value):
    pairs = [(x * 2 + c, x * 2 + 1 - c) for x in range(X) for c in range(C) if not (x + c) % 2]
    return lax.ppermute(value, ("x", "c"), pairs)


def pick_kernel(kept_ref, v_ref, out_ref):
    rows, cap = v_ref.shape[0], kept_ref.shape[1]
    column = jnp.broadcast_to(kept_ref[...], (8, cap)).T[:, :1]
    pick = lax.broadcasted_iota(jnp.int32, (cap, rows), 1) == column
    out_ref[...] = jnp.dot(
        pick.astype(jnp.bfloat16), v_ref[...], preferred_element_type=jnp.float32
    ).astype(out_ref.dtype)


def pick_rows(kept, values, piece, pieces):
    rows, cols = values.shape
    cap = kept.shape[1]
    width = cols // pieces
    return pl.pallas_call(
        pick_kernel,
        grid=(1,),
        in_specs=[
            pl.BlockSpec((1, cap), lambda i: (0, 0)),
            pl.BlockSpec((rows, width), lambda i: (0, piece)),
        ],
        out_specs=pl.BlockSpec((cap, width), lambda i: (0, 0)),
        out_shape=jax.ShapeDtypeStruct((cap, width), values.dtype),
        compiler_params=pltpu.CompilerParams(vmem_limit_bytes=32 * 2**20),
        cost_estimate=pl.CostEstimate(
            flops=2 * cap * rows * width, bytes_accessed=2 * (rows + cap) * width, transcendentals=0
        ),
    )(kept, values)


def scale_kernel(plan, kept_ref, benefit_ref, present_ref, behaviour_ref, u_ref, out_ref):
    rows, cap = u_ref.shape[2], kept_ref.shape[1]
    pick = (lax.broadcasted_iota(jnp.int32, (rows, cap), 0) == kept_ref[...]).astype(jnp.bfloat16)
    rest = benefit_ref[...] * jnp.exp(present_ref[...] - behaviour_ref[...])
    parts = []
    for _ in range(3):
        part = rest.astype(jnp.bfloat16)
        parts.append(part)
        rest = rest - part.astype(jnp.float32)
    weight = jnp.zeros((1, cap), jnp.float32)
    for part in parts[::-1]:
        stacked = jnp.broadcast_to(part, (16, rows))
        weight = weight + jnp.dot(stacked, pick, preferred_element_type=jnp.float32)[:1]
    live = lax.broadcasted_iota(jnp.int32, (1, cap), 1) < plan[1]
    weight = jnp.where(live, weight, 0.0)
    picked = jnp.dot(u_ref[0], pick, preferred_element_type=jnp.float32)
    out_ref[...] = (weight * picked).astype(out_ref.dtype)


def scaled_half(half, tally, kept, benefit, present, behaviour, adjoint):
    _, q, rows = adjoint.shape
    cap = kept.shape[1]
    row_spec = pl.BlockSpec((1, rows), lambda i, plan: (0, 0))
    return pl.pallas_call(
        scale_kernel,
        grid_spec=pltpu.PrefetchScalarGridSpec(
            num_scalar_prefetch=1,
            grid=(1,),
            in_specs=[
                pl.BlockSpec((1, cap), lambda i, plan: (0, 0)),
                row_spec,
                row_spec,
                row_spec,
                pl.BlockSpec((1, q, rows), lambda i, plan: (plan[0], 0, 0)),
            ],
            out_specs=pl.BlockSpec((q, cap), lambda i, plan: (0, 0)),
        ),
        out_shape=jax.ShapeDtypeStruct((q, cap), jnp.bfloat16),
        compiler_params=pltpu.CompilerParams(vmem_limit_bytes=32 * 2**20),
        cost_estimate=pl.CostEstimate(
            flops=2 * q * rows * cap, bytes_accessed=2 * q * (rows + cap), transcendentals=rows
        ),
    )(jnp.stack([half, tally]).astype(jnp.int32), kept, benefit, present, behaviour, adjoint)


def partial_kernel(parts, plan, *refs):
    s_refs, v_refs, out_refs = refs[:4], refs[4:-6], refs[-6:-2]
    s_all, total = refs[-2:]
    own_ref, e1_ref, e3_ref = v_refs[:3]
    opposite = v_refs[3:]
    q, cap = s_refs[0].shape
    tile = total.shape[2]
    for i, ref in enumerate(s_refs):
        side, other = divmod(i, 2)
        s_all[side * q : (side + 1) * q, other * cap : (other + 1) * cap] = ref[...]

    for tile_at in range(0, own_ref.shape[1], tile):
        columns = slice(tile_at, tile_at + tile)

        def dot(lo, v, columns=columns):
            return jnp.dot(
                s_all[:, lo : lo + v.shape[0]], v[:, columns], preferred_element_type=jnp.float32
            )

        near = dot(cap, e1_ref) + dot(0, own_ref)
        far = dot(cap, e3_ref)
        at = 0
        for ref in opposite:
            far = far + dot(at, ref)
            at += ref.shape[0]
        for chunk, value in enumerate((near, far)):
            value = value.astype(total.dtype)
            for side in range(2):
                total[2 * chunk + side] = value[side * q : (side + 1) * q]
        for slot, out_ref in enumerate(out_refs):
            out_ref[:, columns] = total[plan[slot]]


def partials(plan, s_list, own, e1, e3, opposite):
    cap, cols = own.shape
    q = s_list[0].shape[0]
    values = [own, e1, e3, *opposite]
    full = pl.BlockSpec(memory_space=pltpu.VMEM)
    return pl.pallas_call(
        lambda *refs: partial_kernel(len(opposite), *refs),
        in_specs=[pl.BlockSpec(memory_space=pltpu.SMEM)] + [full] * (4 + len(values)),
        out_specs=[full] * 4,
        scratch_shapes=[
            pltpu.VMEM((2 * q, 2 * cap), jnp.bfloat16),
            pltpu.VMEM((4, q, 256), jnp.bfloat16),
        ],
        out_shape=[jax.ShapeDtypeStruct((q, cols), jnp.bfloat16)] * 4,
        compiler_params=pltpu.CompilerParams(vmem_limit_bytes=40 * 2**20),
        cost_estimate=pl.CostEstimate(
            flops=8 * q * 2 * cap * cols, bytes_accessed=8 * 2**20, transcendentals=0
        ),
    )(plan, *s_list, *values)


def rows_kernel(piece_count, plan, *refs):
    ins, outs, mine = refs[: 4 * piece_count], refs[4 * piece_count : -1], refs[-1]
    width = ins[0].shape[1]
    rows = outs[0].shape[0]
    for piece in range(piece_count):
        cross, t3, rb, rp = ins[4 * piece : 4 * piece + 4]
        columns = pl.ds(piece * width, width)

        @pl.when(plan[0] == 1)
        def _(cross=cross, columns=columns):
            mine[:, columns] = cross[...].astype(jnp.float32)

        @pl.when(plan[0] == 0)
        def _(t3=t3, rb=rb, rp=rp, columns=columns):
            mine[:, columns] = (
                t3[...].astype(jnp.float32)
                + rb[...].astype(jnp.float32)
                + rp[...].astype(jnp.float32)
            )

    for step, out in enumerate(outs):
        at = lax.rem(plan[1] + step, Z) * rows
        out[...] = mine[pl.ds(pl.multiple_of(at, 8), rows), :].astype(out.dtype)


def row_blocks(plan, inputs):
    q, width = inputs[0].shape
    cols = width * (len(inputs) // 4)
    full = pl.BlockSpec(memory_space=pltpu.VMEM)
    return pl.pallas_call(
        lambda *refs: rows_kernel(len(inputs) // 4, *refs),
        in_specs=[pl.BlockSpec(memory_space=pltpu.SMEM)] + [full] * len(inputs),
        out_specs=[full] * Z,
        out_shape=[jax.ShapeDtypeStruct((q // Z, cols), jnp.float32)]
        + [jax.ShapeDtypeStruct((q // Z, cols), jnp.bfloat16)] * (Z - 1),
        scratch_shapes=[pltpu.VMEM((q, cols), jnp.float32)],
        compiler_params=pltpu.CompilerParams(vmem_limit_bytes=32 * 2**20),
    )(plan, *inputs)


def sum_kernel(*refs):
    ins, (exact, rounded) = refs[:-2], refs[-2:]
    head = exact.shape[2]
    total = ins[0][...]
    for ref in ins[1:]:
        total = total + ref[...].astype(jnp.float32)
    for j in range(exact.shape[0]):
        block = total[:, j * head : (j + 1) * head]
        exact[j] = block
        rounded[j] = block.astype(rounded.dtype)


def sum_over_z(parts):
    rows, cols = parts[0].shape
    shape = (Z, rows, cols // Z)
    return pl.pallas_call(
        sum_kernel,
        out_shape=[
            jax.ShapeDtypeStruct(shape, jnp.float32),
            jax.ShapeDtypeStruct(shape, jnp.bfloat16),
        ],
    )(*parts)


def choose_kernel(place, *refs):
    ins, out = refs[:-1], refs[-1]
    for t in range(out.shape[0]):
        for d, ref in enumerate(ins):

            @pl.when(place[t] // Z == d)
            def _(t=t, ref=ref):
                out[t] = ref[lax.rem(place[t], Z)]


def choose(place, rows):
    full = pl.BlockSpec(memory_space=pltpu.VMEM)
    return pl.pallas_call(
        choose_kernel,
        in_specs=[pl.BlockSpec(memory_space=pltpu.SMEM)] + [full] * len(rows),
        out_specs=full,
        out_shape=jax.ShapeDtypeStruct(rows[0].shape, rows[0].dtype),
    )(place, *rows)


def polar_kernel(scale, g_ref, *refs):
    out_ref = refs[-1]
    gram = refs[0][...]
    for ref in refs[1:-1]:
        gram = gram + ref[...]

    def mul(a, b):
        return jnp.dot(a, b, precision=highest_precision_mode, preferred_element_type=jnp.float32)

    n = gram.shape[0]
    eye = (
        lax.broadcasted_iota(jnp.int32, (n, n), 0) == lax.broadcasted_iota(jnp.int32, (n, n), 1)
    ).astype(jnp.float32)
    norm = jnp.sqrt(jnp.sum(gram * eye, keepdims=True)) + norm_eps
    a1 = gram / norm / norm
    p1 = coeff_a * eye + coeff_b * a1 + coeff_c * mul(a1, a1)
    a2 = mul(mul(p1, a1), p1)
    p2 = coeff_a * eye + coeff_b * a2 + coeff_c * mul(a2, a2)
    mix = mul(p2, p1) * (scale / norm)
    out_ref[...] = mul(g_ref[...], mix).astype(out_ref.dtype)


def polar(g, grams):
    q, n = g.shape
    return pl.pallas_call(
        lambda *refs: polar_kernel(0.2 * math.sqrt(2 * DHALF), *refs),
        out_shape=jax.ShapeDtypeStruct((q, n), jnp.bfloat16),
        compiler_params=pltpu.CompilerParams(vmem_limit_bytes=16 * 2**20),
    )(g, *grams)


def on_device(
    mixer_vectors,
    upstream_adjoint,
    relative_benefit,
    present_policy_logit,
    behaviour_policy_logit,
    retained_entries,
    tallies,
    keeper_slot,
):
    bf16, f32 = jnp.bfloat16, jnp.float32
    yl, x, z = lax.axis_index("yl"), lax.axis_index("x"), lax.axis_index("z")
    yh, core = lax.axis_index("yh"), lax.axis_index("c")
    q = upstream_adjoint.shape[2]
    barrier = lax.optimization_barrier

    own = [pick_rows(retained_entries, mixer_vectors, piece, PIECES) for piece in range(PIECES)]
    adjoint = upstream_adjoint.transpose(1, 2, 0)
    kept, adjoint, *own = barrier((retained_entries, adjoint, *own))
    rows_of = [
        v[None, :] for v in (relative_benefit, present_policy_logit, behaviour_policy_logit)
    ]
    s_send = scaled_half(1 - yl, tallies[0], kept, *rows_of, adjoint)
    s_keep = scaled_half(yl, tallies[0], kept, *rows_of, adjoint)

    odd = (x + core) % 2
    near = jnp.where((x + odd) % X // 2 == yh, 0, 2)
    far = 2 - near
    plan = jnp.where(
        odd == 1,
        jnp.stack([near + 1, far, near, far + 1]),
        jnp.stack([far, far + 1, near + 1, near]),
    ).astype(jnp.int32)

    def add(*terms):
        return sum([t.astype(f32) for t in terms]).astype(bf16)

    def to_x(terms, ra, rb, beside=()):
        t2, t3 = terms[2:]
        rp = odd_to_even(add(t2, ra), 1)
        rm = odd_to_even(add(t3, rb), -1)
        t2, ra, rm, rp, *beside = barrier((t2, ra, rm, rp, *beside))
        return [even_to_odd_core(add(t2, ra, rm)), t3, rb, rp], beside

    e1, e3 = over_y(own[0], 1), over_y(own[0], 3)
    e1, e3, s_send, s_keep, second = barrier((e1, e3, s_send, s_keep, own[1]))
    opposite = over_y(e1, 3)
    s_recv = over_y(s_send, 1)
    c_keep = shift(s_keep, "c", C, 1)
    opposite, s_recv, c_keep, second = barrier((opposite, s_recv, c_keep, second))
    f1, f3 = over_y(second, 1), over_y(second, 3)
    c_recv = shift(s_recv, "c", C, 1)
    s_list = (s_keep, s_recv, c_keep, c_recv)
    first_terms = partials(plan, s_list, own[0], e1, e3, [opposite])
    cut = second.shape[0] // 2
    ra, rb = shift(first_terms[0], "x", X, 1), shift(first_terms[1], "x", X, -1)
    f1, f3, ra, rb = barrier((f1, f3, ra, rb))
    fa, fb = over_y(f3[:cut], 1), over_y(f1[cut:], 3)
    first_sums, (fa, fb) = to_x(first_terms, ra, rb, (fa, fb))
    second_terms = partials(plan, s_list, second, f1, f3, [fa, fb])
    ra, rb = shift(second_terms[0], "x", X, 1), shift(second_terms[1], "x", X, -1)
    second_sums, _ = to_x(second_terms, ra, rb)

    head = mixer_vectors.shape[1] // Z
    parts = row_blocks(jnp.stack([odd, z]).astype(jnp.int32), first_sums + second_sums)
    got = [shift(parts[d], "z", Z, d) for d in (4, 3, 5, 2, 6, 1, 7)]
    exact, rounded = sum_over_z([parts[0], *got])

    row_of = [rounded] + [shift(rounded, "x", X, d) for d in (1, 2, 3)]
    g = lax.all_to_all(exact, "z", 0, 0, tiled=True).reshape(q, head)
    gram = lax.dot_general(
        g, g, (((0,), (0,)), ((), ())), precision=highest_precision_mode,
        preferred_element_type=f32,
    )
    gram, rounded_rows = barrier((gram, row_of))
    gram = gram + shift(gram, "c", C, 1)
    update = polar(g, [gram] + [over_y(gram, flip) for flip in (2, 1, 3)])

    heads_total = keeper_slot.shape[0]
    heads = jnp.arange(heads_total, dtype=jnp.int32)
    wanted = x * Z + jnp.arange(Z, dtype=jnp.int32)
    source = jnp.sum(
        jnp.where(keeper_slot[None, :] == wanted[:, None], heads[None, :], 0), axis=1
    )
    place = ((x - source // Z) % X * Z + source % Z).astype(jnp.int32)
    chosen = choose(place, rounded_rows)
    arrived = lax.all_to_all(chosen, "z", 0, 0, tiled=True).reshape(q, head)
    gradient = arrived.astype(f32).T
    return (update.T[None], gradient[None])


def solution(mesh):
    wide = Mesh(np.asarray(mesh.devices).reshape(YL, X, Z, YH, C), NAMES)
    dp, mp = ("yl", "x", "z"), ("yh", "c")
    return jax.shard_map(
        on_device,
        mesh=wide,
        in_specs=(
            P(dp, mp),
            P(dp, None, mp),
            P(dp),
            P(dp),
            P(dp),
            P(dp, None),
            P(dp),
            P(),
        ),
        out_specs=(P(dp, None, mp), P(dp, None, mp)),
        check_vma=False,
    )
```

time: 240 us -> 196 us (0.82)
  waiting for transfers between devices: 125 us -> 84.8 us
  Pallas kernels: 12.7 us -> 28 us
  other arithmetic: 16.9 us -> 4.74 us
  starting transfers between devices: 56.7 us -> 65.4 us
  local copies, waits for them, and re-layouts: 16.8 us -> 8.15 us
  matrix products: 6.14 us -> 0.59 us
    ppermute x2 -> x4, waiting for transfers between devices: 25.5 us -> 6.67 us  [odd_to_even(): return lax.ppermute(value, ('x', 'c'), pairs)]
    pallas_call x1 -> x9, Pallas kernels: 11 us -> 25.7 us  [the longest x2 9.4 us: partials(): pl.pallas_call(lambda *refs: partial_kernel(len(opposite), *refs), in_spe...]
    ppermute x5 -> x11, waiting for transfers between devices: 58 us -> 46.7 us  [over_y(): return lax.ppermute(value, ('yl', 'yh'), ring_pairs(flip))]
    ppermute x5 -> x11, starting transfers between devices: 7.15 us -> 18 us  [over_y(): return lax.ppermute(value, ('yl', 'yh'), ring_pairs(flip))]
    ppermute x7 -> x0, starting transfers between devices: 7.54 us -> none  [on_device(): lax.ppermute(gram, ('yl', 'yh', 'c'), [(i, i ^ d) for i in range(8)])]
    gather x2 -> x0, local copies, waits for them, and re-layouts: 5.81 us -> none  [the longest x1 3.58 us: on_device(): own = mixer_vectors.at[kept].get(mode='promise_in_bounds')]
    dot_general x1 -> x0, matrix products: 5.54 us -> none  [on_device(): picked = jnp.dot(adjoint, pick.astype(bf16), preferred_element_type=f32)]
    unnamed x27 -> x44, local copies, waits for them, and re-layouts: 2.88 us -> 8.08 us
  transfers between devices with their start and end apart: 30 -> 36, of which waited for: 21 -> 22; matrix products, arithmetic and copies ran while one was open for 6% -> 2% of each run, Pallas kernels for 1% -> 7%
where the time goes in v2:
time: 196 us; the launch traced here: 193 us
  waiting for transfers between devices  84.8 us (43%)
  starting transfers between devices  65.4 us (33%)
  Pallas kernels  28 us (14%)
  local copies, waits for them, and re-layouts  8.15 us (4%)
  other arithmetic  4.74 us (2%)
    ppermute x11, waiting for transfers between devices, over_y(): return lax.ppermute(value, ('yl', 'yh'), ring_pairs(flip))  46.7 us
    ppermute x17, starting transfers between devices, shift(): lax.ppermute(value, axis, [(i, (i + step) % size) for i in range(size)])  27.4 us
    ppermute x17, waiting for transfers between devices, shift(): lax.ppermute(value, axis, [(i, (i + step) % size) for i in range(size)])  25 us
    ppermute x11, starting transfers between devices, over_y(): return lax.ppermute(value, ('yl', 'yh'), ring_pairs(flip))  18 us
    pallas_call x2, Pallas kernels, partials(): pl.pallas_call(lambda *refs: partial_kernel(len(opposite), *refs), in_spe...  9.4 us
    unnamed x44, local copies, waits for them, and re-layouts  8.08 us
    ppermute x4, waiting for transfers between devices, odd_to_even(): return lax.ppermute(value, ('x', 'c'), pairs)  6.67 us
    pallas_call x2, Pallas kernels, scaled_half(): pl.pallas_call(scale_kernel, grid_spec=pltpu.PrefetchScalarGridSpec(num_s...  5.55 us
  transfers between devices with their start and end apart: 36, of which 22 were waited for; matrix products, arithmetic and copies ran while one was open for 2% of the time, Pallas kernels for 7%

profile of v2, /device:TPU:8, one launch (start us, length us, event | category | flops | bytes accessed | tf_op | source)
XLA Modules:
  0.0 193.3 jit_solution(5678582961200230500)
XLA Ops:
  0.6 1.9 copy-done.1
  3.2 2.6 %shard_map.95.refs_5_ = bf16[768,512]{1,0:T(8,128)(2,1)} custom-call(s32[1,768]{1,0:T(1,128)S(1)} %copy-done.7, bf16[1536,1024]{1,0:T(8,128)(2,1)S(1)} %copy-done.1), custom_call_target="tpu_custom_call" | custom-call | flops 1207959552 | bytes 2359296 | tf_op jit(solution)/shard_map/pallas_call | solution.py:65
  5.8 1.7 shard_map.96.refs_5_
  7.5 0.9 copy-done.3
  8.4 2.2 %collective-permute-start = (bf16[768,512]{1,0:T(8,128)(2,1)}, bf16[768,512]{1,0:T(8,128)(2,1)}, u32[]{:S(2)}, u32[]{:S(2)}) collective-permute-start(bf16[768,512]{1,0:T(8,128)(2,1)} %shard_map.95.refs_5_), channel_id=1, source_target_pairs={{0,128},{128,0},{2,130},{130,2},{1,129},{129,1},{3,131},{131,3},{4... | collective-permute-start | bytes 2359304 | tf_op jit(solution)/shard_map/ppermute | solution.py:33
  12.1 2.8 %shard_map.97 = bf16[448,768]{1,0:T(8,128)(2,1)S(1)} custom-call(s32[2]{0:T(128)S(1)} %get-tuple-element.102.plan, s32[1,768]{1,0:T(1,128)S(1)} %copy-done.8, f32[1,1536]{1,0:T(1,128)S(1)} %broadcast_in_dim.33.benefit_ref, f32[1,1536]{1,0:T(1,128)S(1)} %broadcast_in_dim.34.present_ref, f32[1,1536]{1,0:T(1,128)S(1)} %broadcast_in_dim.35.behaviour_ref, ...), custom_call_target="tpu_custom_call" | custom-call | flops 1056964608 | bytes 2064384 | tf_op jit(solution)/shard_map/pallas_call | solution.py:104
  14.9 2.8 %shard_map.98.refs_1_ = bf16[448,768]{1,0:T(8,128)(2,1)S(1)} custom-call(s32[2]{0:T(128)S(1)} %get-tuple-element.103.plan, s32[1,768]{1,0:T(1,128)S(1)} %copy-done.8, f32[1,1536]{1,0:T(1,128)S(1)} %broadcast_in_dim.33.benefit_ref, f32[1,1536]{1,0:T(1,128)S(1)} %broadcast_in_dim.34.present_ref, f32[1,1536]{1,0:T(1,128)S(1)} %broadcast_in_dim.35.behaviour_ref, ...), custom_call_target="tpu_custom_call" | custom-call | flops 1056964608 | bytes 2064384 | tf_op jit(solution)/shard_map/pallas_call | solution.py:104
  17.7 10.3 %collective-permute-done.refs_6_ = bf16[768,512]{1,0:T(8,128)(2,1)} collective-permute-done((bf16[768,512]{1,0:T(8,128)(2,1)}, bf16[768,512]{1,0:T(8,128)(2,1)}, u32[]{:S(2)}, u32[]{:S(2)}) %collective-permute-start) | collective-permute-done | bytes 786464 | tf_op jit(solution)/shard_map/ppermute | solution.py:33
  28.0 0.9 collective-permute-done.1.refs_7_
  28.9 1.7 collective-permute-start.2
  30.6 2.6 %collective-permute-start.3 = (bf16[448,768]{1,0:T(8,128)(2,1)S(1)}, bf16[448,768]{1,0:T(8,128)(2,1)S(1)}, u32[]{:S(2)}, u32[]{:S(2)}) collective-permute-start(bf16[448,768]{1,0:T(8,128)(2,1)S(1)} %shard_map.97), channel_id=1, source_target_pairs={{0,128},{128,0},{2,130},{130,2},{1,129},{129,1},{3,131},{131,3},{4... | collective-permute-start | bytes 2064392 | tf_op jit(solution)/shard_map/ppermute | solution.py:33
  33.2 14.0 %collective-permute-done.3.refs_2_ = bf16[448,768]{1,0:T(8,128)(2,1)S(1)} collective-permute-done((bf16[448,768]{1,0:T(8,128)(2,1)S(1)}, bf16[448,768]{1,0:T(8,128)(2,1)S(1)}, u32[]{:S(2)}, u32[]{:S(2)}) %collective-permute-start.3) | collective-permute-done | bytes 688160 | tf_op jit(solution)/shard_map/ppermute | solution.py:33
  47.2 0.9 copy-done.5
  48.0 2.3 %collective-permute-start.6 = (bf16[768,512]{1,0:T(8,128)(2,1)}, bf16[768,512]{1,0:T(8,128)(2,1)S(1)}, u32[]{:S(2)}, u32[]{:S(2)}) collective-permute-start(bf16[768,512]{1,0:T(8,128)(2,1)} %copy-done.3), channel_id=1, source_target_pairs={{0,128},{128,0},{2,130},{130,2},{1,129},{129,1},{3,131},{131,3},{4... | collective-permute-start | bytes 2359304 | tf_op jit(solution)/shard_map/ppermute | solution.py:33
  50.3 1.8 collective-permute-start.7
  52.2 1.1 copy-done.6
  53.3 4.9 %shard_map.99 = (bf16[448,512]{1,0:T(8,128)(2,1)S(1)}, bf16[448,512]{1,0:T(8,128)(2,1)S(1)}, bf16[448,512]{1,0:T(8,128)(2,1)S(1)}, bf16[448,512]{1,0:T(8,128)(2,1)S(1)}) custom-call(s32[4]{0:T(128)S(1)} %broadcast_select_fusion.refs_0_, bf16[448,768]{1,0:T(8,128)(2,1)S(1)} %shard_map.98.refs_1_, bf16[448,768]{1,0:T(8,128)(2,1)S(1)} %collective-permute-done.3.refs_2_, ...), custom_call_target="tpu_custom_call" | custom-call | flops 2818572288 | bytes 8388608 | tf_op jit(solution)/shard_map/pallas_call | solution.py:164
  58.2 1.6 collective-permute-start.8
  59.8 1.7 collective-permute-start.9
  61.6 7.2 %collective-permute-done.6.refs_6_ = bf16[768,512]{1,0:T(8,128)(2,1)S(1)} collective-permute-done((bf16[768,512]{1,0:T(8,128)(2,1)}, bf16[768,512]{1,0:T(8,128)(2,1)S(1)}, u32[]{:S(2)}, u32[]{:S(2)}) %collective-permute-start.6) | collective-permute-done | bytes 786464 | tf_op jit(solution)/shard_map/ppermute | solution.py:33
  68.8 1.5 collective-permute-done.7.refs_7_
  70.3 1.6 collective-permute-done.8
  72.0 1.3 collective-permute-start.10
  73.5 1.3 collective-permute-start.11
  74.8 1.0 collective-permute-start.12
  75.8 1.6 collective-permute-start.13
  77.4 8.3 %collective-permute-done.12.refs_8_ = bf16[384,512]{1,0:T(8,128)(2,1)S(1)} collective-permute-done((bf16[384,512]{1,0:T(8,128)(2,1)S(1)}, bf16[384,512]{1,0:T(8,128)(2,1)S(1)}, u32[]{:S(2)}, u32[]{:S(2)}) %collective-permute-start.12) | collective-permute-done | bytes 393248 | tf_op jit(solution)/shard_map/ppermute | solution.py:33
  85.7 1.0 collective-permute-done.13.refs_9_
  86.7 4.5 %shard_map.100 = (bf16[448,512]{1,0:T(8,128)(2,1)S(1)}, bf16[448,512]{1,0:T(8,128)(2,1)S(1)}, bf16[448,512]{1,0:T(8,128)(2,1)S(1)}, bf16[448,512]{1,0:T(8,128)(2,1)S(1)}) custom-call(s32[4]{0:T(128)S(1)} %broadcast_select_fusion.refs_0_, bf16[448,768]{1,0:T(8,128)(2,1)S(1)} %shard_map.98.refs_1_, bf16[448,768]{1,0:T(8,128)(2,1)S(1)} %collective-permute-done.3.refs_2_, ...), custom_call_target="tpu_custom_call" | custom-call | flops 2818572288 | bytes 8388608 | tf_op jit(solution)/shard_map/pallas_call | solution.py:164
  91.2 2.1 %collective-permute-start.16 = (bf16[448,512]{1,0:T(8,128)(2,1)S(1)}, bf16[448,512]{1,0:T(8,128)(2,1)S(1)}, u32[]{:S(2)}, u32[]{:S(2)}) collective-permute-start(bf16[448,512]{1,0:T(8,128)(2,1)S(1)} %get-tuple-element.82), channel_id=1, source_target_pairs={{0,96},{32,0},{64,32},{96,64},{1,97},{33,1},{65,33},{97,65},{2,98}... | collective-permute-start | bytes 1376264 | tf_op jit(solution)/shard_map/ppermute | solution.py:37
  93.3 11.3 %collective-permute-done.16.refs_7_ = bf16[448,512]{1,0:T(8,128)(2,1)S(1)} collective-permute-done((bf16[448,512]{1,0:T(8,128)(2,1)S(1)}, bf16[448,512]{1,0:T(8,128)(2,1)S(1)}, u32[]{:S(2)}, u32[]{:S(2)}) %collective-permute-start.16) | collective-permute-done | bytes 458784 | tf_op jit(solution)/shard_map/ppermute | solution.py:37
  104.7 1.3 collective-permute-start.17
  106.2 1.3 collective-permute-start.18
  107.5 0.9 add_convert_fusion.3
  108.4 2.9 %collective-permute-start.14 = (bf16[448,512]{1,0:T(8,128)(2,1)}, bf16[448,512]{1,0:T(8,128)(2,1)S(1)}, u32[]{:S(2)}, u32[]{:S(2)}) collective-permute-start(bf16[448,512]{1,0:T(8,128)(2,1)} %add_convert_fusion.3), channel_id=1, source_target_pairs={{0,1},{33,32},{64,65},{97,96},{2,3},{35,34},{66,67},{99,98},{4,5},... | collective-permute-start | bytes 1376264 | tf_op jit(solution)/shard_map/ppermute | solution.py:49
  111.3 3.7 %collective-permute-done.17 = bf16[448,512]{1,0:T(8,128)(2,1)S(1)} collective-permute-done((bf16[448,512]{1,0:T(8,128)(2,1)S(1)}, bf16[448,512]{1,0:T(8,128)(2,1)S(1)}, u32[]{:S(2)}, u32[]{:S(2)}) %collective-permute-start.17) | collective-permute-done | bytes 458784 | tf_op jit(solution)/shard_map/ppermute | solution.py:44
  115.1 2.9 %collective-permute-done.18.refs_8_ = bf16[448,512]{1,0:T(8,128)(2,1)S(1)} collective-permute-done((bf16[448,512]{1,0:T(8,128)(2,1)S(1)}, bf16[448,512]{1,0:T(8,128)(2,1)S(1)}, u32[]{:S(2)}, u32[]{:S(2)}) %collective-permute-start.18) | collective-permute-done | bytes 458784 | tf_op jit(solution)/shard_map/ppermute | solution.py:44
  118.0 1.0 add_convert_fusion
  119.0 2.1 %collective-permute-start.19 = (bf16[448,512]{1,0:T(8,128)(2,1)}, bf16[448,512]{1,0:T(8,128)(2,1)}, u32[]{:S(2)}, u32[]{:S(2)}) collective-permute-start(bf16[448,512]{1,0:T(8,128)(2,1)} %add_convert_fusion), channel_id=1, source_target_pairs={{0,1},{33,32},{64,65},{97,96},{2,3},{35,34},{66,67},{99,98},{4,5},... | collective-permute-start | bytes 1376264 | tf_op jit(solution)/shard_map/ppermute | solution.py:49
  121.1 0.9 collective-permute-done.19.refs_5_
  122.0 2.1 %shard_map.101 = (f32[56,1024]{1,0:T(8,128)S(1)}, bf16[56,1024]{1,0:T(8,128)(2,1)S(1)}, bf16[56,1024]{1,0:T(8,128)(2,1)}, bf16[56,1024]{1,0:T(8,128)(2,1)S(1)}, ...) custom-call(s32[2]{0:T(128)S(1)} %pad_add_fusion.refs_0_, ...), custom_call_target="tpu_custom_call" | custom-call | tf_op jit(solution)/shard_map/pallas_call | solution.py:209
  124.9 7.2 %collective-permute-start.20 = (bf16[56,1024]{1,0:T(8,128)(2,1)S(1)}, bf16[56,1024]{1,0:T(8,128)(2,1)S(1)}, u32[]{:S(2)}, u32[]{:S(2)}) collective-permute-start(bf16[56,1024]{1,0:T(8,128)(2,1)S(1)} %get-tuple-element.88), channel_id=1, source_target_pairs={{0,16},{4,20},{8,24},{12,28},{16,0},{20,4},{24,8},{28,12},{1,17},{... | collective-permute-start | bytes 344072 | tf_op jit(solution)/shard_map/ppermute | solution.py:37
  132.0 1.9 %collective-permute-start.21 = (bf16[56,1024]{1,0:T(8,128)(2,1)S(1)}, bf16[56,1024]{1,0:T(8,128)(2,1)S(1)}, u32[]{:S(2)}, u32[]{:S(2)}) collective-permute-start(bf16[56,1024]{1,0:T(8,128)(2,1)S(1)} %get-tuple-element.89), channel_id=1, source_target_pairs={{0,12},{4,16},{8,20},{12,24},{16,28},{20,0},{24,4},{28,8},{1,13},{... | collective-permute-start | bytes 344072 | tf_op jit(solution)/shard_map/ppermute | solution.py:37
  134.0 3.1 %collective-permute-start.22 = (bf16[56,1024]{1,0:T(8,128)(2,1)}, bf16[56,1024]{1,0:T(8,128)(2,1)S(1)}, u32[]{:S(2)}, u32[]{:S(2)}) collective-permute-start(bf16[56,1024]{1,0:T(8,128)(2,1)} %get-tuple-element.90), channel_id=1, source_target_pairs={{0,20},{4,24},{8,28},{12,0},{16,4},{20,8},{24,12},{28,16},{1,21},{... | collective-permute-start | bytes 344072 | tf_op jit(solution)/shard_map/ppermute | solution.py:37
  137.1 1.4 collective-permute-start.23
  138.5 2.7 %collective-permute-start.24 = (bf16[56,1024]{1,0:T(8,128)(2,1)S(1)}, bf16[56,1024]{1,0:T(8,128)(2,1)S(1)}, u32[]{:S(2)}, u32[]{:S(2)}) collective-permute-start(bf16[56,1024]{1,0:T(8,128)(2,1)S(1)} %get-tuple-element.92), channel_id=1, source_target_pairs={{0,24},{4,28},{8,0},{12,4},{16,8},{20,12},{24,16},{28,20},{1,25},{... | collective-permute-start | bytes 344072 | tf_op jit(solution)/shard_map/ppermute | solution.py:37
  141.2 1.0 collective-permute-start.25
  142.2 4.8 %collective-permute-done.21.refs_2_ = bf16[56,1024]{1,0:T(8,128)(2,1)S(1)} collective-permute-done((bf16[56,1024]{1,0:T(8,128)(2,1)S(1)}, bf16[56,1024]{1,0:T(8,128)(2,1)S(1)}, u32[]{:S(2)}, u32[]{:S(2)}) %collective-permute-start.21) | collective-permute-done | bytes 114720 | tf_op jit(solution)/shard_map/ppermute | solution.py:37
  147.6 1.1 collective-permute-done.23.refs_4_
  148.7 2.6 %collective-permute-done.24.refs_5_ = bf16[56,1024]{1,0:T(8,128)(2,1)S(1)} collective-permute-done((bf16[56,1024]{1,0:T(8,128)(2,1)S(1)}, bf16[56,1024]{1,0:T(8,128)(2,1)S(1)}, u32[]{:S(2)}, u32[]{:S(2)}) %collective-permute-start.24) | collective-permute-done | bytes 114720 | tf_op jit(solution)/shard_map/ppermute | solution.py:37
  151.3 1.6 collective-permute-done.25.refs_6_
  154.2 2.2 %shard_map.102 = (f32[8,56,128]{2,1,0:T(8,128)}, bf16[8,56,128]{2,1,0:T(8,128)(2,1)}) custom-call(f32[56,1024]{1,0:T(8,128)} %copy-done, bf16[56,1024]{1,0:T(8,128)(2,1)} %copy-done.9, bf16[56,1024]{1,0:T(8,128)(2,1)} %copy-done.10, bf16[56,1024]{1,0:T(8,128)(2,1)} %copy-done.11, bf16[56,1024]{1,0:T(8,128)(2,1)} %copy-done.12, bf16[56,1024]{1,0:T(8,128)(2,1)} %copy-done.13, ...), custom_call_target="tpu_custom_call" | custom-call | tf_op jit(solution)/shard_map/pallas_call | solution.py:235
  156.3 4.9 %all-to-all-start = ((f32[8,56,128]{2,1,0:T(8,128)}), f32[8,56,128]{2,1,0:T(8,128)S(1)}, u32[]{:S(2)}, u32[]{:S(2)}) async-start(f32[8,56,128]{2,1,0:T(8,128)} %get-tuple-element.95), calls=%async_computation | async-start | bytes 458752 | tf_op jit(solution)/shard_map/all_to_all | solution.py:364
  161.2 0.8 select_reduce_fusion
  162.6 1.9 %collective-permute-start.28 = (bf16[8,56,128]{2,1,0:T(8,128)(2,1)}, bf16[8,56,128]{2,1,0:T(8,128)(2,1)S(1)}, u32[]{:S(2)}, u32[]{:S(2)}) collective-permute-start(bf16[8,56,128]{2,1,0:T(8,128)(2,1)} %get-tuple-element.98.refs_0_), channel_id=1, source_target_pairs={{0,64},{32,96},{64,0},{96,32},{1,65},{33,97},{65,1},{97,33},{2,66}... | collective-permute-start | bytes 344072 | tf_op jit(solution)/shard_map/ppermute | solution.py:37
  164.5 2.1 %collective-permute-start.29 = (bf16[8,56,128]{2,1,0:T(8,128)(2,1)}, bf16[8,56,128]{2,1,0:T(8,128)(2,1)S(1)}, u32[]{:S(2)}, u32[]{:S(2)}) collective-permute-start(bf16[8,56,128]{2,1,0:T(8,128)(2,1)} %get-tuple-element.98.refs_0_), channel_id=1, source_target_pairs={{0,96},{32,0},{64,32},{96,64},{1,97},{33,1},{65,33},{97,65},{2,98}... | collective-permute-start | bytes 344072 | tf_op jit(solution)/shard_map/ppermute | solution.py:37
  166.7 5.5 %all-to-all-done = f32[8,56,128]{2,1,0:T(8,128)S(1)} async-done(((f32[8,56,128]{2,1,0:T(8,128)}), f32[8,56,128]{2,1,0:T(8,128)S(1)}, u32[]{:S(2)}, u32[]{:S(2)}) %all-to-all-start) | async-done | bytes 229408 | tf_op jit(solution)/shard_map/all_to_all | solution.py:364
  174.1 2.2 %shard_map.104 = bf16[8,56,128]{2,1,0:T(8,128)(2,1)} custom-call(s32[8]{0:T(128)} %fusion.place, bf16[8,56,128]{2,1,0:T(8,128)(2,1)} %get-tuple-element.98.refs_0_, bf16[8,56,128]{2,1,0:T(8,128)(2,1)} %copy-done.16, bf16[8,56,128]{2,1,0:T(8,128)(2,1)} %copy-done.17, bf16[8,56,128]{2,1,0:T(8,128)(2,1)} %copy-done.18), custom_call_target="tpu_custom_call" | custom-call | tf_op jit(solution)/shard_map/pallas_call | solution.py:256
  176.3 5.0 %all-to-all-start.1 = ((bf16[8,56,128]{2,1,0:T(8,128)(2,1)}), bf16[8,56,128]{2,1,0:T(8,128)(2,1)S(1)}, u32[]{:S(2)}, u32[]{:S(2)}) async-start(bf16[8,56,128]{2,1,0:T(8,128)(2,1)} %shard_map.104), calls=%async_computation.1 | async-start | bytes 229376 | tf_op jit(solution)/shard_map/all_to_all | solution.py:381
  181.4 1.2 collective-permute-done.30
  182.6 2.4 %collective-permute-start.31 = (f32[128,128]{1,0:T(8,128)S(1)}, f32[128,128]{1,0:T(8,128)S(1)}, u32[]{:S(2)}, u32[]{:S(2)}) collective-permute-start(f32[128,128]{1,0:T(8,128)S(1)} %add.88.refs_1_), channel_id=1, source_target_pairs={{0,2},{128,130},{2,0},{130,128},{1,3},{129,131},{3,1},{131,129},{4... | collective-permute-start | bytes 196616 | tf_op jit(solution)/shard_map/ppermute | solution.py:33
  185.1 1.0 collective-permute-start.32
  186.8 2.0 %collective-permute-done.31.refs_2_ = f32[128,128]{1,0:T(8,128)S(1)} collective-permute-done((f32[128,128]{1,0:T(8,128)S(1)}, f32[128,128]{1,0:T(8,128)S(1)}, u32[]{:S(2)}, u32[]{:S(2)}) %collective-permute-start.31) | collective-permute-done | bytes 65568 | tf_op jit(solution)/shard_map/ppermute | solution.py:33
  190.4 2.2 %shard_map.103 = bf16[448,128]{1,0:T(8,128)(2,1)} custom-call(f32[448,128]{1,0:T(8,128)S(1)} %bitcast.24, f32[128,128]{1,0:T(8,128)S(1)} %add.88.refs_1_, f32[128,128]{1,0:T(8,128)S(1)} %collective-permute-done.31.refs_2_, f32[128,128]{1,0:T(8,128)S(1)} %collective-permute-done.32.refs_3_, f32[128,128]{1,0:T(8,128)S(1)} %collective-permute-done.33.refs_4_), custom_call_target="tpu_custom_call" | custom-call | tf_op jit(solution)/shard_map/pallas_call | solution.py:288
  (82 shorter events, 10.3 us)
Async XLA Ops:
  0.6 1.9 copy-start.1
  2.5 0.7 copy-start.7
  5.8 6.2 %copy-start.19 = (f32[1536]{0:T(1024)S(1)}, f32[1536]{0:T(1024)}, u32[]{:S(2)}) copy-start(f32[1536]{0:T(1024)} %param.10) | copy-start | bytes 18436
  5.8 6.2 %copy-start.20 = (f32[1536]{0:T(1024)S(1)}, f32[1536]{0:T(1024)}, u32[]{:S(2)}) copy-start(f32[1536]{0:T(1024)} %param.11) | copy-start | bytes 18436
  5.8 6.2 %copy-start.21 = (f32[1536]{0:T(1024)S(1)}, f32[1536]{0:T(1024)}, u32[]{:S(2)}) copy-start(f32[1536]{0:T(1024)} %param.12) | copy-start | bytes 18436
  5.8 6.3 %copy-start.2 = (bf16[1536,2,448]{0,2,1:T(8,128)(2,1)S(1)}, bf16[1536,2,448]{0,2,1:T(8,128)(2,1)}, u32[]{:S(2)}) copy-start(bf16[1536,2,448]{0,2,1:T(8,128)(2,1)} %param.9) | copy-start | bytes 8257540
  5.8 6.3 %copy-start.8 = (s32[1,768]{1,0:T(1,128)S(1)}, s32[1,768]{1,0:T(1,128)}, u32[]{:S(2)}) copy-start(s32[1,768]{1,0:T(1,128)} %kept_ref.5) | copy-start | bytes 9220
  7.5 0.9 copy-start.3
  8.4 19.6 %collective-permute-start = (bf16[768,512]{1,0:T(8,128)(2,1)}, bf16[768,512]{1,0:T(8,128)(2,1)}, u32[]{:S(2)}, u32[]{:S(2)}) collective-permute-start(bf16[768,512]{1,0:T(8,128)(2,1)} %shard_map.95.refs_5_), channel_id=1, source_target_pairs={{0,128},{128,0},{2,130},{130,2},{1,129},{129,1},{3,131},{131,3},{4... | collective-permute-start | bytes 2359304 | tf_op jit(solution)/shard_map/ppermute | solution.py:33
  10.6 18.3 %collective-permute-start.1 = (bf16[768,512]{1,0:T(8,128)(2,1)}, bf16[768,512]{1,0:T(8,128)(2,1)}, u32[]{:S(2)}, u32[]{:S(2)}) collective-permute-start(bf16[768,512]{1,0:T(8,128)(2,1)} %shard_map.95.refs_5_), channel_id=1, source_target_pairs={{0,130},{128,2},{2,128},{130,0},{1,131},{129,3},{3,129},{131,1},{4... | collective-permute-start | bytes 2359304 | tf_op jit(solution)/shard_map/ppermute | solution.py:33
  28.9 19.1 %collective-permute-start.2 = (bf16[768,512]{1,0:T(8,128)(2,1)}, bf16[768,512]{1,0:T(8,128)(2,1)S(1)}, u32[]{:S(2)}, u32[]{:S(2)}) collective-permute-start(bf16[768,512]{1,0:T(8,128)(2,1)} %collective-permute-done.refs_6_), channel_id=1, source_target_pairs={{0,130},{128,2},{2,128},{130,0},{1,131},{129,3},{3,129},{131,1},{4... | collective-permute-start | bytes 2359304 | tf_op jit(solution)/shard_map/ppermute | solution.py:33
  30.6 16.5 %collective-permute-start.3 = (bf16[448,768]{1,0:T(8,128)(2,1)S(1)}, bf16[448,768]{1,0:T(8,128)(2,1)S(1)}, u32[]{:S(2)}, u32[]{:S(2)}) collective-permute-start(bf16[448,768]{1,0:T(8,128)(2,1)S(1)} %shard_map.97), channel_id=1, source_target_pairs={{0,128},{128,0},{2,130},{130,2},{1,129},{129,1},{3,131},{131,3},{4... | collective-permute-start | bytes 2064392 | tf_op jit(solution)/shard_map/ppermute | solution.py:33
  33.2 14.0 %collective-permute-start.4 = (bf16[448,768]{1,0:T(8,128)(2,1)S(1)}, bf16[448,768]{1,0:T(8,128)(2,1)S(1)}, u32[]{:S(2)}, u32[]{:S(2)}) collective-permute-start(bf16[448,768]{1,0:T(8,128)(2,1)S(1)} %shard_map.98.refs_1_), channel_id=1, source_target_pairs={{0,1},{1,0},{2,3},{3,2},{4,5},{5,4},{6,7},{7,6},{8,9},{9,8},{10,11... | collective-permute-start | bytes 2064392 | tf_op jit(solution)/shard_map/ppermute | solution.py:37
  47.2 0.9 copy-start.5
  48.0 4.2 %collective-permute-start.5 = (bf16[448,768]{1,0:T(8,128)(2,1)S(1)}, bf16[448,768]{1,0:T(8,128)(2,1)}, u32[]{:S(2)}, u32[]{:S(2)}) collective-permute-start(bf16[448,768]{1,0:T(8,128)(2,1)S(1)} %collective-permute-done.3.refs_2_), channel_id=1, source_target_pairs={{0,1},{1,0},{2,3},{3,2},{4,5},{5,4},{6,7},{7,6},{8,9},{9,8},{10,11... | collective-permute-start | bytes 2064392 | tf_op jit(solution)/shard_map/ppermute | solution.py:37
  48.0 20.7 %collective-permute-start.6 = (bf16[768,512]{1,0:T(8,128)(2,1)}, bf16[768,512]{1,0:T(8,128)(2,1)S(1)}, u32[]{:S(2)}, u32[]{:S(2)}) collective-permute-start(bf16[768,512]{1,0:T(8,128)(2,1)} %copy-done.3), channel_id=1, source_target_pairs={{0,128},{128,0},{2,130},{130,2},{1,129},{129,1},{3,131},{131,3},{4... | collective-permute-start | bytes 2359304 | tf_op jit(solution)/shard_map/ppermute | solution.py:33
  50.3 19.9 %collective-permute-start.7 = (bf16[768,512]{1,0:T(8,128)(2,1)}, bf16[768,512]{1,0:T(8,128)(2,1)S(1)}, u32[]{:S(2)}, u32[]{:S(2)}) collective-permute-start(bf16[768,512]{1,0:T(8,128)(2,1)} %copy-done.3), channel_id=1, source_target_pairs={{0,130},{128,2},{2,128},{130,0},{1,131},{129,3},{3,129},{131,1},{4... | collective-permute-start | bytes 2359304 | tf_op jit(solution)/shard_map/ppermute | solution.py:33
  52.2 1.1 copy-start.6
  58.2 28.5 %copy-start.4 = (bf16[768,512]{1,0:T(8,128)(2,1)S(1)}, bf16[768,512]{1,0:T(8,128)(2,1)}, u32[]{:S(2)}) copy-start(bf16[768,512]{1,0:T(8,128)(2,1)} %copy-done.3) | copy-start | bytes 2359300
  58.2 13.7 %collective-permute-start.8 = (bf16[448,512]{1,0:T(8,128)(2,1)S(1)}, bf16[448,512]{1,0:T(8,128)(2,1)S(1)}, u32[]{:S(2)}, u32[]{:S(2)}) collective-permute-start(bf16[448,512]{1,0:T(8,128)(2,1)S(1)} %get-tuple-element.66), channel_id=1, source_target_pairs={{0,32},{32,64},{64,96},{96,0},{1,33},{33,65},{65,97},{97,1},{2,34}... | collective-permute-start | bytes 1376264 | tf_op jit(solution)/shard_map/ppermute | solution.py:37
  59.8 12.1 %collective-permute-start.9 = (bf16[448,512]{1,0:T(8,128)(2,1)S(1)}, bf16[448,512]{1,0:T(8,128)(2,1)S(1)}, u32[]{:S(2)}, u32[]{:S(2)}) collective-permute-start(bf16[448,512]{1,0:T(8,128)(2,1)S(1)} %get-tuple-element.67), channel_id=1, source_target_pairs={{0,96},{32,0},{64,32},{96,64},{1,97},{33,1},{65,33},{97,65},{2,98}... | collective-permute-start | bytes 1376264 | tf_op jit(solution)/shard_map/ppermute | solution.py:37
  72.0 14.6 %collective-permute-start.10 = (bf16[448,512]{1,0:T(8,128)(2,1)S(1)}, bf16[448,512]{1,0:T(8,128)(2,1)S(1)}, u32[]{:S(2)}, u32[]{:S(2)}) collective-permute-start(bf16[448,512]{1,0:T(8,128)(2,1)S(1)} %add_convert_fusion.5), channel_id=1, source_target_pairs={{1,97},{32,0},{65,33},{96,64},{3,99},{34,2},{67,35},{98,66},{5,101... | collective-permute-start | bytes 1376264 | tf_op jit(solution)/shard_map/ppermute | solution.py:44
  73.5 13.2 %collective-permute-start.11 = (bf16[448,512]{1,0:T(8,128)(2,1)S(1)}, bf16[448,512]{1,0:T(8,128)(2,1)S(1)}, u32[]{:S(2)}, u32[]{:S(2)}) collective-permute-start(bf16[448,512]{1,0:T(8,128)(2,1)S(1)} %add_convert_fusion.4), channel_id=1, source_target_pairs={{1,33},{32,64},{65,97},{96,0},{3,35},{34,66},{67,99},{98,2},{5,37}... | collective-permute-start | bytes 1376264 | tf_op jit(solution)/shard_map/ppermute | solution.py:44
  74.8 10.9 %collective-permute-start.12 = (bf16[384,512]{1,0:T(8,128)(2,1)S(1)}, bf16[384,512]{1,0:T(8,128)(2,1)S(1)}, u32[]{:S(2)}, u32[]{:S(2)}) collective-permute-start(bf16[384,512]{1,0:T(8,128)(2,1)S(1)} %slice.6), channel_id=1, source_target_pairs={{0,128},{128,0},{2,130},{130,2},{1,129},{129,1},{3,131},{131,3},{4... | collective-permute-start | bytes 1179656 | tf_op jit(solution)/shard_map/ppermute | solution.py:33
  75.8 10.9 %collective-permute-start.13 = (bf16[384,512]{1,0:T(8,128)(2,1)S(1)}, bf16[384,512]{1,0:T(8,128)(2,1)S(1)}, u32[]{:S(2)}, u32[]{:S(2)}) collective-permute-start(bf16[384,512]{1,0:T(8,128)(2,1)S(1)} %slice.7), channel_id=1, source_target_pairs={{0,130},{128,2},{2,128},{130,0},{1,131},{129,3},{3,129},{131,1},{4... | collective-permute-start | bytes 1179656 | tf_op jit(solution)/shard_map/ppermute | solution.py:33
  91.2 13.4 %collective-permute-start.16 = (bf16[448,512]{1,0:T(8,128)(2,1)S(1)}, bf16[448,512]{1,0:T(8,128)(2,1)S(1)}, u32[]{:S(2)}, u32[]{:S(2)}) collective-permute-start(bf16[448,512]{1,0:T(8,128)(2,1)S(1)} %get-tuple-element.82), channel_id=1, source_target_pairs={{0,96},{32,0},{64,32},{96,64},{1,97},{33,1},{65,33},{97,65},{2,98}... | collective-permute-start | bytes 1376264 | tf_op jit(solution)/shard_map/ppermute | solution.py:37
  93.2 12.8 %collective-permute-start.15 = (bf16[448,512]{1,0:T(8,128)(2,1)S(1)}, bf16[448,512]{1,0:T(8,128)(2,1)S(1)}, u32[]{:S(2)}, u32[]{:S(2)}) collective-permute-start(bf16[448,512]{1,0:T(8,128)(2,1)S(1)} %get-tuple-element.80), channel_id=1, source_target_pairs={{0,32},{32,64},{64,96},{96,0},{1,33},{33,65},{65,97},{97,1},{2,34}... | collective-permute-start | bytes 1376264 | tf_op jit(solution)/shard_map/ppermute | solution.py:37
  104.7 10.4 %collective-permute-start.17 = (bf16[448,512]{1,0:T(8,128)(2,1)S(1)}, bf16[448,512]{1,0:T(8,128)(2,1)S(1)}, u32[]{:S(2)}, u32[]{:S(2)}) collective-permute-start(bf16[448,512]{1,0:T(8,128)(2,1)S(1)} %add_convert_fusion.2), channel_id=1, source_target_pairs={{1,97},{32,0},{65,33},{96,64},{3,99},{34,2},{67,35},{98,66},{5,101... | collective-permute-start | bytes 1376264 | tf_op jit(solution)/shard_map/ppermute | solution.py:44
  106.2 11.8 %collective-permute-start.18 = (bf16[448,512]{1,0:T(8,128)(2,1)S(1)}, bf16[448,512]{1,0:T(8,128)(2,1)S(1)}, u32[]{:S(2)}, u32[]{:S(2)}) collective-permute-start(bf16[448,512]{1,0:T(8,128)(2,1)S(1)} %add_convert_fusion.1), channel_id=1, source_target_pairs={{1,33},{32,64},{65,97},{96,0},{3,35},{34,66},{67,99},{98,2},{5,37}... | collective-permute-start | bytes 1376264 | tf_op jit(solution)/shard_map/ppermute | solution.py:44
  108.4 12.7 %collective-permute-start.14 = (bf16[448,512]{1,0:T(8,128)(2,1)}, bf16[448,512]{1,0:T(8,128)(2,1)S(1)}, u32[]{:S(2)}, u32[]{:S(2)}) collective-permute-start(bf16[448,512]{1,0:T(8,128)(2,1)} %add_convert_fusion.3), channel_id=1, source_target_pairs={{0,1},{33,32},{64,65},{97,96},{2,3},{35,34},{66,67},{99,98},{4,5},... | collective-permute-start | bytes 1376264 | tf_op jit(solution)/shard_map/ppermute | solution.py:49
  119.0 3.1 %collective-permute-start.19 = (bf16[448,512]{1,0:T(8,128)(2,1)}, bf16[448,512]{1,0:T(8,128)(2,1)}, u32[]{:S(2)}, u32[]{:S(2)}) collective-permute-start(bf16[448,512]{1,0:T(8,128)(2,1)} %add_convert_fusion), channel_id=1, source_target_pairs={{0,1},{33,32},{64,65},{97,96},{2,3},{35,34},{66,67},{99,98},{4,5},... | collective-permute-start | bytes 1376264 | tf_op jit(solution)/shard_map/ppermute | solution.py:49
  124.2 0.7 copy-start
  124.9 16.3 %collective-permute-start.20 = (bf16[56,1024]{1,0:T(8,128)(2,1)S(1)}, bf16[56,1024]{1,0:T(8,128)(2,1)S(1)}, u32[]{:S(2)}, u32[]{:S(2)}) collective-permute-start(bf16[56,1024]{1,0:T(8,128)(2,1)S(1)} %get-tuple-element.88), channel_id=1, source_target_pairs={{0,16},{4,20},{8,24},{12,28},{16,0},{20,4},{24,8},{28,12},{1,17},{... | collective-permute-start | bytes 344072 | tf_op jit(solution)/shard_map/ppermute | solution.py:37
  132.0 15.0 %collective-permute-start.21 = (bf16[56,1024]{1,0:T(8,128)(2,1)S(1)}, bf16[56,1024]{1,0:T(8,128)(2,1)S(1)}, u32[]{:S(2)}, u32[]{:S(2)}) collective-permute-start(bf16[56,1024]{1,0:T(8,128)(2,1)S(1)} %get-tuple-element.89), channel_id=1, source_target_pairs={{0,12},{4,16},{8,20},{12,24},{16,28},{20,0},{24,4},{28,8},{1,13},{... | collective-permute-start | bytes 344072 | tf_op jit(solution)/shard_map/ppermute | solution.py:37
  134.0 13.6 %collective-permute-start.22 = (bf16[56,1024]{1,0:T(8,128)(2,1)}, bf16[56,1024]{1,0:T(8,128)(2,1)S(1)}, u32[]{:S(2)}, u32[]{:S(2)}) collective-permute-start(bf16[56,1024]{1,0:T(8,128)(2,1)} %get-tuple-element.90), channel_id=1, source_target_pairs={{0,20},{4,24},{8,28},{12,0},{16,4},{20,8},{24,12},{28,16},{1,21},{... | collective-permute-start | bytes 344072 | tf_op jit(solution)/shard_map/ppermute | solution.py:37
  137.1 11.6 %collective-permute-start.23 = (bf16[56,1024]{1,0:T(8,128)(2,1)}, bf16[56,1024]{1,0:T(8,128)(2,1)S(1)}, u32[]{:S(2)}, u32[]{:S(2)}) collective-permute-start(bf16[56,1024]{1,0:T(8,128)(2,1)} %get-tuple-element.91), channel_id=1, source_target_pairs={{0,8},{4,12},{8,16},{12,20},{16,24},{20,28},{24,0},{28,4},{1,9},{5... | collective-permute-start | bytes 344072 | tf_op jit(solution)/shard_map/ppermute | solution.py:37
  138.5 12.8 %collective-permute-start.24 = (bf16[56,1024]{1,0:T(8,128)(2,1)S(1)}, bf16[56,1024]{1,0:T(8,128)(2,1)S(1)}, u32[]{:S(2)}, u32[]{:S(2)}) collective-permute-start(bf16[56,1024]{1,0:T(8,128)(2,1)S(1)} %get-tuple-element.92), channel_id=1, source_target_pairs={{0,24},{4,28},{8,0},{12,4},{16,8},{20,12},{24,16},{28,20},{1,25},{... | collective-permute-start | bytes 344072 | tf_op jit(solution)/shard_map/ppermute | solution.py:37
  141.2 12.3 %copy-start.9 = (bf16[56,1024]{1,0:T(8,128)(2,1)}, bf16[56,1024]{1,0:T(8,128)(2,1)S(1)}, u32[]{:S(2)}) copy-start(bf16[56,1024]{1,0:T(8,128)(2,1)S(1)} %collective-permute-done.20.refs_1_) | copy-start | bytes 344068
  141.2 11.7 %collective-permute-start.25 = (bf16[56,1024]{1,0:T(8,128)(2,1)S(1)}, bf16[56,1024]{1,0:T(8,128)(2,1)S(1)}, u32[]{:S(2)}, u32[]{:S(2)}) collective-permute-start(bf16[56,1024]{1,0:T(8,128)(2,1)S(1)} %get-tuple-element.93), channel_id=1, source_target_pairs={{0,4},{4,8},{8,12},{12,16},{16,20},{20,24},{24,28},{28,0},{1,5},{5... | collective-permute-start | bytes 344072 | tf_op jit(solution)/shard_map/ppermute | solution.py:37
  147.0 6.5 %copy-start.10 = (bf16[56,1024]{1,0:T(8,128)(2,1)}, bf16[56,1024]{1,0:T(8,128)(2,1)S(1)}, u32[]{:S(2)}) copy-start(bf16[56,1024]{1,0:T(8,128)(2,1)S(1)} %collective-permute-done.21.refs_2_) | copy-start | bytes 344068
  147.0 6.5 %collective-permute-start.26 = (bf16[56,1024]{1,0:T(8,128)(2,1)S(1)}, bf16[56,1024]{1,0:T(8,128)(2,1)S(1)}, u32[]{:S(2)}, u32[]{:S(2)}) collective-permute-start(bf16[56,1024]{1,0:T(8,128)(2,1)S(1)} %get-tuple-element.94), channel_id=1, source_target_pairs={{0,28},{4,0},{8,4},{12,8},{16,12},{20,16},{24,20},{28,24},{1,29},{... | collective-permute-start | bytes 344072 | tf_op jit(solution)/shard_map/ppermute | solution.py:37
  147.6 6.0 %copy-start.11 = (bf16[56,1024]{1,0:T(8,128)(2,1)}, bf16[56,1024]{1,0:T(8,128)(2,1)S(1)}, u32[]{:S(2)}) copy-start(bf16[56,1024]{1,0:T(8,128)(2,1)S(1)} %collective-permute-done.22.refs_3_) | copy-start | bytes 344068
  148.7 4.9 %copy-start.12 = (bf16[56,1024]{1,0:T(8,128)(2,1)}, bf16[56,1024]{1,0:T(8,128)(2,1)S(1)}, u32[]{:S(2)}) copy-start(bf16[56,1024]{1,0:T(8,128)(2,1)S(1)} %collective-permute-done.23.refs_4_) | copy-start | bytes 344068
  151.3 2.3 %copy-start.13 = (bf16[56,1024]{1,0:T(8,128)(2,1)}, bf16[56,1024]{1,0:T(8,128)(2,1)S(1)}, u32[]{:S(2)}) copy-start(bf16[56,1024]{1,0:T(8,128)(2,1)S(1)} %collective-permute-done.24.refs_5_) | copy-start | bytes 344068
  152.9 0.7 copy-start.14
  153.5 0.7 copy-start.15
  156.3 15.9 %all-to-all-start = ((f32[8,56,128]{2,1,0:T(8,128)}), f32[8,56,128]{2,1,0:T(8,128)S(1)}, u32[]{:S(2)}, u32[]{:S(2)}) async-start(f32[8,56,128]{2,1,0:T(8,128)} %get-tuple-element.95), calls=%async_computation | async-start | bytes 458752 | tf_op jit(solution)/shard_map/all_to_all | solution.py:364
  162.6 10.2 %collective-permute-start.27 = (bf16[8,56,128]{2,1,0:T(8,128)(2,1)}, bf16[8,56,128]{2,1,0:T(8,128)(2,1)S(1)}, u32[]{:S(2)}, u32[]{:S(2)}) collective-permute-start(bf16[8,56,128]{2,1,0:T(8,128)(2,1)} %get-tuple-element.98.refs_0_), channel_id=1, source_target_pairs={{0,32},{32,64},{64,96},{96,0},{1,33},{33,65},{65,97},{97,1},{2,34}... | collective-permute-start | bytes 344072 | tf_op jit(solution)/shard_map/ppermute | solution.py:37
  162.6 10.2 %collective-permute-start.28 = (bf16[8,56,128]{2,1,0:T(8,128)(2,1)}, bf16[8,56,128]{2,1,0:T(8,128)(2,1)S(1)}, u32[]{:S(2)}, u32[]{:S(2)}) collective-permute-start(bf16[8,56,128]{2,1,0:T(8,128)(2,1)} %get-tuple-element.98.refs_0_), channel_id=1, source_target_pairs={{0,64},{32,96},{64,0},{96,32},{1,65},{33,97},{65,1},{97,33},{2,66}... | collective-permute-start | bytes 344072 | tf_op jit(solution)/shard_map/ppermute | solution.py:37
  164.5 8.3 %collective-permute-start.29 = (bf16[8,56,128]{2,1,0:T(8,128)(2,1)}, bf16[8,56,128]{2,1,0:T(8,128)(2,1)S(1)}, u32[]{:S(2)}, u32[]{:S(2)}) collective-permute-start(bf16[8,56,128]{2,1,0:T(8,128)(2,1)} %get-tuple-element.98.refs_0_), channel_id=1, source_target_pairs={{0,96},{32,0},{64,32},{96,64},{1,97},{33,1},{65,33},{97,65},{2,98}... | collective-permute-start | bytes 344072 | tf_op jit(solution)/shard_map/ppermute | solution.py:37
  172.8 0.6 copy-start.16
  172.8 0.7 copy-start.17
  173.5 0.6 copy-start.18
  176.3 16.3 %all-to-all-start.1 = ((bf16[8,56,128]{2,1,0:T(8,128)(2,1)}), bf16[8,56,128]{2,1,0:T(8,128)(2,1)S(1)}, u32[]{:S(2)}, u32[]{:S(2)}) async-start(bf16[8,56,128]{2,1,0:T(8,128)(2,1)} %shard_map.104), calls=%async_computation.1 | async-start | bytes 229376 | tf_op jit(solution)/shard_map/all_to_all | solution.py:381
  181.4 1.3 collective-permute-start.30
  182.6 6.2 %collective-permute-start.31 = (f32[128,128]{1,0:T(8,128)S(1)}, f32[128,128]{1,0:T(8,128)S(1)}, u32[]{:S(2)}, u32[]{:S(2)}) collective-permute-start(f32[128,128]{1,0:T(8,128)S(1)} %add.88.refs_1_), channel_id=1, source_target_pairs={{0,2},{128,130},{2,0},{130,128},{1,3},{129,131},{3,1},{131,129},{4... | collective-permute-start | bytes 196616 | tf_op jit(solution)/shard_map/ppermute | solution.py:33
  185.1 4.6 %collective-permute-start.32 = (f32[128,128]{1,0:T(8,128)S(1)}, f32[128,128]{1,0:T(8,128)S(1)}, u32[]{:S(2)}, u32[]{:S(2)}) collective-permute-start(f32[128,128]{1,0:T(8,128)S(1)} %add.88.refs_1_), channel_id=1, source_target_pairs={{0,128},{128,0},{2,130},{130,2},{1,129},{129,1},{3,131},{131,3},{4... | collective-permute-start | bytes 196616 | tf_op jit(solution)/shard_map/ppermute | solution.py:33
  186.1 4.3 %collective-permute-start.33 = (f32[128,128]{1,0:T(8,128)S(1)}, f32[128,128]{1,0:T(8,128)S(1)}, u32[]{:S(2)}, u32[]{:S(2)}) collective-permute-start(f32[128,128]{1,0:T(8,128)S(1)} %add.88.refs_1_), channel_id=1, source_target_pairs={{0,130},{128,2},{2,128},{130,0},{1,131},{129,3},{3,129},{131,1},{4... | collective-permute-start | bytes 196616 | tf_op jit(solution)/shard_map/ppermute | solution.py:33

commit v3 on v2

v3 whole, which is shorter than its diff:
```python
import math

import jax
import jax.numpy as jnp
import numpy as np
from jax import lax
from jax.experimental import pallas as pl
from jax.experimental.pallas import tpu as pltpu
from jax.sharding import Mesh
from jax.sharding import PartitionSpec as P

DHALF = 1792

coeff_a = 3.4445
coeff_b = -4.775
coeff_c = 2.0315
norm_eps = 1e-06
highest_precision_mode = lax.Precision.HIGHEST

YL, X, Z, YH, C = 2, 4, 8, 2, 2
NAMES = ("yl", "x", "z", "yh", "c")
FIRST = 640


def ring_pairs(flip):
    def index(y):
        return (y % 2) * 2 + y // 2

    return [(index(y), index(y ^ flip)) for y in range(4)]


def over_y(value, flip):
    return lax.ppermute(value, ("yl", "yh"), ring_pairs(flip))


def shift(value, axis, size, step):
    return lax.ppermute(value, axis, [(i, (i + step) % size) for i in range(size)])


def over_xc(value, odd_step, odd_flip, even_step=None, even_flip=0):
    pairs = []
    for x in range(X):
        for c in range(C):
            step, flip = (odd_step, odd_flip) if (x + c) % 2 else (even_step, even_flip)
            if step is not None:
                pairs.append((x * C + c, (x + step) % X * C + (c ^ flip)))
    return lax.ppermute(value, ("x", "c"), pairs)


def pick_kernel(columns, kept_ref, v_ref, out_ref):
    rows, cap = v_ref.shape[0], kept_ref.shape[1]
    column = jnp.broadcast_to(kept_ref[...], (8, cap)).T[:, :1]
    pick = lax.broadcasted_iota(jnp.int32, (cap, rows), 1) == column
    out_ref[...] = jnp.dot(
        pick.astype(jnp.bfloat16), v_ref[:, columns], preferred_element_type=jnp.float32
    ).astype(out_ref.dtype)


def pick_rows(kept, values, start, stop):
    rows = values.shape[0]
    cap = kept.shape[1]
    width = stop - start
    full = pl.BlockSpec(memory_space=pltpu.VMEM)
    return pl.pallas_call(
        lambda *refs: pick_kernel(slice(start, stop), *refs),
        in_specs=[full] * 2,
        out_specs=full,
        out_shape=jax.ShapeDtypeStruct((cap, width), values.dtype),
        compiler_params=pltpu.CompilerParams(vmem_limit_bytes=16 * 2**20),
        cost_estimate=pl.CostEstimate(
            flops=2 * cap * rows * width, bytes_accessed=2 * (rows + cap) * width, transcendentals=0
        ),
    )(kept, values)


def scale_kernel(plan, kept_ref, benefit_ref, present_ref, behaviour_ref, u_ref, out_ref):
    rows, cap = u_ref.shape[2], kept_ref.shape[1]
    pick = (lax.broadcasted_iota(jnp.int32, (rows, cap), 0) == kept_ref[...]).astype(jnp.bfloat16)
    rest = benefit_ref[...] * jnp.exp(present_ref[...] - behaviour_ref[...])
    parts = []
    for _ in range(3):
        part = rest.astype(jnp.bfloat16)
        parts.append(part)
        rest = rest - part.astype(jnp.float32)
    weight = jnp.zeros((1, cap), jnp.float32)
    for part in parts[::-1]:
        stacked = jnp.broadcast_to(part, (16, rows))
        weight = weight + jnp.dot(stacked, pick, preferred_element_type=jnp.float32)[:1]
    live = lax.broadcasted_iota(jnp.int32, (1, cap), 1) < plan[1]
    weight = jnp.where(live, weight, 0.0)
    picked = jnp.dot(u_ref[0], pick, preferred_element_type=jnp.float32)
    out_ref[...] = (weight * picked).astype(out_ref.dtype)


def scaled_half(half, tally, kept, benefit, present, behaviour, adjoint):
    _, q, rows = adjoint.shape
    cap = kept.shape[1]
    row_spec = pl.BlockSpec((1, rows), lambda i, plan: (0, 0))
    return pl.pallas_call(
        scale_kernel,
        grid_spec=pltpu.PrefetchScalarGridSpec(
            num_scalar_prefetch=1,
            grid=(1,),
            in_specs=[
                pl.BlockSpec((1, cap), lambda i, plan: (0, 0)),
                row_spec,
                row_spec,
                row_spec,
                pl.BlockSpec((1, q, rows), lambda i, plan: (plan[0], 0, 0)),
            ],
            out_specs=pl.BlockSpec((q, cap), lambda i, plan: (0, 0)),
        ),
        out_shape=jax.ShapeDtypeStruct((q, cap), jnp.bfloat16),
        compiler_params=pltpu.CompilerParams(vmem_limit_bytes=20 * 2**20),
        cost_estimate=pl.CostEstimate(
            flops=2 * q * rows * cap, bytes_accessed=2 * q * (rows + cap), transcendentals=rows
        ),
    )(jnp.stack([half, tally]).astype(jnp.int32), kept, benefit, present, behaviour, adjoint)


def partial_kernel(counts, plan, *refs):
    s_refs, out_refs = refs[:4], refs[-6:-2]
    s_all, total = refs[-2:]
    q, cap = s_refs[0].shape
    for i, ref in enumerate(s_refs):
        side, other = divmod(i, 2)
        s_all[side * q : (side + 1) * q, other * cap : (other + 1) * cap] = ref[...]

    at = 4
    for chunk in range(2):
        value = None
        for other in range(2):
            count = counts[2 * chunk + other]
            blocks = [ref[...] for ref in refs[at : at + count]]
            at += count
            block = blocks[0] if count == 1 else jnp.concatenate(blocks, axis=0)
            term = jnp.dot(
                s_all[:, other * cap : (other + 1) * cap],
                block,
                preferred_element_type=jnp.float32,
            )
            value = term if value is None else value + term
        value = value.astype(total.dtype)
        for side in range(2):
            total[2 * chunk + side] = value[side * q : (side + 1) * q]
    for slot, out_ref in enumerate(out_refs):
        out_ref[...] = total[plan[slot]]


def partials(plan, s_list, own, e1, opposite, e3, after=()):
    q, cap = s_list[0].shape
    cols = own[0].shape[1]
    groups = (own, e1, opposite, e3)
    counts = tuple(len(group) for group in groups)
    values = [block for group in groups for block in group]
    full = pl.BlockSpec(memory_space=pltpu.VMEM)
    return pl.pallas_call(
        lambda *refs: partial_kernel(counts, *refs),
        in_specs=[pl.BlockSpec(memory_space=pltpu.SMEM)]
        + [full] * (4 + len(values))
        + [pl.BlockSpec(memory_space=pl.ANY)] * len(after),
        out_specs=[full] * 4,
        scratch_shapes=[
            pltpu.VMEM((2 * q, 2 * cap), jnp.bfloat16),
            pltpu.VMEM((4, q, cols), jnp.bfloat16),
        ],
        out_shape=[jax.ShapeDtypeStruct((q, cols), jnp.bfloat16)] * 4,
        compiler_params=pltpu.CompilerParams(vmem_limit_bytes=20 * 2**20),
        cost_estimate=pl.CostEstimate(
            flops=8 * q * 2 * cap * cols, bytes_accessed=8 * 2**20, transcendentals=0
        ),
    )(plan, *s_list, *values, *after)


def rows_kernel(piece_count, plan, *refs):
    ins, outs, mine = refs[: 5 * piece_count], refs[5 * piece_count : -1], refs[-1]
    start = 0
    for piece in range(piece_count):
        *got, last, kept = ins[5 * piece : 5 * piece + 5]
        columns = slice(start, start + kept.shape[1])
        start += kept.shape[1]
        total = got[0][...].astype(jnp.float32)
        for ref in got[1:]:
            total = total + ref[...].astype(jnp.float32)

        @pl.when(plan[0] == 1)
        def _(total=total, last=last, columns=columns):
            mine[:, columns] = total + last[...].astype(jnp.float32)

        @pl.when(plan[0] == 0)
        def _(total=total, kept=kept, columns=columns):
            mine[:, columns] = total + kept[...].astype(jnp.float32)

    for step, out in enumerate(outs):
        heads, rows, head = out.shape
        at = pl.multiple_of(lax.rem(plan[1] + step, Z) * rows, 8)
        for j in range(heads):
            out[j] = mine[pl.ds(at, rows), j * head : (j + 1) * head].astype(out.dtype)


def row_blocks(plan, inputs):
    q = inputs[0].shape[0]
    cols = sum(t.shape[1] for t in inputs[::5])
    shape = (Z, q // Z, cols // Z)
    full = pl.BlockSpec(memory_space=pltpu.VMEM)
    return pl.pallas_call(
        lambda *refs: rows_kernel(len(inputs) // 5, *refs),
        in_specs=[pl.BlockSpec(memory_space=pltpu.SMEM)] + [full] * len(inputs),
        out_specs=[full] * Z,
        out_shape=[jax.ShapeDtypeStruct(shape, jnp.float32)]
        + [jax.ShapeDtypeStruct(shape, jnp.bfloat16)] * (Z - 1),
        scratch_shapes=[pltpu.VMEM((q, cols), jnp.float32)],
        compiler_params=pltpu.CompilerParams(vmem_limit_bytes=16 * 2**20),
    )(plan, *inputs)


def choose_kernel(place, *refs):
    ins, out = refs[:-1], refs[-1]
    for t in range(out.shape[0]):
        for d, ref in enumerate(ins):

            @pl.when(place[t] // Z == d)
            def _(t=t, ref=ref):
                out[t] = ref[lax.rem(place[t], Z)]


def choose(place, rows):
    full = pl.BlockSpec(memory_space=pltpu.VMEM)
    return pl.pallas_call(
        choose_kernel,
        in_specs=[pl.BlockSpec(memory_space=pltpu.SMEM)] + [full] * len(rows),
        out_specs=full,
        out_shape=jax.ShapeDtypeStruct(rows[0].shape, rows[0].dtype),
    )(place, *rows)


def polar_kernel(scale, g_ref, *refs):
    out_ref = refs[-1]
    gram = refs[0][...]
    for ref in refs[1:-1]:
        gram = gram + ref[...]

    def mul(a, b):
        return jnp.dot(a, b, precision=highest_precision_mode, preferred_element_type=jnp.float32)

    n = gram.shape[0]
    eye = (
        lax.broadcasted_iota(jnp.int32, (n, n), 0) == lax.broadcasted_iota(jnp.int32, (n, n), 1)
    ).astype(jnp.float32)
    norm = jnp.sqrt(jnp.sum(gram * eye, keepdims=True)) + norm_eps
    a1 = gram / norm / norm
    p1 = coeff_a * eye + coeff_b * a1 + coeff_c * mul(a1, a1)
    a2 = mul(mul(p1, a1), p1)
    p2 = coeff_a * eye + coeff_b * a2 + coeff_c * mul(a2, a2)
    mix = mul(p2, p1) * (scale / norm)
    out_ref[...] = mul(g_ref[...], mix).astype(out_ref.dtype)


def polar(g, grams):
    q, n = g.shape
    return pl.pallas_call(
        lambda *refs: polar_kernel(0.2 * math.sqrt(2 * DHALF), *refs),
        out_shape=jax.ShapeDtypeStruct((q, n), jnp.bfloat16),
        compiler_params=pltpu.CompilerParams(vmem_limit_bytes=16 * 2**20),
    )(g, *grams)


def on_device(
    mixer_vectors,
    upstream_adjoint,
    relative_benefit,
    present_policy_logit,
    behaviour_policy_logit,
    retained_entries,
    tallies,
    keeper_slot,
):
    bf16, f32 = jnp.bfloat16, jnp.float32
    yl, x, z = lax.axis_index("yl"), lax.axis_index("x"), lax.axis_index("z")
    yh, core = lax.axis_index("yh"), lax.axis_index("c")
    q = upstream_adjoint.shape[2]
    barrier = lax.optimization_barrier

    own = [
        pick_rows(retained_entries, mixer_vectors, start, stop)
        for start, stop in ((0, FIRST), (FIRST, mixer_vectors.shape[1]))
    ]
    adjoint = upstream_adjoint.transpose(1, 2, 0)
    kept, adjoint, *own = barrier((retained_entries, adjoint, *own))
    rows_of = [
        v[None, :] for v in (relative_benefit, present_policy_logit, behaviour_policy_logit)
    ]
    s_send = scaled_half(1 - yl, tallies[0], kept, *rows_of, adjoint)
    s_keep = scaled_half(yl, tallies[0], kept, *rows_of, adjoint)

    odd = (x + core) % 2
    near = jnp.where((x + odd) % X // 2 == yh, 0, 2)
    far = 2 - near
    plan = jnp.where(
        odd == 1,
        jnp.stack([near, far, near + 1, far + 1]),
        jnp.stack([far + 1, near + 1, far, near]),
    ).astype(jnp.int32)

    def over_x(terms):
        return [
            over_xc(terms[0], 1, 0, 2, 1),
            over_xc(terms[1], -1, 0, 0, 1),
            over_xc(terms[2], 1, 1, 2, 0),
            over_xc(terms[3], -1, 1),
            terms[3],
        ]

    e1, e3 = over_y(own[0], 1), over_y(own[0], 3)
    e1, e3, s_send, s_keep, second = barrier((e1, e3, s_send, s_keep, own[1]))
    opposite = over_y(e1, 3)
    s_recv = over_y(s_send, 1)
    c_keep = shift(s_keep, "c", C, 1)
    opposite, s_recv, c_keep, second = barrier((opposite, s_recv, c_keep, second))
    f1, f3 = over_y(second, 1), over_y(second, 3)
    c_recv = shift(s_recv, "c", C, 1)
    s_list = (s_keep, s_recv, c_keep, c_recv)
    first_terms = partials(plan, s_list, [own[0]], [e1], [opposite], [e3])
    first_sums = over_x(first_terms)
    cut = second.shape[0] // 2
    fa, fb = over_y(f3[:cut], 1), over_y(f1[cut:], 3)
    second_terms = partials(plan, s_list, [second], [f1], [fa, fb], [f3], first_sums[:1])
    second_sums = over_x(second_terms)

    head = mixer_vectors.shape[1] // Z
    parts = row_blocks(jnp.stack([odd, z]).astype(jnp.int32), first_sums + second_sums)
    exact = parts[0]
    for got in [shift(parts[d], "z", Z, d) for d in (4, 3, 5, 2, 6, 1, 7)]:
        exact = exact + got.astype(f32)
    rounded = exact.astype(bf16)

    heads_total = keeper_slot.shape[0]
    heads = jnp.arange(heads_total, dtype=jnp.int32)
    wanted = x * Z + jnp.arange(Z, dtype=jnp.int32)
    source = jnp.sum(
        jnp.where(keeper_slot[None, :] == wanted[:, None], heads[None, :], 0), axis=1
    )
    place = ((x - source // Z) % X * Z + source % Z).astype(jnp.int32)
    chosen = choose(place, [rounded] + [shift(rounded, "x", X, d) for d in (1, 2, 3)])
    arrived = lax.all_to_all(chosen, "z", 0, 0, tiled=True).reshape(q, head)

    g = lax.all_to_all(exact, "z", 0, 0, tiled=True).reshape(q, head)
    gram = lax.dot_general(
        g, g, (((0,), (0,)), ((), ())), precision=highest_precision_mode,
        preferred_element_type=f32,
    )
    gram = gram + shift(gram, "c", C, 1)
    update = polar(g, [gram] + [over_y(gram, flip) for flip in (2, 1, 3)])
    gradient = arrived.astype(f32).T
    return (update.T[None], gradient[None])


def solution(mesh):
    wide = Mesh(np.asarray(mesh.devices).reshape(YL, X, Z, YH, C), NAMES)
    dp, mp = ("yl", "x", "z"), ("yh", "c")
    return jax.shard_map(
        on_device,
        mesh=wide,
        in_specs=(
            P(dp, mp),
            P(dp, None, mp),
            P(dp),
            P(dp),
            P(dp),
            P(dp, None),
            P(dp),
            P(),
        ),
        out_specs=(P(dp, None, mp), P(dp, None, mp)),
        check_vma=False,
    )
```

time: 196 us -> 183 us (0.934)
  waiting for transfers between devices: 84.8 us -> 73 us
  other arithmetic: 4.74 us -> 2.53 us
    ppermute x17 -> x13, waiting for transfers between devices: 25 us -> 15.9 us  [shift(): lax.ppermute(value, axis, [(i, (i + step) % size) for i in range(size)])]
    ppermute x6 -> x8, waiting for transfers between devices: 7.57 us -> 15.6 us  [over_xc(): return lax.ppermute(value, ('x', 'c'), pairs)]
    ppermute x11, waiting for transfers between devices: 46.7 us -> 38.7 us  [over_y(): return lax.ppermute(value, ('yl', 'yh'), ring_pairs(flip))]
    ppermute x17 -> x13, starting transfers between devices: 27.4 us -> 20.8 us  [shift(): lax.ppermute(value, axis, [(i, (i + step) % size) for i in range(size)])]
    all_to_all x1, waiting for transfers between devices: 5.52 us -> 0.01 us  [on_device(): g = lax.all_to_all(exact, 'z', 0, 0, tiled=True).reshape(q, head)]
    ppermute x11, starting transfers between devices: 18 us -> 21.6 us  [over_y(): return lax.ppermute(value, ('yl', 'yh'), ring_pairs(flip))]
    all_to_all x1, waiting for transfers between devices: 0.01 us -> 2.77 us  [on_device(): arrived = lax.all_to_all(chosen, 'z', 0, 0, tiled=True).reshape(q, head)]
    pallas_call x6 -> x5, Pallas kernels: 18 us -> 19.7 us  [the longest x2 11.9 us: partials(): pl.pallas_call(lambda *refs: partial_kernel(counts, *refs), in_specs=[pl....]
  transfers between devices with their start and end apart: 36 -> 34, of which waited for: 22 -> 18; matrix products, arithmetic and copies ran while one was open for 2% -> 1% of each run, Pallas kernels for 7% -> 11%
where the time goes in v3:
time: 183 us; the launch traced here: 182 us
  waiting for transfers between devices  73 us (40%)
  starting transfers between devices  66.6 us (36%)
  Pallas kernels  29.7 us (16%)
  local copies, waits for them, and re-layouts  7.6 us (4%)
  other arithmetic  2.53 us (1%)
    ppermute x11, waiting for transfers between devices, over_y(): return lax.ppermute(value, ('yl', 'yh'), ring_pairs(flip))  38.7 us
    ppermute x11, starting transfers between devices, over_y(): return lax.ppermute(value, ('yl', 'yh'), ring_pairs(flip))  21.6 us
    ppermute x13, starting transfers between devices, shift(): lax.ppermute(value, axis, [(i, (i + step) % size) for i in range(size)])  20.8 us
    ppermute x13, waiting for transfers between devices, shift(): lax.ppermute(value, axis, [(i, (i + step) % size) for i in range(size)])  15.9 us
    ppermute x8, waiting for transfers between devices, over_xc(): return lax.ppermute(value, ('x', 'c'), pairs)  15.6 us
    pallas_call x2, Pallas kernels, partials(): pl.pallas_call(lambda *refs: partial_kernel(counts, *refs), in_specs=[pl....  11.9 us
    ppermute x8, starting transfers between devices, over_xc(): return lax.ppermute(value, ('x', 'c'), pairs)  10.6 us
    unnamed x36, local copies, waits for them, and re-layouts  7.52 us
  transfers between devices with their start and end apart: 34, of which 18 were waited for; matrix products, arithmetic and copies ran while one was open for 1% of the time, Pallas kernels for 11%

profile of v3, /device:TPU:8, one launch (start us, length us, event | category | flops | bytes accessed | tf_op | source)
XLA Modules:
  0.0 181.5 jit_solution(14692954678119518562)
XLA Ops:
  0.6 1.9 %copy-done = bf16[1536,1024]{1,0:T(8,128)(2,1)S(1)} copy-done((bf16[1536,1024]{1,0:T(8,128)(2,1)S(1)}, bf16[1536,1024]{1,0:T(8,128)(2,1)}, u32[]{:S(2)}) %copy-start) | copy-done | bytes 3145752
  2.5 0.7 copy-done.1
  3.2 3.3 %shard_map.95.refs_5_ = bf16[768,640]{1,0:T(8,128)(2,1)} custom-call(s32[1,768]{1,0:T(1,128)S(1)} %copy-done.1, bf16[1536,1024]{1,0:T(8,128)(2,1)S(1)} %copy-done), custom_call_target="tpu_custom_call" | custom-call | flops 1509949440 | bytes 2949120 | tf_op jit(solution)/shard_map/pallas_call | solution.py:64
  6.5 1.7 shard_map.96.refs_5_
  8.3 2.3 %collective-permute-start = (bf16[768,640]{1,0:T(8,128)(2,1)}, bf16[768,640]{1,0:T(8,128)(2,1)}, u32[]{:S(2)}, u32[]{:S(2)}) collective-permute-start(bf16[768,640]{1,0:T(8,128)(2,1)} %shard_map.95.refs_5_), channel_id=1, source_target_pairs={{0,128},{128,0},{2,130},{130,2},{1,129},{129,1},{3,131},{131,3},{4... | collective-permute-start | bytes 2949128 | tf_op jit(solution)/shard_map/ppermute | solution.py:33
  10.5 0.7 collective-permute-start.1
  12.0 2.8 %shard_map.97 = bf16[448,768]{1,0:T(8,128)(2,1)S(1)} custom-call(s32[2]{0:T(128)S(1)} %get-tuple-element.62.plan, s32[1,768]{1,0:T(1,128)S(1)} %copy-done.2, f32[1,1536]{1,0:T(1,128)S(1)} %broadcast_in_dim.33.benefit_ref, f32[1,1536]{1,0:T(1,128)S(1)} %broadcast_in_dim.34.present_ref, f32[1,1536]{1,0:T(1,128)S(1)} %broadcast_in_dim.35.behaviour_ref, ...), custom_call_target="tpu_custom_call" | custom-call | flops 1056964608 | bytes 2064384 | tf_op jit(solution)/shard_map/pallas_call | solution.py:99
  14.8 2.8 %shard_map.98.refs_1_ = bf16[448,768]{1,0:T(8,128)(2,1)S(1)} custom-call(s32[2]{0:T(128)S(1)} %get-tuple-element.63.plan, s32[1,768]{1,0:T(1,128)S(1)} %copy-done.2, f32[1,1536]{1,0:T(1,128)S(1)} %broadcast_in_dim.33.benefit_ref, f32[1,1536]{1,0:T(1,128)S(1)} %broadcast_in_dim.34.present_ref, f32[1,1536]{1,0:T(1,128)S(1)} %broadcast_in_dim.35.behaviour_ref, ...), custom_call_target="tpu_custom_call" | custom-call | flops 1056964608 | bytes 2064384 | tf_op jit(solution)/shard_map/pallas_call | solution.py:99
  17.6 14.6 %collective-permute-done.refs_6_ = bf16[768,640]{1,0:T(8,128)(2,1)} collective-permute-done((bf16[768,640]{1,0:T(8,128)(2,1)}, bf16[768,640]{1,0:T(8,128)(2,1)}, u32[]{:S(2)}, u32[]{:S(2)}) %collective-permute-start) | collective-permute-done | bytes 983072 | tf_op jit(solution)/shard_map/ppermute | solution.py:33
  32.1 0.9 collective-permute-done.1.refs_8_
  33.0 1.7 collective-permute-start.2
  34.7 2.6 %collective-permute-start.3 = (bf16[448,768]{1,0:T(8,128)(2,1)S(1)}, bf16[448,768]{1,0:T(8,128)(2,1)S(1)}, u32[]{:S(2)}, u32[]{:S(2)}) collective-permute-start(bf16[448,768]{1,0:T(8,128)(2,1)S(1)} %shard_map.97), channel_id=1, source_target_pairs={{0,128},{128,0},{2,130},{130,2},{1,129},{129,1},{3,131},{131,3},{4... | collective-permute-start | bytes 2064392 | tf_op jit(solution)/shard_map/ppermute | solution.py:33
  37.3 0.9 copy-done.4
  38.2 13.1 %collective-permute-done.3.refs_2_ = bf16[448,768]{1,0:T(8,128)(2,1)S(1)} collective-permute-done((bf16[448,768]{1,0:T(8,128)(2,1)S(1)}, bf16[448,768]{1,0:T(8,128)(2,1)S(1)}, u32[]{:S(2)}, u32[]{:S(2)}) %collective-permute-start.3) | collective-permute-done | bytes 688160 | tf_op jit(solution)/shard_map/ppermute | solution.py:33
  51.3 4.2 %collective-permute-done.2.refs_7_ = bf16[768,640]{1,0:T(8,128)(2,1)S(1)} collective-permute-done((bf16[768,640]{1,0:T(8,128)(2,1)}, bf16[768,640]{1,0:T(8,128)(2,1)S(1)}, u32[]{:S(2)}, u32[]{:S(2)}) %collective-permute-start.2) | collective-permute-done | bytes 983072 | tf_op jit(solution)/shard_map/ppermute | solution.py:33
  55.5 1.7 collective-permute-start.11
  57.3 4.0 %collective-permute-start.10 = (bf16[768,384]{1,0:T(8,128)(2,1)S(1)}, bf16[768,384]{1,0:T(8,128)(2,1)S(1)}, u32[]{:S(2)}, u32[]{:S(2)}) collective-permute-start(bf16[768,384]{1,0:T(8,128)(2,1)S(1)} %shard_map.96.refs_5_), channel_id=1, source_target_pairs={{0,128},{128,0},{2,130},{130,2},{1,129},{129,1},{3,131},{131,3},{4... | collective-permute-start | bytes 1769480 | tf_op jit(solution)/shard_map/ppermute | solution.py:33
  61.3 1.1 copy-done.5
  62.4 6.6 %shard_map.99 = (bf16[448,640]{1,0:T(8,128)(2,1)S(1)}, bf16[448,640]{1,0:T(8,128)(2,1)S(1)}, bf16[448,640]{1,0:T(8,128)(2,1)S(1)}, bf16[448,640]{1,0:T(8,128)(2,1)S(1)}) custom-call(s32[4]{0:T(128)S(1)} %broadcast_select_fusion.refs_0_, bf16[448,768]{1,0:T(8,128)(2,1)S(1)} %copy-done.5, bf16[448,768]{1,0:T(8,128)(2,1)S(1)} %collective-permute-done.3.refs_2_, ...), custom_call_target="tpu_custom_call" | custom-call | flops 3523215360 | bytes 8388608 | tf_op jit(solution)/shard_map/pallas_call | solution.py:157
  69.1 2.7 %collective-permute-start.6 = (bf16[448,640]{1,0:T(8,128)(2,1)S(1)}, bf16[448,640]{1,0:T(8,128)(2,1)S(1)}, u32[]{:S(2)}, u32[]{:S(2)}) collective-permute-start(bf16[448,640]{1,0:T(8,128)(2,1)S(1)} %get-tuple-element.43), channel_id=1, source_target_pairs={{0,65},{1,33},{32,64},{33,96},{64,1},{65,97},{96,0},{97,32},{2,67}... | collective-permute-start | bytes 1720328 | tf_op jit(solution)/shard_map/ppermute | solution.py:47
  71.7 1.3 collective-permute-start.8
  73.1 2.6 %collective-permute-start.12 = (bf16[384,384]{1,0:T(8,128)(2,1)S(1)}, bf16[384,384]{1,0:T(8,128)(2,1)S(1)}, u32[]{:S(2)}, u32[]{:S(2)}) collective-permute-start(bf16[384,384]{1,0:T(8,128)(2,1)S(1)} %slice.8), channel_id=1, source_target_pairs={{0,128},{128,0},{2,130},{130,2},{1,129},{129,1},{3,131},{131,3},{4... | collective-permute-start | bytes 884744 | tf_op jit(solution)/shard_map/ppermute | solution.py:33
  75.7 1.9 %collective-permute-start.13 = (bf16[384,384]{1,0:T(8,128)(2,1)S(1)}, bf16[384,384]{1,0:T(8,128)(2,1)S(1)}, u32[]{:S(2)}, u32[]{:S(2)}) collective-permute-start(bf16[384,384]{1,0:T(8,128)(2,1)S(1)} %slice.9), channel_id=1, source_target_pairs={{0,130},{128,2},{2,128},{130,0},{1,131},{129,3},{3,129},{131,1},{4... | collective-permute-start | bytes 884744 | tf_op jit(solution)/shard_map/ppermute | solution.py:33
  77.6 5.3 %collective-permute-done.12.refs_7_ = bf16[384,384]{1,0:T(8,128)(2,1)S(1)} collective-permute-done((bf16[384,384]{1,0:T(8,128)(2,1)S(1)}, bf16[384,384]{1,0:T(8,128)(2,1)S(1)}, u32[]{:S(2)}, u32[]{:S(2)}) %collective-permute-start.12) | collective-permute-done | bytes 294944 | tf_op jit(solution)/shard_map/ppermute | solution.py:33
  82.9 0.7 collective-permute-start.9
  83.6 0.6 collective-permute-done.13.refs_8_
  84.2 2.0 %collective-permute-done.6.refs_10_.refs_1_ = bf16[448,640]{1,0:T(8,128)(2,1)S(1)} collective-permute-done((bf16[448,640]{1,0:T(8,128)(2,1)S(1)}, bf16[448,640]{1,0:T(8,128)(2,1)S(1)}, u32[]{:S(2)}, u32[]{:S(2)}) %collective-permute-start.6) | collective-permute-done | bytes 573472 | tf_op jit(solution)/shard_map/ppermute | solution.py:47
  86.2 1.1 copy-done.7
  87.3 1.1 copy-done.9
  88.4 5.2 %shard_map.100 = (bf16[448,384]{1,0:T(8,128)(2,1)}, bf16[448,384]{1,0:T(8,128)(2,1)}, bf16[448,384]{1,0:T(8,128)(2,1)}, bf16[448,384]{1,0:T(8,128)(2,1)}) custom-call(s32[4]{0:T(128)S(1)} %broadcast_select_fusion.refs_0_, bf16[448,768]{1,0:T(8,128)(2,1)S(1)} %copy-done.5, bf16[448,768]{1,0:T(8,128)(2,1)S(1)} %copy-done.7, bf16[448,768]{1,0:T(8,128)(2,1)S(1)} %copy-done.9, ...), custom_call_target="tpu_custom_call" | custom-call | flops 2113929216 | bytes 8388608 | tf_op jit(solution)/shard_map/pallas_call | solution.py:157
  93.6 2.4 %collective-permute-start.14 = (bf16[448,384]{1,0:T(8,128)(2,1)}, bf16[448,384]{1,0:T(8,128)(2,1)S(1)}, u32[]{:S(2)}, u32[]{:S(2)}) collective-permute-start(bf16[448,384]{1,0:T(8,128)(2,1)} %get-tuple-element.48), channel_id=1, source_target_pairs={{0,65},{1,33},{32,64},{33,96},{64,1},{65,97},{96,0},{97,32},{2,67}... | collective-permute-start | bytes 1032200 | tf_op jit(solution)/shard_map/ppermute | solution.py:47
  96.0 2.2 %collective-permute-start.16 = (bf16[448,384]{1,0:T(8,128)(2,1)}, bf16[448,384]{1,0:T(8,128)(2,1)}, u32[]{:S(2)}, u32[]{:S(2)}) collective-permute-start(bf16[448,384]{1,0:T(8,128)(2,1)} %get-tuple-element.50), channel_id=1, source_target_pairs={{0,64},{1,32},{32,65},{33,97},{64,0},{65,96},{96,1},{97,33},{2,66}... | collective-permute-start | bytes 1032200 | tf_op jit(solution)/shard_map/ppermute | solution.py:47
  98.2 1.4 collective-permute-start.17
  99.7 5.1 %collective-permute-done.14.refs_6_ = bf16[448,384]{1,0:T(8,128)(2,1)S(1)} collective-permute-done((bf16[448,384]{1,0:T(8,128)(2,1)}, bf16[448,384]{1,0:T(8,128)(2,1)S(1)}, u32[]{:S(2)}, u32[]{:S(2)}) %collective-permute-start.14) | collective-permute-done | bytes 344096 | tf_op jit(solution)/shard_map/ppermute | solution.py:47
  104.9 2.5 %collective-permute-done.15.refs_7_ = bf16[448,384]{1,0:T(8,128)(2,1)} collective-permute-done((bf16[448,384]{1,0:T(8,128)(2,1)}, bf16[448,384]{1,0:T(8,128)(2,1)}, u32[]{:S(2)}, u32[]{:S(2)}) %collective-permute-start.15) | collective-permute-done | bytes 344096 | tf_op jit(solution)/shard_map/ppermute | solution.py:47
  107.3 6.0 %collective-permute-done.16.refs_8_ = bf16[448,384]{1,0:T(8,128)(2,1)} collective-permute-done((bf16[448,384]{1,0:T(8,128)(2,1)}, bf16[448,384]{1,0:T(8,128)(2,1)}, u32[]{:S(2)}, u32[]{:S(2)}) %collective-permute-start.16) | collective-permute-done | bytes 344096 | tf_op jit(solution)/shard_map/ppermute | solution.py:47
  113.3 2.8 %shard_map.101 = (f32[8,56,128]{2,1,0:T(8,128)S(1)}, bf16[8,56,128]{2,1,0:T(8,128)(2,1)S(1)}, bf16[8,56,128]{2,1,0:T(8,128)(2,1)}, bf16[8,56,128]{2,1,0:T(8,128)...) custom-call(s32[2]{0:T(128)S(1)} %pad_add_fusion.refs_0_, ...), custom_call_target="tpu_custom_call" | custom-call | tf_op jit(solution)/shard_map/pallas_call | solution.py:206
  116.1 5.9 %collective-permute-start.24 = (bf16[8,56,128]{2,1,0:T(8,128)(2,1)S(1)}, bf16[8,56,128]{2,1,0:T(8,128)(2,1)S(1)}, u32[]{:S(2)}, u32[]{:S(2)}) collective-permute-start(bf16[8,56,128]{2,1,0:T(8,128)(2,1)S(1)} %get-tuple-element.59), channel_id=1, source_target_pairs={{0,28},{4,0},{8,4},{12,8},{16,12},{20,16},{24,20},{28,24},{1,29},{... | collective-permute-start | bytes 344072 | tf_op jit(solution)/shard_map/ppermute | solution.py:37
  122.0 2.5 %collective-permute-start.22 = (bf16[8,56,128]{2,1,0:T(8,128)(2,1)}, bf16[8,56,128]{2,1,0:T(8,128)(2,1)S(1)}, u32[]{:S(2)}, u32[]{:S(2)}) collective-permute-start(bf16[8,56,128]{2,1,0:T(8,128)(2,1)} %get-tuple-element.57), channel_id=1, source_target_pairs={{0,24},{4,28},{8,0},{12,4},{16,8},{20,12},{24,16},{28,20},{1,25},{... | collective-permute-start | bytes 344072 | tf_op jit(solution)/shard_map/ppermute | solution.py:37
  124.5 0.4 collective-permute-start.21
  124.9 2.9 %collective-permute-start.20 = (bf16[8,56,128]{2,1,0:T(8,128)(2,1)}, bf16[8,56,128]{2,1,0:T(8,128)(2,1)S(1)}, u32[]{:S(2)}, u32[]{:S(2)}) collective-permute-start(bf16[8,56,128]{2,1,0:T(8,128)(2,1)} %get-tuple-element.55), channel_id=1, source_target_pairs={{0,20},{4,24},{8,28},{12,0},{16,4},{20,8},{24,12},{28,16},{1,21},{... | collective-permute-start | bytes 344072 | tf_op jit(solution)/shard_map/ppermute | solution.py:37
  127.9 0.9 collective-permute-start.19
  128.8 3.9 %collective-permute-start.18 = (bf16[8,56,128]{2,1,0:T(8,128)(2,1)}, bf16[8,56,128]{2,1,0:T(8,128)(2,1)S(1)}, u32[]{:S(2)}, u32[]{:S(2)}) collective-permute-start(bf16[8,56,128]{2,1,0:T(8,128)(2,1)} %get-tuple-element.53), channel_id=1, source_target_pairs={{0,16},{4,20},{8,24},{12,28},{16,0},{20,4},{24,8},{28,12},{1,17},{... | collective-permute-start | bytes 344072 | tf_op jit(solution)/shard_map/ppermute | solution.py:37
  132.7 2.8 %collective-permute-done.21 = bf16[8,56,128]{2,1,0:T(8,128)(2,1)S(1)} collective-permute-done((bf16[8,56,128]{2,1,0:T(8,128)(2,1)}, bf16[8,56,128]{2,1,0:T(8,128)(2,1)S(1)}, u32[]{:S(2)}, u32[]{:S(2)}) %collective-permute-start.21) | collective-permute-done | bytes 114720 | tf_op jit(solution)/shard_map/ppermute | solution.py:37
  135.4 6.6 %collective-permute-done.19 = bf16[8,56,128]{2,1,0:T(8,128)(2,1)S(1)} collective-permute-done((bf16[8,56,128]{2,1,0:T(8,128)(2,1)}, bf16[8,56,128]{2,1,0:T(8,128)(2,1)S(1)}, u32[]{:S(2)}, u32[]{:S(2)}) %collective-permute-start.19) | collective-permute-done | bytes 114720 | tf_op jit(solution)/shard_map/ppermute | solution.py:37
  142.0 1.2 collective-permute-done.18
  143.2 0.8 fusion.3
  144.0 6.7 %all-to-all-start = ((f32[8,56,128]{2,1,0:T(8,128)}), f32[8,56,128]{2,1,0:T(8,128)S(1)}, u32[]{:S(2)}, u32[]{:S(2)}) async-start(f32[8,56,128]{2,1,0:T(8,128)} %get-tuple-element.61), calls=%async_computation | async-start | bytes 458752 | tf_op jit(solution)/shard_map/all_to_all | solution.py:347
  150.9 0.8 collective-permute-start.29
  151.6 3.0 %collective-permute-start.30 = (bf16[8,56,128]{2,1,0:T(8,128)(2,1)S(1)}, bf16[8,56,128]{2,1,0:T(8,128)(2,1)S(1)}, u32[]{:S(2)}, u32[]{:S(2)}) collective-permute-start(bf16[8,56,128]{2,1,0:T(8,128)(2,1)S(1)} %get-tuple-element.60.refs_0_), channel_id=1, source_target_pairs={{0,64},{32,96},{64,0},{96,32},{1,65},{33,97},{65,1},{97,33},{2,66}... | collective-permute-start | bytes 344072 | tf_op jit(solution)/shard_map/ppermute | solution.py:37
  155.1 0.6 fusion.place
  155.7 3.5 %collective-permute-done.29.refs_1_ = bf16[8,56,128]{2,1,0:T(8,128)(2,1)S(1)} collective-permute-done((bf16[8,56,128]{2,1,0:T(8,128)(2,1)S(1)}, bf16[8,56,128]{2,1,0:T(8,128)(2,1)S(1)}, u32[]{:S(2)}, u32[]{:S(2)}) %collective-permute-start.29) | collective-permute-done | bytes 114720 | tf_op jit(solution)/shard_map/ppermute | solution.py:37
  159.2 0.6 collective-permute-done.31.refs_3_
  159.9 0.6 copy-done.13
  160.5 2.2 %shard_map.103 = bf16[8,56,128]{2,1,0:T(8,128)(2,1)} custom-call(s32[8]{0:T(128)} %fusion.place, bf16[8,56,128]{2,1,0:T(8,128)(2,1)} %copy-done.10, bf16[8,56,128]{2,1,0:T(8,128)(2,1)} %copy-done.11, bf16[8,56,128]{2,1,0:T(8,128)(2,1)} %copy-done.12, bf16[8,56,128]{2,1,0:T(8,128)(2,1)} %copy-done.13), custom_call_target="tpu_custom_call" | custom-call | tf_op jit(solution)/shard_map/pallas_call | solution.py:229
  162.7 6.9 %all-to-all-start.1 = ((bf16[8,56,128]{2,1,0:T(8,128)(2,1)}), bf16[8,56,128]{2,1,0:T(8,128)(2,1)S(1)}, u32[]{:S(2)}, u32[]{:S(2)}) async-start(bf16[8,56,128]{2,1,0:T(8,128)(2,1)} %shard_map.103), calls=%async_computation.1 | async-start | bytes 229376 | tf_op jit(solution)/shard_map/all_to_all | solution.py:345
  169.6 0.6 convolution_bitcast_fusion
  170.3 1.2 collective-permute-done.25
  171.6 1.4 collective-permute-start.26
  172.9 1.2 collective-permute-start.27
  174.2 1.6 collective-permute-start.28
  175.8 2.8 %all-to-all-done.1 = bf16[8,56,128]{2,1,0:T(8,128)(2,1)S(1)} async-done(((bf16[8,56,128]{2,1,0:T(8,128)(2,1)}), bf16[8,56,128]{2,1,0:T(8,128)(2,1)S(1)}, u32[]{:S(2)}, u32[]{:S(2)}) %all-to-all-start.1) | async-done | bytes 114720 | tf_op jit(solution)/shard_map/all_to_all | solution.py:345
  178.5 0.7 convert_bitcast_fusion
  179.3 2.2 %shard_map.102 = bf16[448,128]{1,0:T(8,128)(2,1)} custom-call(f32[448,128]{1,0:T(8,128)S(1)} %bitcast.24, f32[128,128]{1,0:T(8,128)S(1)} %add.84.refs_1_, f32[128,128]{1,0:T(8,128)S(1)} %collective-permute-done.26.refs_2_, f32[128,128]{1,0:T(8,128)S(1)} %collective-permute-done.27.refs_3_, f32[128,128]{1,0:T(8,128)S(1)} %collective-permute-done.28.refs_4_), custom_call_target="tpu_custom_call" | custom-call | tf_op jit(solution)/shard_map/pallas_call | solution.py:261
  (64 shorter events, 1.3 us)
Async XLA Ops:
  0.6 1.9 %copy-start = (bf16[1536,1024]{1,0:T(8,128)(2,1)S(1)}, bf16[1536,1024]{1,0:T(8,128)(2,1)}, u32[]{:S(2)}) copy-start(bf16[1536,1024]{1,0:T(8,128)(2,1)} %refs_1_.3) | copy-start | bytes 9437188
  2.5 0.7 copy-start.1
  6.5 5.3 %copy-start.14 = (f32[1536]{0:T(1024)S(1)}, f32[1536]{0:T(1024)}, u32[]{:S(2)}) copy-start(f32[1536]{0:T(1024)} %param.10) | copy-start | bytes 18436
  6.5 5.3 %copy-start.15 = (f32[1536]{0:T(1024)S(1)}, f32[1536]{0:T(1024)}, u32[]{:S(2)}) copy-start(f32[1536]{0:T(1024)} %param.11) | copy-start | bytes 18436
  6.5 5.4 %copy-start.16 = (f32[1536]{0:T(1024)S(1)}, f32[1536]{0:T(1024)}, u32[]{:S(2)}) copy-start(f32[1536]{0:T(1024)} %param.12) | copy-start | bytes 18436
  6.5 5.5 %copy-start.2 = (s32[1,768]{1,0:T(1,128)S(1)}, s32[1,768]{1,0:T(1,128)}, u32[]{:S(2)}) copy-start(s32[1,768]{1,0:T(1,128)} %kept_ref.1) | copy-start | bytes 9220
  6.5 5.5 %copy-start.3 = (bf16[1536,2,448]{0,2,1:T(8,128)(2,1)S(1)}, bf16[1536,2,448]{0,2,1:T(8,128)(2,1)}, u32[]{:S(2)}) copy-start(bf16[1536,2,448]{0,2,1:T(8,128)(2,1)} %param.9) | copy-start | bytes 8257540
  8.3 23.9 %collective-permute-start = (bf16[768,640]{1,0:T(8,128)(2,1)}, bf16[768,640]{1,0:T(8,128)(2,1)}, u32[]{:S(2)}, u32[]{:S(2)}) collective-permute-start(bf16[768,640]{1,0:T(8,128)(2,1)} %shard_map.95.refs_5_), channel_id=1, source_target_pairs={{0,128},{128,0},{2,130},{130,2},{1,129},{129,1},{3,131},{131,3},{4... | collective-permute-start | bytes 2949128 | tf_op jit(solution)/shard_map/ppermute | solution.py:33
  10.5 22.5 %collective-permute-start.1 = (bf16[768,640]{1,0:T(8,128)(2,1)}, bf16[768,640]{1,0:T(8,128)(2,1)}, u32[]{:S(2)}, u32[]{:S(2)}) collective-permute-start(bf16[768,640]{1,0:T(8,128)(2,1)} %shard_map.95.refs_5_), channel_id=1, source_target_pairs={{0,130},{128,2},{2,128},{130,0},{1,131},{129,3},{3,129},{131,1},{4... | collective-permute-start | bytes 2949128 | tf_op jit(solution)/shard_map/ppermute | solution.py:33
  33.0 22.5 %collective-permute-start.2 = (bf16[768,640]{1,0:T(8,128)(2,1)}, bf16[768,640]{1,0:T(8,128)(2,1)S(1)}, u32[]{:S(2)}, u32[]{:S(2)}) collective-permute-start(bf16[768,640]{1,0:T(8,128)(2,1)} %collective-permute-done.refs_6_), channel_id=1, source_target_pairs={{0,130},{128,2},{2,128},{130,0},{1,131},{129,3},{3,129},{131,1},{4... | collective-permute-start | bytes 2949128 | tf_op jit(solution)/shard_map/ppermute | solution.py:33
  34.7 16.5 %collective-permute-start.3 = (bf16[448,768]{1,0:T(8,128)(2,1)S(1)}, bf16[448,768]{1,0:T(8,128)(2,1)S(1)}, u32[]{:S(2)}, u32[]{:S(2)}) collective-permute-start(bf16[448,768]{1,0:T(8,128)(2,1)S(1)} %shard_map.97), channel_id=1, source_target_pairs={{0,128},{128,0},{2,130},{130,2},{1,129},{129,1},{3,131},{131,3},{4... | collective-permute-start | bytes 2064392 | tf_op jit(solution)/shard_map/ppermute | solution.py:33
  37.3 14.0 %collective-permute-start.4 = (bf16[448,768]{1,0:T(8,128)(2,1)S(1)}, bf16[448,768]{1,0:T(8,128)(2,1)S(1)}, u32[]{:S(2)}, u32[]{:S(2)}) collective-permute-start(bf16[448,768]{1,0:T(8,128)(2,1)S(1)} %shard_map.98.refs_1_), channel_id=1, source_target_pairs={{0,1},{1,0},{2,3},{3,2},{4,5},{5,4},{6,7},{7,6},{8,9},{9,8},{10,11... | collective-permute-start | bytes 2064392 | tf_op jit(solution)/shard_map/ppermute | solution.py:37
  37.3 0.9 copy-start.4
  51.2 17.8 %copy-start.6 = (bf16[448,768]{1,0:T(8,128)(2,1)}, bf16[448,768]{1,0:T(8,128)(2,1)S(1)}, u32[]{:S(2)}) copy-start(bf16[448,768]{1,0:T(8,128)(2,1)S(1)} %collective-permute-done.3.refs_2_) | copy-start | bytes 2064388
  51.2 17.8 %copy-start.8 = (bf16[448,768]{1,0:T(8,128)(2,1)}, bf16[448,768]{1,0:T(8,128)(2,1)S(1)}, u32[]{:S(2)}) copy-start(bf16[448,768]{1,0:T(8,128)(2,1)S(1)} %collective-permute-done.4.refs_3_) | copy-start | bytes 2064388
  55.5 5.8 %collective-permute-start.5 = (bf16[448,768]{1,0:T(8,128)(2,1)S(1)}, bf16[448,768]{1,0:T(8,128)(2,1)}, u32[]{:S(2)}, u32[]{:S(2)}) collective-permute-start(bf16[448,768]{1,0:T(8,128)(2,1)S(1)} %collective-permute-done.3.refs_2_), channel_id=1, source_target_pairs={{0,1},{1,0},{2,3},{3,2},{4,5},{5,4},{6,7},{7,6},{8,9},{9,8},{10,11... | collective-permute-start | bytes 2064392 | tf_op jit(solution)/shard_map/ppermute | solution.py:37
  55.5 17.5 %collective-permute-start.11 = (bf16[768,384]{1,0:T(8,128)(2,1)S(1)}, bf16[768,384]{1,0:T(8,128)(2,1)S(1)}, u32[]{:S(2)}, u32[]{:S(2)}) collective-permute-start(bf16[768,384]{1,0:T(8,128)(2,1)S(1)} %shard_map.96.refs_5_), channel_id=1, source_target_pairs={{0,130},{128,2},{2,128},{130,0},{1,131},{129,3},{3,129},{131,1},{4... | collective-permute-start | bytes 1769480 | tf_op jit(solution)/shard_map/ppermute | solution.py:33
  57.3 18.3 %collective-permute-start.10 = (bf16[768,384]{1,0:T(8,128)(2,1)S(1)}, bf16[768,384]{1,0:T(8,128)(2,1)S(1)}, u32[]{:S(2)}, u32[]{:S(2)}) collective-permute-start(bf16[768,384]{1,0:T(8,128)(2,1)S(1)} %shard_map.96.refs_5_), channel_id=1, source_target_pairs={{0,128},{128,0},{2,130},{130,2},{1,129},{129,1},{3,131},{131,3},{4... | collective-permute-start | bytes 1769480 | tf_op jit(solution)/shard_map/ppermute | solution.py:33
  61.3 1.1 copy-start.5
  69.1 17.1 %collective-permute-start.6 = (bf16[448,640]{1,0:T(8,128)(2,1)S(1)}, bf16[448,640]{1,0:T(8,128)(2,1)S(1)}, u32[]{:S(2)}, u32[]{:S(2)}) collective-permute-start(bf16[448,640]{1,0:T(8,128)(2,1)S(1)} %get-tuple-element.43), channel_id=1, source_target_pairs={{0,65},{1,33},{32,64},{33,96},{64,1},{65,97},{96,0},{97,32},{2,67}... | collective-permute-start | bytes 1720328 | tf_op jit(solution)/shard_map/ppermute | solution.py:47
  71.7 24.3 %collective-permute-start.7 = (bf16[448,640]{1,0:T(8,128)(2,1)S(1)}, bf16[448,640]{1,0:T(8,128)(2,1)S(1)}, u32[]{:S(2)}, u32[]{:S(2)}) collective-permute-start(bf16[448,640]{1,0:T(8,128)(2,1)S(1)} %get-tuple-element.44), channel_id=1, source_target_pairs={{0,1},{1,97},{32,0},{33,32},{64,65},{65,33},{96,64},{97,96},{2,3},... | collective-permute-start | bytes 1720328 | tf_op jit(solution)/shard_map/ppermute | solution.py:47
  71.7 26.5 %collective-permute-start.8 = (bf16[448,640]{1,0:T(8,128)(2,1)S(1)}, bf16[448,640]{1,0:T(8,128)(2,1)S(1)}, u32[]{:S(2)}, u32[]{:S(2)}) collective-permute-start(bf16[448,640]{1,0:T(8,128)(2,1)S(1)} %get-tuple-element.45), channel_id=1, source_target_pairs={{0,64},{1,32},{32,65},{33,97},{64,0},{65,96},{96,1},{97,33},{2,66}... | collective-permute-start | bytes 1720328 | tf_op jit(solution)/shard_map/ppermute | solution.py:47
  73.1 9.8 %collective-permute-start.12 = (bf16[384,384]{1,0:T(8,128)(2,1)S(1)}, bf16[384,384]{1,0:T(8,128)(2,1)S(1)}, u32[]{:S(2)}, u32[]{:S(2)}) collective-permute-start(bf16[384,384]{1,0:T(8,128)(2,1)S(1)} %slice.8), channel_id=1, source_target_pairs={{0,128},{128,0},{2,130},{130,2},{1,129},{129,1},{3,131},{131,3},{4... | collective-permute-start | bytes 884744 | tf_op jit(solution)/shard_map/ppermute | solution.py:33
  75.7 8.6 %collective-permute-start.13 = (bf16[384,384]{1,0:T(8,128)(2,1)S(1)}, bf16[384,384]{1,0:T(8,128)(2,1)S(1)}, u32[]{:S(2)}, u32[]{:S(2)}) collective-permute-start(bf16[384,384]{1,0:T(8,128)(2,1)S(1)} %slice.9), channel_id=1, source_target_pairs={{0,130},{128,2},{2,128},{130,0},{1,131},{129,3},{3,129},{131,1},{4... | collective-permute-start | bytes 884744 | tf_op jit(solution)/shard_map/ppermute | solution.py:33
  82.9 16.8 %collective-permute-start.9 = (bf16[448,640]{1,0:T(8,128)(2,1)S(1)}, bf16[448,640]{1,0:T(8,128)(2,1)S(1)}, u32[]{:S(2)}, u32[]{:S(2)}) collective-permute-start(bf16[448,640]{1,0:T(8,128)(2,1)S(1)} %get-tuple-element.46.refs_5_), channel_id=1, source_target_pairs={{1,96},{32,1},{65,32},{96,65},{3,98},{34,3},{67,34},{98,67},{5,100... | collective-permute-start | bytes 1720328 | tf_op jit(solution)/shard_map/ppermute | solution.py:47
  86.2 1.1 copy-start.7
  87.3 1.1 copy-start.9
  93.6 11.2 %collective-permute-start.14 = (bf16[448,384]{1,0:T(8,128)(2,1)}, bf16[448,384]{1,0:T(8,128)(2,1)S(1)}, u32[]{:S(2)}, u32[]{:S(2)}) collective-permute-start(bf16[448,384]{1,0:T(8,128)(2,1)} %get-tuple-element.48), channel_id=1, source_target_pairs={{0,65},{1,33},{32,64},{33,96},{64,1},{65,97},{96,0},{97,32},{2,67}... | collective-permute-start | bytes 1032200 | tf_op jit(solution)/shard_map/ppermute | solution.py:47
  96.0 11.3 %collective-permute-start.15 = (bf16[448,384]{1,0:T(8,128)(2,1)}, bf16[448,384]{1,0:T(8,128)(2,1)}, u32[]{:S(2)}, u32[]{:S(2)}) collective-permute-start(bf16[448,384]{1,0:T(8,128)(2,1)} %get-tuple-element.49), channel_id=1, source_target_pairs={{0,1},{1,97},{32,0},{33,32},{64,65},{65,33},{96,64},{97,96},{2,3},... | collective-permute-start | bytes 1032200 | tf_op jit(solution)/shard_map/ppermute | solution.py:47
  96.0 17.3 %collective-permute-start.16 = (bf16[448,384]{1,0:T(8,128)(2,1)}, bf16[448,384]{1,0:T(8,128)(2,1)}, u32[]{:S(2)}, u32[]{:S(2)}) collective-permute-start(bf16[448,384]{1,0:T(8,128)(2,1)} %get-tuple-element.50), channel_id=1, source_target_pairs={{0,64},{1,32},{32,65},{33,97},{64,0},{65,96},{96,1},{97,33},{2,66}... | collective-permute-start | bytes 1032200 | tf_op jit(solution)/shard_map/ppermute | solution.py:47
  98.2 15.1 %collective-permute-start.17 = (bf16[448,384]{1,0:T(8,128)(2,1)}, bf16[448,384]{1,0:T(8,128)(2,1)}, u32[]{:S(2)}, u32[]{:S(2)}) collective-permute-start(bf16[448,384]{1,0:T(8,128)(2,1)} %get-tuple-element.51.refs_10_), channel_id=1, source_target_pairs={{1,96},{32,1},{65,32},{96,65},{3,98},{34,3},{67,34},{98,67},{5,100... | collective-permute-start | bytes 1032200 | tf_op jit(solution)/shard_map/ppermute | solution.py:47
  99.7 51.0 %copy-start.17 = (s32[32]{0:T(128)S(1)}, s32[32]{0:T(128)}, u32[]{:S(2)}) copy-start(s32[32]{0:T(128)} %param.15) | copy-start | bytes 388
  116.1 11.7 %collective-permute-start.24 = (bf16[8,56,128]{2,1,0:T(8,128)(2,1)S(1)}, bf16[8,56,128]{2,1,0:T(8,128)(2,1)S(1)}, u32[]{:S(2)}, u32[]{:S(2)}) collective-permute-start(bf16[8,56,128]{2,1,0:T(8,128)(2,1)S(1)} %get-tuple-element.59), channel_id=1, source_target_pairs={{0,28},{4,0},{8,4},{12,8},{16,12},{20,16},{24,20},{28,24},{1,29},{... | collective-permute-start | bytes 344072 | tf_op jit(solution)/shard_map/ppermute | solution.py:37
  122.0 6.8 %collective-permute-start.23 = (bf16[8,56,128]{2,1,0:T(8,128)(2,1)S(1)}, bf16[8,56,128]{2,1,0:T(8,128)(2,1)S(1)}, u32[]{:S(2)}, u32[]{:S(2)}) collective-permute-start(bf16[8,56,128]{2,1,0:T(8,128)(2,1)S(1)} %get-tuple-element.58), channel_id=1, source_target_pairs={{0,4},{4,8},{8,12},{12,16},{16,20},{20,24},{24,28},{28,0},{1,5},{5... | collective-permute-start | bytes 344072 | tf_op jit(solution)/shard_map/ppermute | solution.py:37
  122.0 10.6 %collective-permute-start.22 = (bf16[8,56,128]{2,1,0:T(8,128)(2,1)}, bf16[8,56,128]{2,1,0:T(8,128)(2,1)S(1)}, u32[]{:S(2)}, u32[]{:S(2)}) collective-permute-start(bf16[8,56,128]{2,1,0:T(8,128)(2,1)} %get-tuple-element.57), channel_id=1, source_target_pairs={{0,24},{4,28},{8,0},{12,4},{16,8},{20,12},{24,16},{28,20},{1,25},{... | collective-permute-start | bytes 344072 | tf_op jit(solution)/shard_map/ppermute | solution.py:37
  124.5 10.9 %collective-permute-start.21 = (bf16[8,56,128]{2,1,0:T(8,128)(2,1)}, bf16[8,56,128]{2,1,0:T(8,128)(2,1)S(1)}, u32[]{:S(2)}, u32[]{:S(2)}) collective-permute-start(bf16[8,56,128]{2,1,0:T(8,128)(2,1)} %get-tuple-element.56), channel_id=1, source_target_pairs={{0,8},{4,12},{8,16},{12,20},{16,24},{20,28},{24,0},{28,4},{1,9},{5... | collective-permute-start | bytes 344072 | tf_op jit(solution)/shard_map/ppermute | solution.py:37
  124.9 10.5 %collective-permute-start.20 = (bf16[8,56,128]{2,1,0:T(8,128)(2,1)}, bf16[8,56,128]{2,1,0:T(8,128)(2,1)S(1)}, u32[]{:S(2)}, u32[]{:S(2)}) collective-permute-start(bf16[8,56,128]{2,1,0:T(8,128)(2,1)} %get-tuple-element.55), channel_id=1, source_target_pairs={{0,20},{4,24},{8,28},{12,0},{16,4},{20,8},{24,12},{28,16},{1,21},{... | collective-permute-start | bytes 344072 | tf_op jit(solution)/shard_map/ppermute | solution.py:37
  127.9 14.2 %collective-permute-start.19 = (bf16[8,56,128]{2,1,0:T(8,128)(2,1)}, bf16[8,56,128]{2,1,0:T(8,128)(2,1)S(1)}, u32[]{:S(2)}, u32[]{:S(2)}) collective-permute-start(bf16[8,56,128]{2,1,0:T(8,128)(2,1)} %get-tuple-element.54), channel_id=1, source_target_pairs={{0,12},{4,16},{8,20},{12,24},{16,28},{20,0},{24,4},{28,8},{1,13},{... | collective-permute-start | bytes 344072 | tf_op jit(solution)/shard_map/ppermute | solution.py:37
  128.8 14.4 %collective-permute-start.18 = (bf16[8,56,128]{2,1,0:T(8,128)(2,1)}, bf16[8,56,128]{2,1,0:T(8,128)(2,1)S(1)}, u32[]{:S(2)}, u32[]{:S(2)}) collective-permute-start(bf16[8,56,128]{2,1,0:T(8,128)(2,1)} %get-tuple-element.53), channel_id=1, source_target_pairs={{0,16},{4,20},{8,24},{12,28},{16,0},{20,4},{24,8},{28,12},{1,17},{... | collective-permute-start | bytes 344072 | tf_op jit(solution)/shard_map/ppermute | solution.py:37
  144.0 15.7 %copy-start.10 = (bf16[8,56,128]{2,1,0:T(8,128)(2,1)}, bf16[8,56,128]{2,1,0:T(8,128)(2,1)S(1)}, u32[]{:S(2)}) copy-start(bf16[8,56,128]{2,1,0:T(8,128)(2,1)S(1)} %get-tuple-element.60.refs_0_) | copy-start | bytes 344068
  144.0 18.7 %all-to-all-start = ((f32[8,56,128]{2,1,0:T(8,128)}), f32[8,56,128]{2,1,0:T(8,128)S(1)}, u32[]{:S(2)}, u32[]{:S(2)}) async-start(f32[8,56,128]{2,1,0:T(8,128)} %get-tuple-element.61), calls=%async_computation | async-start | bytes 458752 | tf_op jit(solution)/shard_map/all_to_all | solution.py:347
  150.9 8.3 %collective-permute-start.29 = (bf16[8,56,128]{2,1,0:T(8,128)(2,1)S(1)}, bf16[8,56,128]{2,1,0:T(8,128)(2,1)S(1)}, u32[]{:S(2)}, u32[]{:S(2)}) collective-permute-start(bf16[8,56,128]{2,1,0:T(8,128)(2,1)S(1)} %get-tuple-element.60.refs_0_), channel_id=1, source_target_pairs={{0,32},{32,64},{64,96},{96,0},{1,33},{33,65},{65,97},{97,1},{2,34}... | collective-permute-start | bytes 344072 | tf_op jit(solution)/shard_map/ppermute | solution.py:37
  151.6 7.5 %collective-permute-start.30 = (bf16[8,56,128]{2,1,0:T(8,128)(2,1)S(1)}, bf16[8,56,128]{2,1,0:T(8,128)(2,1)S(1)}, u32[]{:S(2)}, u32[]{:S(2)}) collective-permute-start(bf16[8,56,128]{2,1,0:T(8,128)(2,1)S(1)} %get-tuple-element.60.refs_0_), channel_id=1, source_target_pairs={{0,64},{32,96},{64,0},{96,32},{1,65},{33,97},{65,1},{97,33},{2,66}... | collective-permute-start | bytes 344072 | tf_op jit(solution)/shard_map/ppermute | solution.py:37
  154.7 5.1 %collective-permute-start.31 = (bf16[8,56,128]{2,1,0:T(8,128)(2,1)S(1)}, bf16[8,56,128]{2,1,0:T(8,128)(2,1)S(1)}, u32[]{:S(2)}, u32[]{:S(2)}) collective-permute-start(bf16[8,56,128]{2,1,0:T(8,128)(2,1)S(1)} %get-tuple-element.60.refs_0_), channel_id=1, source_target_pairs={{0,96},{32,0},{64,32},{96,64},{1,97},{33,1},{65,33},{97,65},{2,98}... | collective-permute-start | bytes 344072 | tf_op jit(solution)/shard_map/ppermute | solution.py:37
  159.2 0.7 copy-start.11
  159.2 0.7 copy-start.12
  159.8 0.6 copy-start.13
  162.7 15.8 %all-to-all-start.1 = ((bf16[8,56,128]{2,1,0:T(8,128)(2,1)}), bf16[8,56,128]{2,1,0:T(8,128)(2,1)S(1)}, u32[]{:S(2)}, u32[]{:S(2)}) async-start(bf16[8,56,128]{2,1,0:T(8,128)(2,1)} %shard_map.103), calls=%async_computation.1 | async-start | bytes 229376 | tf_op jit(solution)/shard_map/all_to_all | solution.py:345
  170.2 1.3 collective-permute-start.25
  171.6 7.7 %collective-permute-start.26 = (f32[128,128]{1,0:T(8,128)S(1)}, f32[128,128]{1,0:T(8,128)S(1)}, u32[]{:S(2)}, u32[]{:S(2)}) collective-permute-start(f32[128,128]{1,0:T(8,128)S(1)} %add.84.refs_1_), channel_id=1, source_target_pairs={{0,2},{128,130},{2,0},{130,128},{1,3},{129,131},{3,1},{131,129},{4... | collective-permute-start | bytes 196616 | tf_op jit(solution)/shard_map/ppermute | solution.py:33
  172.9 6.3 %collective-permute-start.27 = (f32[128,128]{1,0:T(8,128)S(1)}, f32[128,128]{1,0:T(8,128)S(1)}, u32[]{:S(2)}, u32[]{:S(2)}) collective-permute-start(f32[128,128]{1,0:T(8,128)S(1)} %add.84.refs_1_), channel_id=1, source_target_pairs={{0,128},{128,0},{2,130},{130,2},{1,129},{129,1},{3,131},{131,3},{4... | collective-permute-start | bytes 196616 | tf_op jit(solution)/shard_map/ppermute | solution.py:33
  174.2 5.1 %collective-permute-start.28 = (f32[128,128]{1,0:T(8,128)S(1)}, f32[128,128]{1,0:T(8,128)S(1)}, u32[]{:S(2)}, u32[]{:S(2)}) collective-permute-start(f32[128,128]{1,0:T(8,128)S(1)} %add.84.refs_1_), channel_id=1, source_target_pairs={{0,130},{128,2},{2,128},{130,0},{1,131},{129,3},{3,129},{131,1},{4... | collective-permute-start | bytes 196616 | tf_op jit(solution)/shard_map/ppermute | solution.py:33

commit v4 on v3

--- a/solution.py
+++ b/solution.py
@@ -119,14 +119,19 @@
 
 
 def partial_kernel(counts, plan, *refs):
-    s_refs, out_refs = refs[:4], refs[-6:-2]
-    s_all, total = refs[-2:]
-    q, cap = s_refs[0].shape
-    for i, ref in enumerate(s_refs):
-        side, other = divmod(i, 2)
-        s_all[side * q : (side + 1) * q, other * cap : (other + 1) * cap] = ref[...]
-
-    at = 4
+    total, refs = refs[-1], refs[:-1]
+    if len(counts) == 5:
+        s_refs, out_refs, s_all = refs[:4], refs[-5:-1], refs[-1]
+        q, cap = s_refs[0].shape
+        for i, ref in enumerate(s_refs):
+            side, other = divmod(i, 2)
+            s_all[side * q : (side + 1) * q, other * cap : (other + 1) * cap] = ref[...]
+        at = 4
+    else:
+        out_refs, s_all = refs[-4:], refs[0]
+        q, cap = s_all.shape[0] // 2, s_all.shape[1] // 2
+        at = 1
+
     for chunk in range(2):
         value = None
         for other in range(2):
@@ -148,23 +153,27 @@
 
 
 def partials(plan, s_list, own, e1, opposite, e3, after=()):
-    q, cap = s_list[0].shape
+    if len(s_list) == 4:
+        q, cap = s_list[0].shape
+    else:
+        q, cap = s_list[0].shape[0] // 2, s_list[0].shape[1] // 2
     cols = own[0].shape[1]
     groups = (own, e1, opposite, e3)
     counts = tuple(len(group) for group in groups)
     values = [block for group in groups for block in group]
     full = pl.BlockSpec(memory_space=pltpu.VMEM)
+    shapes = [jax.ShapeDtypeStruct((q, cols), jnp.bfloat16)] * 4
+    if len(s_list) == 4:
+        shapes.append(jax.ShapeDtypeStruct((2 * q, 2 * cap), jnp.bfloat16))
+        counts += (1,)
     return pl.pallas_call(
         lambda *refs: partial_kernel(counts, *refs),
         in_specs=[pl.BlockSpec(memory_space=pltpu.SMEM)]
-        + [full] * (4 + len(values))
+        + [full] * (len(s_list) + len(values))
         + [pl.BlockSpec(memory_space=pl.ANY)] * len(after),
-        out_specs=[full] * 4,
-        scratch_shapes=[
-            pltpu.VMEM((2 * q, 2 * cap), jnp.bfloat16),
-            pltpu.VMEM((4, q, cols), jnp.bfloat16),
-        ],
-        out_shape=[jax.ShapeDtypeStruct((q, cols), jnp.bfloat16)] * 4,
+        out_specs=[full] * len(shapes),
+        scratch_shapes=[pltpu.VMEM((4, q, cols), jnp.bfloat16)],
+        out_shape=shapes,
         compiler_params=pltpu.CompilerParams(vmem_limit_bytes=20 * 2**20),
         cost_estimate=pl.CostEstimate(
             flops=8 * q * 2 * cap * cols, bytes_accessed=8 * 2**20, transcendentals=0
@@ -286,7 +295,7 @@
         for start, stop in ((0, FIRST), (FIRST, mixer_vectors.shape[1]))
     ]
     adjoint = upstream_adjoint.transpose(1, 2, 0)
-    kept, adjoint, *own = barrier((retained_entries, adjoint, *own))
+    kept, adjoint, own[0] = barrier((retained_entries, adjoint, own[0]))
     rows_of = [
         v[None, :] for v in (relative_benefit, present_policy_logit, behaviour_policy_logit)
     ]
@@ -312,19 +321,19 @@
         ]
 
     e1, e3 = over_y(own[0], 1), over_y(own[0], 3)
-    e1, e3, s_send, s_keep, second = barrier((e1, e3, s_send, s_keep, own[1]))
+    e1, e3, s_send, s_keep = barrier((e1, e3, s_send, s_keep))
     opposite = over_y(e1, 3)
     s_recv = over_y(s_send, 1)
     c_keep = shift(s_keep, "c", C, 1)
-    opposite, s_recv, c_keep, second = barrier((opposite, s_recv, c_keep, second))
+    opposite, s_recv, c_keep, second = barrier((opposite, s_recv, c_keep, own[1]))
     f1, f3 = over_y(second, 1), over_y(second, 3)
     c_recv = shift(s_recv, "c", C, 1)
     s_list = (s_keep, s_recv, c_keep, c_recv)
-    first_terms = partials(plan, s_list, [own[0]], [e1], [opposite], [e3])
+    *first_terms, s_all = partials(plan, s_list, [own[0]], [e1], [opposite], [e3])
     first_sums = over_x(first_terms)
     cut = second.shape[0] // 2
     fa, fb = over_y(f3[:cut], 1), over_y(f1[cut:], 3)
-    second_terms = partials(plan, s_list, [second], [f1], [fa, fb], [f3], first_sums[:1])
+    second_terms = partials(plan, [s_all], [second], [f1], [fa, fb], [f3], first_sums[:1])
     second_sums = over_x(second_terms)
 
     head = mixer_vectors.shape[1] // Z

time: 183 us -> 181 us (0.989)
  local copies, waits for them, and re-layouts: 7.6 us -> 4.53 us
  waiting for transfers between devices: 73 us -> 75.5 us
    unnamed x36 -> x30, local copies, waits for them, and re-layouts: 7.52 us -> 4.45 us
    ppermute x8, waiting for transfers between devices: 15.6 us -> 18.3 us  [over_xc(): return lax.ppermute(value, ('x', 'c'), pairs)]
  transfers between devices with their start and end apart: 34 -> 34, of which waited for: 18 -> 18; matrix products, arithmetic and copies ran while one was open for 1% -> 1% of each run, Pallas kernels for 11% -> 12%
where the time goes in v4:
time: 181 us; the launch traced here: 180 us
  waiting for transfers between devices  75.5 us (42%)
  starting transfers between devices  65.8 us (36%)
  Pallas kernels  29.4 us (16%)
  local copies, waits for them, and re-layouts  4.53 us (3%)
  other arithmetic  2.53 us (1%)
    ppermute x11, waiting for transfers between devices, over_y(): return lax.ppermute(value, ('yl', 'yh'), ring_pairs(flip))  37.9 us
    ppermute x11, starting transfers between devices, over_y(): return lax.ppermute(value, ('yl', 'yh'), ring_pairs(flip))  21.5 us
    ppermute x13, starting transfers between devices, shift(): lax.ppermute(value, axis, [(i, (i + step) % size) for i in range(size)])  21.1 us
    ppermute x8, waiting for transfers between devices, over_xc(): return lax.ppermute(value, ('x', 'c'), pairs)  18.3 us
    ppermute x13, waiting for transfers between devices, shift(): lax.ppermute(value, axis, [(i, (i + step) % size) for i in range(size)])  16.6 us
    pallas_call x2, Pallas kernels, partials(): pl.pallas_call(lambda *refs: partial_kernel(counts, *refs), in_specs=[pl....  11.3 us
    ppermute x8, starting transfers between devices, over_xc(): return lax.ppermute(value, ('x', 'c'), pairs)  10.5 us
    all_to_all x1, starting transfers between devices, on_device(): arrived = lax.all_to_all(chosen, 'z', 0, 0, tiled=True).reshape(q, head)  6.95 us
  transfers between devices with their start and end apart: 34, of which 18 were waited for; matrix products, arithmetic and copies ran while one was open for 1% of the time, Pallas kernels for 12%

profile of v4, /device:TPU:8, one launch (start us, length us, event | category | flops | bytes accessed | tf_op | source)
XLA Modules:
  0.0 179.9 jit_solution(15724761684746263991)
XLA Ops:
  0.6 1.9 %copy-done = bf16[1536,1024]{1,0:T(8,128)(2,1)S(1)} copy-done((bf16[1536,1024]{1,0:T(8,128)(2,1)S(1)}, bf16[1536,1024]{1,0:T(8,128)(2,1)}, u32[]{:S(2)}) %copy-start) | copy-done | bytes 3145752
  2.5 0.7 copy-done.2
  3.2 3.3 %shard_map.95.refs_5_ = bf16[768,640]{1,0:T(8,128)(2,1)} custom-call(s32[1,768]{1,0:T(1,128)S(1)} %copy-done.2, bf16[1536,1024]{1,0:T(8,128)(2,1)S(1)} %copy-done), custom_call_target="tpu_custom_call" | custom-call | flops 1509949440 | bytes 2949120 | tf_op jit(solution)/shard_map/pallas_call | solution.py:64
  6.5 2.2 %collective-permute-start = (bf16[768,640]{1,0:T(8,128)(2,1)}, bf16[768,640]{1,0:T(8,128)(2,1)}, u32[]{:S(2)}, u32[]{:S(2)}) collective-permute-start(bf16[768,640]{1,0:T(8,128)(2,1)} %shard_map.95.refs_5_), channel_id=1, source_target_pairs={{0,128},{128,0},{2,130},{130,2},{1,129},{129,1},{3,131},{131,3},{4... | collective-permute-start | bytes 2949128 | tf_op jit(solution)/shard_map/ppermute | solution.py:33
  8.7 0.7 collective-permute-start.1
  10.2 2.8 %shard_map.96 = bf16[448,768]{1,0:T(8,128)(2,1)S(1)} custom-call(s32[2]{0:T(128)S(1)} %get-tuple-element.60.plan, s32[1,768]{1,0:T(1,128)S(1)} %copy-done.3, f32[1,1536]{1,0:T(1,128)S(1)} %broadcast_in_dim.33.benefit_ref, f32[1,1536]{1,0:T(1,128)S(1)} %broadcast_in_dim.34.present_ref, f32[1,1536]{1,0:T(1,128)S(1)} %broadcast_in_dim.35.behaviour_ref, ...), custom_call_target="tpu_custom_call" | custom-call | flops 1056964608 | bytes 2064384 | tf_op jit(solution)/shard_map/pallas_call | solution.py:99
  13.0 2.8 %shard_map.97.refs_1_ = bf16[448,768]{1,0:T(8,128)(2,1)S(1)} custom-call(s32[2]{0:T(128)S(1)} %get-tuple-element.61.plan, s32[1,768]{1,0:T(1,128)S(1)} %copy-done.3, f32[1,1536]{1,0:T(1,128)S(1)} %broadcast_in_dim.33.benefit_ref, f32[1,1536]{1,0:T(1,128)S(1)} %broadcast_in_dim.34.present_ref, f32[1,1536]{1,0:T(1,128)S(1)} %broadcast_in_dim.35.behaviour_ref, ...), custom_call_target="tpu_custom_call" | custom-call | flops 1056964608 | bytes 2064384 | tf_op jit(solution)/shard_map/pallas_call | solution.py:99
  15.8 14.6 %collective-permute-done.refs_6_ = bf16[768,640]{1,0:T(8,128)(2,1)} collective-permute-done((bf16[768,640]{1,0:T(8,128)(2,1)}, bf16[768,640]{1,0:T(8,128)(2,1)}, u32[]{:S(2)}, u32[]{:S(2)}) %collective-permute-start) | collective-permute-done | bytes 983072 | tf_op jit(solution)/shard_map/ppermute | solution.py:33
  30.4 0.9 collective-permute-done.1.refs_8_
  31.2 1.7 collective-permute-start.2
  32.9 2.6 %collective-permute-start.3 = (bf16[448,768]{1,0:T(8,128)(2,1)S(1)}, bf16[448,768]{1,0:T(8,128)(2,1)S(1)}, u32[]{:S(2)}, u32[]{:S(2)}) collective-permute-start(bf16[448,768]{1,0:T(8,128)(2,1)S(1)} %shard_map.96), channel_id=1, source_target_pairs={{0,128},{128,0},{2,130},{130,2},{1,129},{129,1},{3,131},{131,3},{4... | collective-permute-start | bytes 2064392 | tf_op jit(solution)/shard_map/ppermute | solution.py:33
  35.5 1.7 shard_map.98.refs_2_
  37.2 12.2 %collective-permute-done.3.refs_2_ = bf16[448,768]{1,0:T(8,128)(2,1)S(1)} collective-permute-done((bf16[448,768]{1,0:T(8,128)(2,1)S(1)}, bf16[448,768]{1,0:T(8,128)(2,1)S(1)}, u32[]{:S(2)}, u32[]{:S(2)}) %collective-permute-start.3) | collective-permute-done | bytes 688160 | tf_op jit(solution)/shard_map/ppermute | solution.py:33
  49.5 4.2 %collective-permute-done.2.refs_7_ = bf16[768,640]{1,0:T(8,128)(2,1)S(1)} collective-permute-done((bf16[768,640]{1,0:T(8,128)(2,1)}, bf16[768,640]{1,0:T(8,128)(2,1)S(1)}, u32[]{:S(2)}, u32[]{:S(2)}) %collective-permute-start.2) | collective-permute-done | bytes 983072 | tf_op jit(solution)/shard_map/ppermute | solution.py:33
  53.7 1.7 collective-permute-start.11
  55.5 4.0 %collective-permute-start.10 = (bf16[768,384]{1,0:T(8,128)(2,1)S(1)}, bf16[768,384]{1,0:T(8,128)(2,1)S(1)}, u32[]{:S(2)}, u32[]{:S(2)}) collective-permute-start(bf16[768,384]{1,0:T(8,128)(2,1)S(1)} %shard_map.98.refs_2_), channel_id=1, source_target_pairs={{0,128},{128,0},{2,130},{130,2},{1,129},{129,1},{3,131},{131,3},{4... | collective-permute-start | bytes 1769480 | tf_op jit(solution)/shard_map/ppermute | solution.py:33
  59.5 1.1 copy-done.6
  60.6 6.7 %shard_map.99 = (bf16[448,640]{1,0:T(8,128)(2,1)S(1)}, bf16[448,640]{1,0:T(8,128)(2,1)S(1)}, bf16[448,640]{1,0:T(8,128)(2,1)S(1)}, bf16[448,640]{1,0:T(8,128)(2,1)S(1)}, bf16[896,1536]{1,0:T(8,128)(2,1)S(1)}) custom-call(s32[4]{0:T(128)S(1)} %broadcast_select_fusion.refs_0_, bf16[448,768]{1,0:T(8,128)(2,1)S(1)} %copy-done.6, ...), custom_call_target="tpu_custom_call" | custom-call | flops 3523215360 | bytes 8388608 | tf_op jit(solution)/shard_map/pallas_call | solution.py:169
  67.3 2.7 %collective-permute-start.6 = (bf16[448,640]{1,0:T(8,128)(2,1)S(1)}, bf16[448,640]{1,0:T(8,128)(2,1)S(1)}, u32[]{:S(2)}, u32[]{:S(2)}) collective-permute-start(bf16[448,640]{1,0:T(8,128)(2,1)S(1)} %get-tuple-element.40), channel_id=1, source_target_pairs={{0,65},{1,33},{32,64},{33,96},{64,1},{65,97},{96,0},{97,32},{2,67}... | collective-permute-start | bytes 1720328 | tf_op jit(solution)/shard_map/ppermute | solution.py:47
  70.0 1.3 collective-permute-start.8
  71.3 2.6 %collective-permute-start.12 = (bf16[384,384]{1,0:T(8,128)(2,1)S(1)}, bf16[384,384]{1,0:T(8,128)(2,1)S(1)}, u32[]{:S(2)}, u32[]{:S(2)}) collective-permute-start(bf16[384,384]{1,0:T(8,128)(2,1)S(1)} %slice.8), channel_id=1, source_target_pairs={{0,128},{128,0},{2,130},{130,2},{1,129},{129,1},{3,131},{131,3},{4... | collective-permute-start | bytes 884744 | tf_op jit(solution)/shard_map/ppermute | solution.py:33
  74.0 1.8 %collective-permute-start.13 = (bf16[384,384]{1,0:T(8,128)(2,1)S(1)}, bf16[384,384]{1,0:T(8,128)(2,1)S(1)}, u32[]{:S(2)}, u32[]{:S(2)}) collective-permute-start(bf16[384,384]{1,0:T(8,128)(2,1)S(1)} %slice.9), channel_id=1, source_target_pairs={{0,130},{128,2},{2,128},{130,0},{1,131},{129,3},{3,129},{131,1},{4... | collective-permute-start | bytes 884744 | tf_op jit(solution)/shard_map/ppermute | solution.py:33
  75.8 5.3 %collective-permute-done.12.refs_4_ = bf16[384,384]{1,0:T(8,128)(2,1)S(1)} collective-permute-done((bf16[384,384]{1,0:T(8,128)(2,1)S(1)}, bf16[384,384]{1,0:T(8,128)(2,1)S(1)}, u32[]{:S(2)}, u32[]{:S(2)}) %collective-permute-start.12) | collective-permute-done | bytes 294944 | tf_op jit(solution)/shard_map/ppermute | solution.py:33
  81.2 0.7 collective-permute-start.9
  81.9 0.6 collective-permute-done.13.refs_5_
  82.4 2.0 %collective-permute-done.6.refs_7_.refs_1_ = bf16[448,640]{1,0:T(8,128)(2,1)S(1)} collective-permute-done((bf16[448,640]{1,0:T(8,128)(2,1)S(1)}, bf16[448,640]{1,0:T(8,128)(2,1)S(1)}, u32[]{:S(2)}, u32[]{:S(2)}) %collective-permute-start.6) | collective-permute-done | bytes 573472 | tf_op jit(solution)/shard_map/ppermute | solution.py:47
  84.4 4.7 %shard_map.100 = (bf16[448,384]{1,0:T(8,128)(2,1)}, bf16[448,384]{1,0:T(8,128)(2,1)}, bf16[448,384]{1,0:T(8,128)(2,1)}, bf16[448,384]{1,0:T(8,128)(2,1)}) custom-call(s32[4]{0:T(128)S(1)} %broadcast_select_fusion.refs_0_, bf16[896,1536]{1,0:T(8,128)(2,1)S(1)} %get-tuple-element.44.refs_1_, bf16[768,384]{1,0:T(8,128)(2,1)S(1)} %shard_map.98.refs_2_, ...), custom_call_target="tpu_custom_call" | custom-call | flops 2113929216 | bytes 8388608 | tf_op jit(solution)/shard_map/pallas_call | solution.py:169
  89.1 2.4 %collective-permute-start.14 = (bf16[448,384]{1,0:T(8,128)(2,1)}, bf16[448,384]{1,0:T(8,128)(2,1)S(1)}, u32[]{:S(2)}, u32[]{:S(2)}) collective-permute-start(bf16[448,384]{1,0:T(8,128)(2,1)} %get-tuple-element.46), channel_id=1, source_target_pairs={{0,65},{1,33},{32,64},{33,96},{64,1},{65,97},{96,0},{97,32},{2,67}... | collective-permute-start | bytes 1032200 | tf_op jit(solution)/shard_map/ppermute | solution.py:47
  91.5 2.1 %collective-permute-start.16 = (bf16[448,384]{1,0:T(8,128)(2,1)}, bf16[448,384]{1,0:T(8,128)(2,1)}, u32[]{:S(2)}, u32[]{:S(2)}) collective-permute-start(bf16[448,384]{1,0:T(8,128)(2,1)} %get-tuple-element.48), channel_id=1, source_target_pairs={{0,64},{1,32},{32,65},{33,97},{64,0},{65,96},{96,1},{97,33},{2,66}... | collective-permute-start | bytes 1032200 | tf_op jit(solution)/shard_map/ppermute | solution.py:47
  93.6 2.9 %collective-permute-done.8.refs_3_ = bf16[448,640]{1,0:T(8,128)(2,1)S(1)} collective-permute-done((bf16[448,640]{1,0:T(8,128)(2,1)S(1)}, bf16[448,640]{1,0:T(8,128)(2,1)S(1)}, u32[]{:S(2)}, u32[]{:S(2)}) %collective-permute-start.8) | collective-permute-done | bytes 573472 | tf_op jit(solution)/shard_map/ppermute | solution.py:47
  96.5 1.4 collective-permute-start.17
  98.0 6.1 %collective-permute-done.14.refs_6_ = bf16[448,384]{1,0:T(8,128)(2,1)S(1)} collective-permute-done((bf16[448,384]{1,0:T(8,128)(2,1)}, bf16[448,384]{1,0:T(8,128)(2,1)S(1)}, u32[]{:S(2)}, u32[]{:S(2)}) %collective-permute-start.14) | collective-permute-done | bytes 344096 | tf_op jit(solution)/shard_map/ppermute | solution.py:47
  104.1 1.7 collective-permute-done.15.refs_7_
  105.8 5.6 %collective-permute-done.16.refs_8_ = bf16[448,384]{1,0:T(8,128)(2,1)} collective-permute-done((bf16[448,384]{1,0:T(8,128)(2,1)}, bf16[448,384]{1,0:T(8,128)(2,1)}, u32[]{:S(2)}, u32[]{:S(2)}) %collective-permute-start.16) | collective-permute-done | bytes 344096 | tf_op jit(solution)/shard_map/ppermute | solution.py:47
  111.3 3.1 %shard_map.101 = (f32[8,56,128]{2,1,0:T(8,128)S(1)}, bf16[8,56,128]{2,1,0:T(8,128)(2,1)S(1)}, bf16[8,56,128]{2,1,0:T(8,128)(2,1)}, bf16[8,56,128]{2,1,0:T(8,128)...) custom-call(s32[2]{0:T(128)S(1)} %pad_add_fusion.refs_0_, ...), custom_call_target="tpu_custom_call" | custom-call | tf_op jit(solution)/shard_map/pallas_call | solution.py:215
  114.4 5.9 %collective-permute-start.24 = (bf16[8,56,128]{2,1,0:T(8,128)(2,1)S(1)}, bf16[8,56,128]{2,1,0:T(8,128)(2,1)S(1)}, u32[]{:S(2)}, u32[]{:S(2)}) collective-permute-start(bf16[8,56,128]{2,1,0:T(8,128)(2,1)S(1)} %get-tuple-element.57), channel_id=1, source_target_pairs={{0,28},{4,0},{8,4},{12,8},{16,12},{20,16},{24,20},{28,24},{1,29},{... | collective-permute-start | bytes 344072 | tf_op jit(solution)/shard_map/ppermute | solution.py:37
  120.3 2.4 %collective-permute-start.22 = (bf16[8,56,128]{2,1,0:T(8,128)(2,1)}, bf16[8,56,128]{2,1,0:T(8,128)(2,1)S(1)}, u32[]{:S(2)}, u32[]{:S(2)}) collective-permute-start(bf16[8,56,128]{2,1,0:T(8,128)(2,1)} %get-tuple-element.55), channel_id=1, source_target_pairs={{0,24},{4,28},{8,0},{12,4},{16,8},{20,12},{24,16},{28,20},{1,25},{... | collective-permute-start | bytes 344072 | tf_op jit(solution)/shard_map/ppermute | solution.py:37
  122.7 0.5 collective-permute-start.21
  123.2 2.9 %collective-permute-start.20 = (bf16[8,56,128]{2,1,0:T(8,128)(2,1)}, bf16[8,56,128]{2,1,0:T(8,128)(2,1)S(1)}, u32[]{:S(2)}, u32[]{:S(2)}) collective-permute-start(bf16[8,56,128]{2,1,0:T(8,128)(2,1)} %get-tuple-element.53), channel_id=1, source_target_pairs={{0,20},{4,24},{8,28},{12,0},{16,4},{20,8},{24,12},{28,16},{1,21},{... | collective-permute-start | bytes 344072 | tf_op jit(solution)/shard_map/ppermute | solution.py:37
  126.1 0.9 collective-permute-start.19
  127.0 3.9 %collective-permute-start.18 = (bf16[8,56,128]{2,1,0:T(8,128)(2,1)}, bf16[8,56,128]{2,1,0:T(8,128)(2,1)S(1)}, u32[]{:S(2)}, u32[]{:S(2)}) collective-permute-start(bf16[8,56,128]{2,1,0:T(8,128)(2,1)} %get-tuple-element.51), channel_id=1, source_target_pairs={{0,16},{4,20},{8,24},{12,28},{16,0},{20,4},{24,8},{28,12},{1,17},{... | collective-permute-start | bytes 344072 | tf_op jit(solution)/shard_map/ppermute | solution.py:37
  130.9 2.6 %collective-permute-done.21 = bf16[8,56,128]{2,1,0:T(8,128)(2,1)S(1)} collective-permute-done((bf16[8,56,128]{2,1,0:T(8,128)(2,1)}, bf16[8,56,128]{2,1,0:T(8,128)(2,1)S(1)}, u32[]{:S(2)}, u32[]{:S(2)}) %collective-permute-start.21) | collective-permute-done | bytes 114720 | tf_op jit(solution)/shard_map/ppermute | solution.py:37
  133.5 6.9 %collective-permute-done.19 = bf16[8,56,128]{2,1,0:T(8,128)(2,1)S(1)} collective-permute-done((bf16[8,56,128]{2,1,0:T(8,128)(2,1)}, bf16[8,56,128]{2,1,0:T(8,128)(2,1)S(1)}, u32[]{:S(2)}, u32[]{:S(2)}) %collective-permute-start.19) | collective-permute-done | bytes 114720 | tf_op jit(solution)/shard_map/ppermute | solution.py:37
  140.4 2.0 %collective-permute-done.18 = bf16[8,56,128]{2,1,0:T(8,128)(2,1)S(1)} collective-permute-done((bf16[8,56,128]{2,1,0:T(8,128)(2,1)}, bf16[8,56,128]{2,1,0:T(8,128)(2,1)S(1)}, u32[]{:S(2)}, u32[]{:S(2)}) %collective-permute-start.18) | collective-permute-done | bytes 114720 | tf_op jit(solution)/shard_map/ppermute | solution.py:37
  142.4 0.8 fusion.3
  143.2 5.7 %all-to-all-start = ((f32[8,56,128]{2,1,0:T(8,128)}), f32[8,56,128]{2,1,0:T(8,128)S(1)}, u32[]{:S(2)}, u32[]{:S(2)}) async-start(f32[8,56,128]{2,1,0:T(8,128)} %get-tuple-element.59), calls=%async_computation | async-start | bytes 458752 | tf_op jit(solution)/shard_map/all_to_all | solution.py:356
  148.9 0.2 select_reduce_fusion
  149.1 0.8 collective-permute-start.29
  149.9 3.2 %collective-permute-start.30 = (bf16[8,56,128]{2,1,0:T(8,128)(2,1)S(1)}, bf16[8,56,128]{2,1,0:T(8,128)(2,1)S(1)}, u32[]{:S(2)}, u32[]{:S(2)}) collective-permute-start(bf16[8,56,128]{2,1,0:T(8,128)(2,1)S(1)} %get-tuple-element.58.refs_0_), channel_id=1, source_target_pairs={{0,64},{32,96},{64,0},{96,32},{1,65},{33,97},{65,1},{97,33},{2,66}... | collective-permute-start | bytes 344072 | tf_op jit(solution)/shard_map/ppermute | solution.py:37
  153.1 0.5 collective-permute-start.31
  153.6 0.6 fusion.place
  154.2 3.3 %collective-permute-done.29.refs_1_ = bf16[8,56,128]{2,1,0:T(8,128)(2,1)S(1)} collective-permute-done((bf16[8,56,128]{2,1,0:T(8,128)(2,1)S(1)}, bf16[8,56,128]{2,1,0:T(8,128)(2,1)S(1)}, u32[]{:S(2)}, u32[]{:S(2)}) %collective-permute-start.29) | collective-permute-done | bytes 114720 | tf_op jit(solution)/shard_map/ppermute | solution.py:37
  157.5 0.6 collective-permute-done.31.refs_3_
  158.2 0.6 copy-done.10
  158.8 2.2 %shard_map.103 = bf16[8,56,128]{2,1,0:T(8,128)(2,1)} custom-call(s32[8]{0:T(128)} %fusion.place, bf16[8,56,128]{2,1,0:T(8,128)(2,1)} %copy-done.7, bf16[8,56,128]{2,1,0:T(8,128)(2,1)} %copy-done.8, bf16[8,56,128]{2,1,0:T(8,128)(2,1)} %copy-done.9, bf16[8,56,128]{2,1,0:T(8,128)(2,1)} %copy-done.10), custom_call_target="tpu_custom_call" | custom-call | tf_op jit(solution)/shard_map/pallas_call | solution.py:238
  161.0 6.9 %all-to-all-start.1 = ((bf16[8,56,128]{2,1,0:T(8,128)(2,1)}), bf16[8,56,128]{2,1,0:T(8,128)(2,1)S(1)}, u32[]{:S(2)}, u32[]{:S(2)}) async-start(bf16[8,56,128]{2,1,0:T(8,128)(2,1)} %shard_map.103), calls=%async_computation.1 | async-start | bytes 229376 | tf_op jit(solution)/shard_map/all_to_all | solution.py:354
  168.0 0.6 convolution_bitcast_fusion
  168.7 1.2 collective-permute-done.25
  169.9 0.9 collective-permute-start.26
  170.8 1.7 collective-permute-start.27
  172.5 1.6 collective-permute-start.28
  174.1 2.8 %all-to-all-done.1 = bf16[8,56,128]{2,1,0:T(8,128)(2,1)S(1)} async-done(((bf16[8,56,128]{2,1,0:T(8,128)(2,1)}), bf16[8,56,128]{2,1,0:T(8,128)(2,1)S(1)}, u32[]{:S(2)}, u32[]{:S(2)}) %all-to-all-start.1) | async-done | bytes 114720 | tf_op jit(solution)/shard_map/all_to_all | solution.py:354
  176.9 0.7 convert_bitcast_fusion
  177.6 2.2 %shard_map.102 = bf16[448,128]{1,0:T(8,128)(2,1)} custom-call(f32[448,128]{1,0:T(8,128)S(1)} %bitcast.24, f32[128,128]{1,0:T(8,128)S(1)} %add.84.refs_1_, f32[128,128]{1,0:T(8,128)S(1)} %collective-permute-done.26.refs_2_, f32[128,128]{1,0:T(8,128)S(1)} %collective-permute-done.27.refs_3_, f32[128,128]{1,0:T(8,128)S(1)} %collective-permute-done.28.refs_4_), custom_call_target="tpu_custom_call" | custom-call | tf_op jit(solution)/shard_map/pallas_call | solution.py:270
  (58 shorter events, 0.6 us)
Async XLA Ops:
  0.6 1.9 %copy-start = (bf16[1536,1024]{1,0:T(8,128)(2,1)S(1)}, bf16[1536,1024]{1,0:T(8,128)(2,1)}, u32[]{:S(2)}) copy-start(bf16[1536,1024]{1,0:T(8,128)(2,1)} %refs_1_.3) | copy-start | bytes 9437188
  2.5 0.7 copy-start.2
  3.2 6.8 %copy-start.11 = (f32[1536]{0:T(1024)S(1)}, f32[1536]{0:T(1024)}, u32[]{:S(2)}) copy-start(f32[1536]{0:T(1024)} %param.10) | copy-start | bytes 18436
  3.2 6.9 %copy-start.12 = (f32[1536]{0:T(1024)S(1)}, f32[1536]{0:T(1024)}, u32[]{:S(2)}) copy-start(f32[1536]{0:T(1024)} %param.11) | copy-start | bytes 18436
  3.2 6.9 %copy-start.13 = (f32[1536]{0:T(1024)S(1)}, f32[1536]{0:T(1024)}, u32[]{:S(2)}) copy-start(f32[1536]{0:T(1024)} %param.12) | copy-start | bytes 18436
  3.2 7.0 %copy-start.3 = (s32[1,768]{1,0:T(1,128)S(1)}, s32[1,768]{1,0:T(1,128)}, u32[]{:S(2)}) copy-start(s32[1,768]{1,0:T(1,128)} %refs_0_.3) | copy-start | bytes 9220
  3.2 7.0 %copy-start.4 = (bf16[1536,2,448]{0,2,1:T(8,128)(2,1)S(1)}, bf16[1536,2,448]{0,2,1:T(8,128)(2,1)}, u32[]{:S(2)}) copy-start(bf16[1536,2,448]{0,2,1:T(8,128)(2,1)} %param.9) | copy-start | bytes 8257540
  6.5 23.8 %collective-permute-start = (bf16[768,640]{1,0:T(8,128)(2,1)}, bf16[768,640]{1,0:T(8,128)(2,1)}, u32[]{:S(2)}, u32[]{:S(2)}) collective-permute-start(bf16[768,640]{1,0:T(8,128)(2,1)} %shard_map.95.refs_5_), channel_id=1, source_target_pairs={{0,128},{128,0},{2,130},{130,2},{1,129},{129,1},{3,131},{131,3},{4... | collective-permute-start | bytes 2949128 | tf_op jit(solution)/shard_map/ppermute | solution.py:33
  8.7 22.5 %collective-permute-start.1 = (bf16[768,640]{1,0:T(8,128)(2,1)}, bf16[768,640]{1,0:T(8,128)(2,1)}, u32[]{:S(2)}, u32[]{:S(2)}) collective-permute-start(bf16[768,640]{1,0:T(8,128)(2,1)} %shard_map.95.refs_5_), channel_id=1, source_target_pairs={{0,130},{128,2},{2,128},{130,0},{1,131},{129,3},{3,129},{131,1},{4... | collective-permute-start | bytes 2949128 | tf_op jit(solution)/shard_map/ppermute | solution.py:33
  13.0 22.5 %copy-start.1 = (bf16[1536,1024]{1,0:T(8,128)(2,1)S(1)}, bf16[1536,1024]{1,0:T(8,128)(2,1)}, u32[]{:S(2)}) copy-start(bf16[1536,1024]{1,0:T(8,128)(2,1)} %refs_1_.3) | copy-start | bytes 9437188
  15.8 37.9 %copy-start.5 = (bf16[448,768]{1,0:T(8,128)(2,1)}, bf16[448,768]{1,0:T(8,128)(2,1)S(1)}, u32[]{:S(2)}) copy-start(bf16[448,768]{1,0:T(8,128)(2,1)S(1)} %shard_map.97.refs_1_) | copy-start | bytes 2064388
  31.2 22.5 %collective-permute-start.2 = (bf16[768,640]{1,0:T(8,128)(2,1)}, bf16[768,640]{1,0:T(8,128)(2,1)S(1)}, u32[]{:S(2)}, u32[]{:S(2)}) collective-permute-start(bf16[768,640]{1,0:T(8,128)(2,1)} %collective-permute-done.refs_6_), channel_id=1, source_target_pairs={{0,130},{128,2},{2,128},{130,0},{1,131},{129,3},{3,129},{131,1},{4... | collective-permute-start | bytes 2949128 | tf_op jit(solution)/shard_map/ppermute | solution.py:33
  32.9 16.5 %collective-permute-start.3 = (bf16[448,768]{1,0:T(8,128)(2,1)S(1)}, bf16[448,768]{1,0:T(8,128)(2,1)S(1)}, u32[]{:S(2)}, u32[]{:S(2)}) collective-permute-start(bf16[448,768]{1,0:T(8,128)(2,1)S(1)} %shard_map.96), channel_id=1, source_target_pairs={{0,128},{128,0},{2,130},{130,2},{1,129},{129,1},{3,131},{131,3},{4... | collective-permute-start | bytes 2064392 | tf_op jit(solution)/shard_map/ppermute | solution.py:33
  35.5 14.0 %collective-permute-start.4 = (bf16[448,768]{1,0:T(8,128)(2,1)S(1)}, bf16[448,768]{1,0:T(8,128)(2,1)S(1)}, u32[]{:S(2)}, u32[]{:S(2)}) collective-permute-start(bf16[448,768]{1,0:T(8,128)(2,1)S(1)} %shard_map.97.refs_1_), channel_id=1, source_target_pairs={{0,1},{1,0},{2,3},{3,2},{4,5},{5,4},{6,7},{7,6},{8,9},{9,8},{10,11... | collective-permute-start | bytes 2064392 | tf_op jit(solution)/shard_map/ppermute | solution.py:37
  53.7 5.8 %collective-permute-start.5 = (bf16[448,768]{1,0:T(8,128)(2,1)S(1)}, bf16[448,768]{1,0:T(8,128)(2,1)}, u32[]{:S(2)}, u32[]{:S(2)}) collective-permute-start(bf16[448,768]{1,0:T(8,128)(2,1)S(1)} %collective-permute-done.3.refs_2_), channel_id=1, source_target_pairs={{0,1},{1,0},{2,3},{3,2},{4,5},{5,4},{6,7},{7,6},{8,9},{9,8},{10,11... | collective-permute-start | bytes 2064392 | tf_op jit(solution)/shard_map/ppermute | solution.py:37
  53.7 17.6 %collective-permute-start.11 = (bf16[768,384]{1,0:T(8,128)(2,1)S(1)}, bf16[768,384]{1,0:T(8,128)(2,1)S(1)}, u32[]{:S(2)}, u32[]{:S(2)}) collective-permute-start(bf16[768,384]{1,0:T(8,128)(2,1)S(1)} %shard_map.98.refs_2_), channel_id=1, source_target_pairs={{0,130},{128,2},{2,128},{130,0},{1,131},{129,3},{3,129},{131,1},{4... | collective-permute-start | bytes 1769480 | tf_op jit(solution)/shard_map/ppermute | solution.py:33
  55.5 18.4 %collective-permute-start.10 = (bf16[768,384]{1,0:T(8,128)(2,1)S(1)}, bf16[768,384]{1,0:T(8,128)(2,1)S(1)}, u32[]{:S(2)}, u32[]{:S(2)}) collective-permute-start(bf16[768,384]{1,0:T(8,128)(2,1)S(1)} %shard_map.98.refs_2_), channel_id=1, source_target_pairs={{0,128},{128,0},{2,130},{130,2},{1,129},{129,1},{3,131},{131,3},{4... | collective-permute-start | bytes 1769480 | tf_op jit(solution)/shard_map/ppermute | solution.py:33
  59.5 1.1 copy-start.6
  67.3 17.1 %collective-permute-start.6 = (bf16[448,640]{1,0:T(8,128)(2,1)S(1)}, bf16[448,640]{1,0:T(8,128)(2,1)S(1)}, u32[]{:S(2)}, u32[]{:S(2)}) collective-permute-start(bf16[448,640]{1,0:T(8,128)(2,1)S(1)} %get-tuple-element.40), channel_id=1, source_target_pairs={{0,65},{1,33},{32,64},{33,96},{64,1},{65,97},{96,0},{97,32},{2,67}... | collective-permute-start | bytes 1720328 | tf_op jit(solution)/shard_map/ppermute | solution.py:47
  70.0 21.5 %collective-permute-start.7 = (bf16[448,640]{1,0:T(8,128)(2,1)S(1)}, bf16[448,640]{1,0:T(8,128)(2,1)S(1)}, u32[]{:S(2)}, u32[]{:S(2)}) collective-permute-start(bf16[448,640]{1,0:T(8,128)(2,1)S(1)} %get-tuple-element.41), channel_id=1, source_target_pairs={{0,1},{1,97},{32,0},{33,32},{64,65},{65,33},{96,64},{97,96},{2,3},... | collective-permute-start | bytes 1720328 | tf_op jit(solution)/shard_map/ppermute | solution.py:47
  70.0 26.5 %collective-permute-start.8 = (bf16[448,640]{1,0:T(8,128)(2,1)S(1)}, bf16[448,640]{1,0:T(8,128)(2,1)S(1)}, u32[]{:S(2)}, u32[]{:S(2)}) collective-permute-start(bf16[448,640]{1,0:T(8,128)(2,1)S(1)} %get-tuple-element.42), channel_id=1, source_target_pairs={{0,64},{1,32},{32,65},{33,97},{64,0},{65,96},{96,1},{97,33},{2,66}... | collective-permute-start | bytes 1720328 | tf_op jit(solution)/shard_map/ppermute | solution.py:47
  71.3 9.9 %collective-permute-start.12 = (bf16[384,384]{1,0:T(8,128)(2,1)S(1)}, bf16[384,384]{1,0:T(8,128)(2,1)S(1)}, u32[]{:S(2)}, u32[]{:S(2)}) collective-permute-start(bf16[384,384]{1,0:T(8,128)(2,1)S(1)} %slice.8), channel_id=1, source_target_pairs={{0,128},{128,0},{2,130},{130,2},{1,129},{129,1},{3,131},{131,3},{4... | collective-permute-start | bytes 884744 | tf_op jit(solution)/shard_map/ppermute | solution.py:33
  74.0 8.4 %collective-permute-start.13 = (bf16[384,384]{1,0:T(8,128)(2,1)S(1)}, bf16[384,384]{1,0:T(8,128)(2,1)S(1)}, u32[]{:S(2)}, u32[]{:S(2)}) collective-permute-start(bf16[384,384]{1,0:T(8,128)(2,1)S(1)} %slice.9), channel_id=1, source_target_pairs={{0,130},{128,2},{2,128},{130,0},{1,131},{129,3},{3,129},{131,1},{4... | collective-permute-start | bytes 884744 | tf_op jit(solution)/shard_map/ppermute | solution.py:33
  81.2 16.8 %collective-permute-start.9 = (bf16[448,640]{1,0:T(8,128)(2,1)S(1)}, bf16[448,640]{1,0:T(8,128)(2,1)S(1)}, u32[]{:S(2)}, u32[]{:S(2)}) collective-permute-start(bf16[448,640]{1,0:T(8,128)(2,1)S(1)} %get-tuple-element.43.refs_5_), channel_id=1, source_target_pairs={{1,96},{32,1},{65,32},{96,65},{3,98},{34,3},{67,34},{98,67},{5,100... | collective-permute-start | bytes 1720328 | tf_op jit(solution)/shard_map/ppermute | solution.py:47
  89.1 15.0 %collective-permute-start.14 = (bf16[448,384]{1,0:T(8,128)(2,1)}, bf16[448,384]{1,0:T(8,128)(2,1)S(1)}, u32[]{:S(2)}, u32[]{:S(2)}) collective-permute-start(bf16[448,384]{1,0:T(8,128)(2,1)} %get-tuple-element.46), channel_id=1, source_target_pairs={{0,65},{1,33},{32,64},{33,96},{64,1},{65,97},{96,0},{97,32},{2,67}... | collective-permute-start | bytes 1032200 | tf_op jit(solution)/shard_map/ppermute | solution.py:47
  91.5 14.3 %collective-permute-start.15 = (bf16[448,384]{1,0:T(8,128)(2,1)}, bf16[448,384]{1,0:T(8,128)(2,1)}, u32[]{:S(2)}, u32[]{:S(2)}) collective-permute-start(bf16[448,384]{1,0:T(8,128)(2,1)} %get-tuple-element.47), channel_id=1, source_target_pairs={{0,1},{1,97},{32,0},{33,32},{64,65},{65,33},{96,64},{97,96},{2,3},... | collective-permute-start | bytes 1032200 | tf_op jit(solution)/shard_map/ppermute | solution.py:47
  91.5 19.8 %collective-permute-start.16 = (bf16[448,384]{1,0:T(8,128)(2,1)}, bf16[448,384]{1,0:T(8,128)(2,1)}, u32[]{:S(2)}, u32[]{:S(2)}) collective-permute-start(bf16[448,384]{1,0:T(8,128)(2,1)} %get-tuple-element.48), channel_id=1, source_target_pairs={{0,64},{1,32},{32,65},{33,97},{64,0},{65,96},{96,1},{97,33},{2,66}... | collective-permute-start | bytes 1032200 | tf_op jit(solution)/shard_map/ppermute | solution.py:47
  96.5 14.9 %collective-permute-start.17 = (bf16[448,384]{1,0:T(8,128)(2,1)}, bf16[448,384]{1,0:T(8,128)(2,1)}, u32[]{:S(2)}, u32[]{:S(2)}) collective-permute-start(bf16[448,384]{1,0:T(8,128)(2,1)} %get-tuple-element.49.refs_10_), channel_id=1, source_target_pairs={{1,96},{32,1},{65,32},{96,65},{3,98},{34,3},{67,34},{98,67},{5,100... | collective-permute-start | bytes 1032200 | tf_op jit(solution)/shard_map/ppermute | solution.py:47
  98.0 50.9 %copy-start.14 = (s32[32]{0:T(128)S(1)}, s32[32]{0:T(128)}, u32[]{:S(2)}) copy-start(s32[32]{0:T(128)} %param.15) | copy-start | bytes 388
  114.4 11.7 %collective-permute-start.24 = (bf16[8,56,128]{2,1,0:T(8,128)(2,1)S(1)}, bf16[8,56,128]{2,1,0:T(8,128)(2,1)S(1)}, u32[]{:S(2)}, u32[]{:S(2)}) collective-permute-start(bf16[8,56,128]{2,1,0:T(8,128)(2,1)S(1)} %get-tuple-element.57), channel_id=1, source_target_pairs={{0,28},{4,0},{8,4},{12,8},{16,12},{20,16},{24,20},{28,24},{1,29},{... | collective-permute-start | bytes 344072 | tf_op jit(solution)/shard_map/ppermute | solution.py:37
  120.3 6.8 %collective-permute-start.23 = (bf16[8,56,128]{2,1,0:T(8,128)(2,1)S(1)}, bf16[8,56,128]{2,1,0:T(8,128)(2,1)S(1)}, u32[]{:S(2)}, u32[]{:S(2)}) collective-permute-start(bf16[8,56,128]{2,1,0:T(8,128)(2,1)S(1)} %get-tuple-element.56), channel_id=1, source_target_pairs={{0,4},{4,8},{8,12},{12,16},{16,20},{20,24},{24,28},{28,0},{1,5},{5... | collective-permute-start | bytes 344072 | tf_op jit(solution)/shard_map/ppermute | solution.py:37
  120.3 10.6 %collective-permute-start.22 = (bf16[8,56,128]{2,1,0:T(8,128)(2,1)}, bf16[8,56,128]{2,1,0:T(8,128)(2,1)S(1)}, u32[]{:S(2)}, u32[]{:S(2)}) collective-permute-start(bf16[8,56,128]{2,1,0:T(8,128)(2,1)} %get-tuple-element.55), channel_id=1, source_target_pairs={{0,24},{4,28},{8,0},{12,4},{16,8},{20,12},{24,16},{28,20},{1,25},{... | collective-permute-start | bytes 344072 | tf_op jit(solution)/shard_map/ppermute | solution.py:37
  122.7 10.8 %collective-permute-start.21 = (bf16[8,56,128]{2,1,0:T(8,128)(2,1)}, bf16[8,56,128]{2,1,0:T(8,128)(2,1)S(1)}, u32[]{:S(2)}, u32[]{:S(2)}) collective-permute-start(bf16[8,56,128]{2,1,0:T(8,128)(2,1)} %get-tuple-element.54), channel_id=1, source_target_pairs={{0,8},{4,12},{8,16},{12,20},{16,24},{20,28},{24,0},{28,4},{1,9},{5... | collective-permute-start | bytes 344072 | tf_op jit(solution)/shard_map/ppermute | solution.py:37
  123.2 10.3 %collective-permute-start.20 = (bf16[8,56,128]{2,1,0:T(8,128)(2,1)}, bf16[8,56,128]{2,1,0:T(8,128)(2,1)S(1)}, u32[]{:S(2)}, u32[]{:S(2)}) collective-permute-start(bf16[8,56,128]{2,1,0:T(8,128)(2,1)} %get-tuple-element.53), channel_id=1, source_target_pairs={{0,20},{4,24},{8,28},{12,0},{16,4},{20,8},{24,12},{28,16},{1,21},{... | collective-permute-start | bytes 344072 | tf_op jit(solution)/shard_map/ppermute | solution.py:37
  126.1 14.3 %collective-permute-start.19 = (bf16[8,56,128]{2,1,0:T(8,128)(2,1)}, bf16[8,56,128]{2,1,0:T(8,128)(2,1)S(1)}, u32[]{:S(2)}, u32[]{:S(2)}) collective-permute-start(bf16[8,56,128]{2,1,0:T(8,128)(2,1)} %get-tuple-element.52), channel_id=1, source_target_pairs={{0,12},{4,16},{8,20},{12,24},{16,28},{20,0},{24,4},{28,8},{1,13},{... | collective-permute-start | bytes 344072 | tf_op jit(solution)/shard_map/ppermute | solution.py:37
  127.0 15.4 %collective-permute-start.18 = (bf16[8,56,128]{2,1,0:T(8,128)(2,1)}, bf16[8,56,128]{2,1,0:T(8,128)(2,1)S(1)}, u32[]{:S(2)}, u32[]{:S(2)}) collective-permute-start(bf16[8,56,128]{2,1,0:T(8,128)(2,1)} %get-tuple-element.51), channel_id=1, source_target_pairs={{0,16},{4,20},{8,24},{12,28},{16,0},{20,4},{24,8},{28,12},{1,17},{... | collective-permute-start | bytes 344072 | tf_op jit(solution)/shard_map/ppermute | solution.py:37
  143.2 14.9 %copy-start.7 = (bf16[8,56,128]{2,1,0:T(8,128)(2,1)}, bf16[8,56,128]{2,1,0:T(8,128)(2,1)S(1)}, u32[]{:S(2)}) copy-start(bf16[8,56,128]{2,1,0:T(8,128)(2,1)S(1)} %get-tuple-element.58.refs_0_) | copy-start | bytes 344068
  143.2 17.8 %all-to-all-start = ((f32[8,56,128]{2,1,0:T(8,128)}), f32[8,56,128]{2,1,0:T(8,128)S(1)}, u32[]{:S(2)}, u32[]{:S(2)}) async-start(f32[8,56,128]{2,1,0:T(8,128)} %get-tuple-element.59), calls=%async_computation | async-start | bytes 458752 | tf_op jit(solution)/shard_map/all_to_all | solution.py:356
  149.1 8.4 %collective-permute-start.29 = (bf16[8,56,128]{2,1,0:T(8,128)(2,1)S(1)}, bf16[8,56,128]{2,1,0:T(8,128)(2,1)S(1)}, u32[]{:S(2)}, u32[]{:S(2)}) collective-permute-start(bf16[8,56,128]{2,1,0:T(8,128)(2,1)S(1)} %get-tuple-element.58.refs_0_), channel_id=1, source_target_pairs={{0,32},{32,64},{64,96},{96,0},{1,33},{33,65},{65,97},{97,1},{2,34}... | collective-permute-start | bytes 344072 | tf_op jit(solution)/shard_map/ppermute | solution.py:37
  149.9 7.6 %collective-permute-start.30 = (bf16[8,56,128]{2,1,0:T(8,128)(2,1)S(1)}, bf16[8,56,128]{2,1,0:T(8,128)(2,1)S(1)}, u32[]{:S(2)}, u32[]{:S(2)}) collective-permute-start(bf16[8,56,128]{2,1,0:T(8,128)(2,1)S(1)} %get-tuple-element.58.refs_0_), channel_id=1, source_target_pairs={{0,64},{32,96},{64,0},{96,32},{1,65},{33,97},{65,1},{97,33},{2,66}... | collective-permute-start | bytes 344072 | tf_op jit(solution)/shard_map/ppermute | solution.py:37
  153.1 5.0 %collective-permute-start.31 = (bf16[8,56,128]{2,1,0:T(8,128)(2,1)S(1)}, bf16[8,56,128]{2,1,0:T(8,128)(2,1)S(1)}, u32[]{:S(2)}, u32[]{:S(2)}) collective-permute-start(bf16[8,56,128]{2,1,0:T(8,128)(2,1)S(1)} %get-tuple-element.58.refs_0_), channel_id=1, source_target_pairs={{0,96},{32,0},{64,32},{96,64},{1,97},{33,1},{65,33},{97,65},{2,98}... | collective-permute-start | bytes 344072 | tf_op jit(solution)/shard_map/ppermute | solution.py:37
  157.5 0.6 copy-start.8
  157.5 0.7 copy-start.9
  158.2 0.6 copy-start.10
  161.0 15.9 %all-to-all-start.1 = ((bf16[8,56,128]{2,1,0:T(8,128)(2,1)}), bf16[8,56,128]{2,1,0:T(8,128)(2,1)S(1)}, u32[]{:S(2)}, u32[]{:S(2)}) async-start(bf16[8,56,128]{2,1,0:T(8,128)(2,1)} %shard_map.103), calls=%async_computation.1 | async-start | bytes 229376 | tf_op jit(solution)/shard_map/all_to_all | solution.py:354
  168.6 1.3 collective-permute-start.25
  169.9 7.7 %collective-permute-start.26 = (f32[128,128]{1,0:T(8,128)S(1)}, f32[128,128]{1,0:T(8,128)S(1)}, u32[]{:S(2)}, u32[]{:S(2)}) collective-permute-start(f32[128,128]{1,0:T(8,128)S(1)} %add.84.refs_1_), channel_id=1, source_target_pairs={{0,2},{128,130},{2,0},{130,128},{1,3},{129,131},{3,1},{131,129},{4... | collective-permute-start | bytes 196616 | tf_op jit(solution)/shard_map/ppermute | solution.py:33
  170.8 6.8 %collective-permute-start.27 = (f32[128,128]{1,0:T(8,128)S(1)}, f32[128,128]{1,0:T(8,128)S(1)}, u32[]{:S(2)}, u32[]{:S(2)}) collective-permute-start(f32[128,128]{1,0:T(8,128)S(1)} %add.84.refs_1_), channel_id=1, source_target_pairs={{0,128},{128,0},{2,130},{130,2},{1,129},{129,1},{3,131},{131,3},{4... | collective-permute-start | bytes 196616 | tf_op jit(solution)/shard_map/ppermute | solution.py:33
  172.5 5.1 %collective-permute-start.28 = (f32[128,128]{1,0:T(8,128)S(1)}, f32[128,128]{1,0:T(8,128)S(1)}, u32[]{:S(2)}, u32[]{:S(2)}) collective-permute-start(f32[128,128]{1,0:T(8,128)S(1)} %add.84.refs_1_), channel_id=1, source_target_pairs={{0,130},{128,2},{2,128},{130,0},{1,131},{129,3},{3,129},{131,1},{4... | collective-permute-start | bytes 196616 | tf_op jit(solution)/shard_map/ppermute | solution.py:33

commit v5 on v3

--- a/solution.py
+++ b/solution.py
@@ -118,58 +118,89 @@
     )(jnp.stack([half, tally]).astype(jnp.int32), kept, benefit, present, behaviour, adjoint)
 
 
-def partial_kernel(counts, plan, *refs):
-    s_refs, out_refs = refs[:4], refs[-6:-2]
-    s_all, total = refs[-2:]
+def dots(s_all, groups):
+    cap = s_all.shape[1] // len(groups)
+    value = None
+    for i, group in enumerate(groups):
+        blocks = [ref[...] for ref in group]
+        block = blocks[0] if len(blocks) == 1 else jnp.concatenate(blocks, axis=0)
+        term = jnp.dot(
+            s_all[:, i * cap : (i + 1) * cap], block, preferred_element_type=jnp.float32
+        )
+        value = term if value is None else value + term
+    return value
+
+
+def near_kernel(*refs):
+    s_refs, (own, e1, near, s_all) = refs[:4], refs[4:]
     q, cap = s_refs[0].shape
     for i, ref in enumerate(s_refs):
         side, other = divmod(i, 2)
         s_all[side * q : (side + 1) * q, other * cap : (other + 1) * cap] = ref[...]
-
-    at = 4
+    near[...] = dots(s_all, ((own,), (e1,))).astype(near.dtype)
+
+
+def near_terms(s_list, own, e1):
+    q, cap = s_list[0].shape
+    cols = own.shape[1]
+    full = pl.BlockSpec(memory_space=pltpu.VMEM)
+    return pl.pallas_call(
+        near_kernel,
+        in_specs=[full] * 6,
+        out_specs=[full] * 2,
+        out_shape=[
+            jax.ShapeDtypeStruct((2 * q, cols), jnp.bfloat16),
+            jax.ShapeDtypeStruct((2 * q, 2 * cap), jnp.bfloat16),
+        ],
+        compiler_params=pltpu.CompilerParams(vmem_limit_bytes=20 * 2**20),
+        cost_estimate=pl.CostEstimate(
+            flops=8 * q * cap * cols, bytes_accessed=6 * 2**20, transcendentals=0
+        ),
+    )(*s_list, own, e1)
+
+
+def terms_kernel(counts, plan, s_all, *refs):
+    total, out_refs = refs[-1], refs[-5:-1]
+    q = out_refs[0].shape[0]
+    at = 0
+    chunks = []
     for chunk in range(2):
-        value = None
-        for other in range(2):
-            count = counts[2 * chunk + other]
-            blocks = [ref[...] for ref in refs[at : at + count]]
+        groups = []
+        for count in counts[chunk]:
+            groups.append(refs[at : at + count])
             at += count
-            block = blocks[0] if count == 1 else jnp.concatenate(blocks, axis=0)
-            term = jnp.dot(
-                s_all[:, other * cap : (other + 1) * cap],
-                block,
-                preferred_element_type=jnp.float32,
-            )
-            value = term if value is None else value + term
-        value = value.astype(total.dtype)
+        if len(groups) == 1:
+            chunks.append(groups[0][0][...])
+        else:
+            chunks.append(dots(s_all, groups).astype(total.dtype))
+    for chunk, value in enumerate(chunks):
         for side in range(2):
             total[2 * chunk + side] = value[side * q : (side + 1) * q]
     for slot, out_ref in enumerate(out_refs):
         out_ref[...] = total[plan[slot]]
 
 
-def partials(plan, s_list, own, e1, opposite, e3, after=()):
-    q, cap = s_list[0].shape
-    cols = own[0].shape[1]
-    groups = (own, e1, opposite, e3)
-    counts = tuple(len(group) for group in groups)
+def terms_of(plan, s_all, near, far, after=()):
+    q, cols = s_all.shape[0] // 2, far[0][0].shape[1]
+    groups = (*near, *far)
+    counts = (tuple(len(group) for group in near), tuple(len(group) for group in far))
     values = [block for group in groups for block in group]
     full = pl.BlockSpec(memory_space=pltpu.VMEM)
     return pl.pallas_call(
-        lambda *refs: partial_kernel(counts, *refs),
+        lambda *refs: terms_kernel(counts, *refs),
         in_specs=[pl.BlockSpec(memory_space=pltpu.SMEM)]
-        + [full] * (4 + len(values))
+        + [full] * (1 + len(values))
         + [pl.BlockSpec(memory_space=pl.ANY)] * len(after),
         out_specs=[full] * 4,
-        scratch_shapes=[
-            pltpu.VMEM((2 * q, 2 * cap), jnp.bfloat16),
-            pltpu.VMEM((4, q, cols), jnp.bfloat16),
-        ],
+        scratch_shapes=[pltpu.VMEM((4, q, cols), jnp.bfloat16)],
         out_shape=[jax.ShapeDtypeStruct((q, cols), jnp.bfloat16)] * 4,
         compiler_params=pltpu.CompilerParams(vmem_limit_bytes=20 * 2**20),
         cost_estimate=pl.CostEstimate(
-            flops=8 * q * 2 * cap * cols, bytes_accessed=8 * 2**20, transcendentals=0
-        ),
-    )(plan, *s_list, *values, *after)
+            flops=2 * s_all.shape[0] * s_all.shape[1] * cols * len(groups) // 2,
+            bytes_accessed=8 * 2**20,
+            transcendentals=0,
+        ),
+    )(plan, s_all, *values, *after)
 
 
 def rows_kernel(piece_count, plan, *refs):
@@ -286,7 +317,7 @@
         for start, stop in ((0, FIRST), (FIRST, mixer_vectors.shape[1]))
     ]
     adjoint = upstream_adjoint.transpose(1, 2, 0)
-    kept, adjoint, *own = barrier((retained_entries, adjoint, *own))
+    kept, adjoint, own[0] = barrier((retained_entries, adjoint, own[0]))
     rows_of = [
         v[None, :] for v in (relative_benefit, present_policy_logit, behaviour_policy_logit)
     ]
@@ -312,19 +343,21 @@
         ]
 
     e1, e3 = over_y(own[0], 1), over_y(own[0], 3)
-    e1, e3, s_send, s_keep, second = barrier((e1, e3, s_send, s_keep, own[1]))
+    e1, e3, s_send, s_keep = barrier((e1, e3, s_send, s_keep))
     opposite = over_y(e1, 3)
     s_recv = over_y(s_send, 1)
     c_keep = shift(s_keep, "c", C, 1)
-    opposite, s_recv, c_keep, second = barrier((opposite, s_recv, c_keep, second))
+    s_list = (s_keep, s_recv, c_keep, shift(s_recv, "c", C, 1))
+    near_product, s_all = near_terms(s_list, own[0], e1)
+    opposite, near_product, second = barrier((opposite, near_product, own[1]))
     f1, f3 = over_y(second, 1), over_y(second, 3)
-    c_recv = shift(s_recv, "c", C, 1)
-    s_list = (s_keep, s_recv, c_keep, c_recv)
-    first_terms = partials(plan, s_list, [own[0]], [e1], [opposite], [e3])
+    first_terms = terms_of(plan, s_all, [[near_product]], [[opposite], [e3]])
     first_sums = over_x(first_terms)
     cut = second.shape[0] // 2
     fa, fb = over_y(f3[:cut], 1), over_y(f1[cut:], 3)
-    second_terms = partials(plan, s_list, [second], [f1], [fa, fb], [f3], first_sums[:1])
+    second_terms = terms_of(
+        plan, s_all, [[second], [f1]], [[fa, fb], [f3]], first_sums[:1]
+    )
     second_sums = over_x(second_terms)
 
     head = mixer_vectors.shape[1] // Z

time: 183 us -> 178 us (0.973)
  local copies, waits for them, and re-layouts: 7.6 us -> 4.1 us
  waiting for transfers between devices: 73 us -> 69.7 us
  Pallas kernels: 29.7 us -> 31.9 us
    ppermute x11, waiting for transfers between devices: 38.7 us -> 31.5 us  [over_y(): return lax.ppermute(value, ('yl', 'yh'), ring_pairs(flip))]
    unnamed x36 -> x28, local copies, waits for them, and re-layouts: 7.52 us -> 4.02 us
    ppermute x8, waiting for transfers between devices: 15.6 us -> 19.1 us  [over_xc(): return lax.ppermute(value, ('x', 'c'), pairs)]
    ppermute x11, starting transfers between devices: 21.6 us -> 19.4 us  [over_y(): return lax.ppermute(value, ('yl', 'yh'), ring_pairs(flip))]
    ppermute x13, starting transfers between devices: 20.8 us -> 22.7 us  [shift(): lax.ppermute(value, axis, [(i, (i + step) % size) for i in range(size)])]
    pallas_call x2 -> x3, Pallas kernels: 11.9 us -> 13.2 us  [the longest x2 8.61 us: terms_of(): pl.pallas_call(lambda *refs: terms_kernel(counts, *refs), in_specs=[pl.Bl...]
  transfers between devices with their start and end apart: 34 -> 34, of which waited for: 18 -> 20; matrix products, arithmetic and copies ran while one was open for 1% -> 2% of each run, Pallas kernels for 11% -> 13%
where the time goes in v5:
time: 178 us; the launch traced here: 177 us
  waiting for transfers between devices  69.7 us (39%)
  starting transfers between devices  65.6 us (37%)
  Pallas kernels  31.9 us (18%)
  other arithmetic  4.12 us (2%)
  local copies, waits for them, and re-layouts  4.1 us (2%)
    ppermute x11, waiting for transfers between devices, over_y(): return lax.ppermute(value, ('yl', 'yh'), ring_pairs(flip))  31.5 us
    ppermute x13, starting transfers between devices, shift(): lax.ppermute(value, axis, [(i, (i + step) % size) for i in range(size)])  22.7 us
    ppermute x11, starting transfers between devices, over_y(): return lax.ppermute(value, ('yl', 'yh'), ring_pairs(flip))  19.4 us
    ppermute x8, waiting for transfers between devices, over_xc(): return lax.ppermute(value, ('x', 'c'), pairs)  19.1 us
    ppermute x13, waiting for transfers between devices, shift(): lax.ppermute(value, axis, [(i, (i + step) % size) for i in range(size)])  16.3 us
    ppermute x8, starting transfers between devices, over_xc(): return lax.ppermute(value, ('x', 'c'), pairs)  11.5 us
    pallas_call x2, Pallas kernels, terms_of(): pl.pallas_call(lambda *refs: terms_kernel(counts, *refs), in_specs=[pl.Bl...  8.61 us
    all_to_all x1, starting transfers between devices, on_device(): arrived = lax.all_to_all(chosen, 'z', 0, 0, tiled=True).reshape(q, head)  7.13 us
  transfers between devices with their start and end apart: 34, of which 20 were waited for; matrix products, arithmetic and copies ran while one was open for 2% of the time, Pallas kernels for 13%

profile of v5, /device:TPU:8, one launch (start us, length us, event | category | flops | bytes accessed | tf_op | source)
XLA Modules:
  0.0 177.5 jit_solution(11036871777097001343)
XLA Ops:
  0.6 1.9 %copy-done = bf16[1536,1024]{1,0:T(8,128)(2,1)S(1)} copy-done((bf16[1536,1024]{1,0:T(8,128)(2,1)S(1)}, bf16[1536,1024]{1,0:T(8,128)(2,1)}, u32[]{:S(2)}) %copy-start) | copy-done | bytes 3145752
  2.5 0.7 copy-done.3
  3.2 3.3 %shard_map.95.refs_4_ = bf16[768,640]{1,0:T(8,128)(2,1)} custom-call(s32[1,768]{1,0:T(1,128)S(1)} %copy-done.3, bf16[1536,1024]{1,0:T(8,128)(2,1)S(1)} %copy-done), custom_call_target="tpu_custom_call" | custom-call | flops 1509949440 | bytes 2949120 | tf_op jit(solution)/shard_map/pallas_call | solution.py:64
  6.5 2.2 %collective-permute-start = (bf16[768,640]{1,0:T(8,128)(2,1)}, bf16[768,640]{1,0:T(8,128)(2,1)}, u32[]{:S(2)}, u32[]{:S(2)}) collective-permute-start(bf16[768,640]{1,0:T(8,128)(2,1)} %shard_map.95.refs_4_), channel_id=1, source_target_pairs={{0,128},{128,0},{2,130},{130,2},{1,129},{129,1},{3,131},{131,3},{4... | collective-permute-start | bytes 2949128 | tf_op jit(solution)/shard_map/ppermute | solution.py:33
  8.7 0.7 collective-permute-start.1
  10.2 2.8 %shard_map.96 = bf16[448,768]{1,0:T(8,128)(2,1)S(1)} custom-call(s32[2]{0:T(128)S(1)} %get-tuple-element.60.plan, s32[1,768]{1,0:T(1,128)S(1)} %copy-done.4, f32[1,1536]{1,0:T(1,128)S(1)} %broadcast_in_dim.33.benefit_ref, f32[1,1536]{1,0:T(1,128)S(1)} %broadcast_in_dim.34.present_ref, f32[1,1536]{1,0:T(1,128)S(1)} %broadcast_in_dim.35.behaviour_ref, ...), custom_call_target="tpu_custom_call" | custom-call | flops 1056964608 | bytes 2064384 | tf_op jit(solution)/shard_map/pallas_call | solution.py:99
  13.0 3.6 %shard_map.97.refs_0_ = bf16[448,768]{1,0:T(8,128)(2,1)} custom-call(s32[2]{0:T(128)S(1)} %get-tuple-element.61.plan, s32[1,768]{1,0:T(1,128)S(1)} %copy-done.4, f32[1,1536]{1,0:T(1,128)S(1)} %broadcast_in_dim.33.benefit_ref, f32[1,1536]{1,0:T(1,128)S(1)} %broadcast_in_dim.34.present_ref, f32[1,1536]{1,0:T(1,128)S(1)} %broadcast_in_dim.35.behaviour_ref, ...), custom_call_target="tpu_custom_call" | custom-call | flops 1056964608 | bytes 2064384 | tf_op jit(solution)/shard_map/pallas_call | solution.py:99
  16.7 13.7 %collective-permute-done.refs_5_ = bf16[768,640]{1,0:T(8,128)(2,1)} collective-permute-done((bf16[768,640]{1,0:T(8,128)(2,1)}, bf16[768,640]{1,0:T(8,128)(2,1)}, u32[]{:S(2)}, u32[]{:S(2)}) %collective-permute-start) | collective-permute-done | bytes 983072 | tf_op jit(solution)/shard_map/ppermute | solution.py:33
  30.3 0.9 collective-permute-done.1.refs_4_
  31.2 2.1 %collective-permute-start.2 = (bf16[448,768]{1,0:T(8,128)(2,1)S(1)}, bf16[448,768]{1,0:T(8,128)(2,1)}, u32[]{:S(2)}, u32[]{:S(2)}) collective-permute-start(bf16[448,768]{1,0:T(8,128)(2,1)S(1)} %shard_map.96), channel_id=1, source_target_pairs={{0,128},{128,0},{2,130},{130,2},{1,129},{129,1},{3,131},{131,3},{4... | collective-permute-start | bytes 2064392 | tf_op jit(solution)/shard_map/ppermute | solution.py:33
  33.3 1.6 collective-permute-start.5
  34.9 12.6 %collective-permute-done.2.refs_1_ = bf16[448,768]{1,0:T(8,128)(2,1)} collective-permute-done((bf16[448,768]{1,0:T(8,128)(2,1)S(1)}, bf16[448,768]{1,0:T(8,128)(2,1)}, u32[]{:S(2)}, u32[]{:S(2)}) %collective-permute-start.2) | collective-permute-done | bytes 688160 | tf_op jit(solution)/shard_map/ppermute | solution.py:33
  47.5 1.7 shard_map.99.refs_2_
  49.2 0.8 collective-permute-done.4.refs_3_
  50.0 4.6 %shard_map.98 = (bf16[896,640]{1,0:T(8,128)(2,1)S(1)}, bf16[896,1536]{1,0:T(8,128)(2,1)S(1)}) custom-call(bf16[448,768]{1,0:T(8,128)(2,1)} %shard_map.97.refs_0_, bf16[448,768]{1,0:T(8,128)(2,1)} %collective-permute-done.2.refs_1_, bf16[448,768]{1,0:T(8,128)(2,1)} %collective-permute-done.3.refs_2_, bf16[448,768]{1,0:T(8,128)(2,1)} %collective-permute-done.4.refs_3_, ...), custom_call_target="tpu_custom_call" | custom-call | flops 1761607680 | bytes 6291456 | tf_op jit(solution)/shard_map/pallas_call | solution.py:147
  54.6 0.9 collective-permute-done.5.refs_3_
  55.5 1.7 collective-permute-start.11
  57.2 2.1 %collective-permute-start.10 = (bf16[768,384]{1,0:T(8,128)(2,1)S(1)}, bf16[768,384]{1,0:T(8,128)(2,1)S(1)}, u32[]{:S(2)}, u32[]{:S(2)}) collective-permute-start(bf16[768,384]{1,0:T(8,128)(2,1)S(1)} %shard_map.99.refs_2_), channel_id=1, source_target_pairs={{0,128},{128,0},{2,130},{130,2},{1,129},{129,1},{3,131},{131,3},{4... | collective-permute-start | bytes 1769480 | tf_op jit(solution)/shard_map/ppermute | solution.py:33
  59.4 4.1 %shard_map.100 = (bf16[448,640]{1,0:T(8,128)(2,1)S(1)}, bf16[448,640]{1,0:T(8,128)(2,1)S(1)}, bf16[448,640]{1,0:T(8,128)(2,1)S(1)}, bf16[448,640]{1,0:T(8,128)(2,1)S(1)}) custom-call(s32[4]{0:T(128)S(1)} %broadcast_select_fusion.refs_0_, bf16[896,1536]{1,0:T(8,128)(2,1)S(1)} %get-tuple-element.36.refs_1_, bf16[896,640]{1,0:T(8,128)(2,1)S(1)} %get-tuple-element.38.refs_2_, ...), custom_call_target="tpu_custom_call" | custom-call | flops 2642411520 | bytes 8388608 | tf_op jit(solution)/shard_map/pallas_call | solution.py:189
  63.5 1.9 %collective-permute-start.6 = (bf16[448,640]{1,0:T(8,128)(2,1)S(1)}, bf16[448,640]{1,0:T(8,128)(2,1)S(1)}, u32[]{:S(2)}, u32[]{:S(2)}) collective-permute-start(bf16[448,640]{1,0:T(8,128)(2,1)S(1)} %get-tuple-element.41), channel_id=1, source_target_pairs={{0,65},{1,33},{32,64},{33,96},{64,1},{65,97},{96,0},{97,32},{2,67}... | collective-permute-start | bytes 1720328 | tf_op jit(solution)/shard_map/ppermute | solution.py:47
  65.4 1.4 collective-permute-start.8
  66.8 3.5 %collective-permute-done.11.refs_6_ = bf16[768,384]{1,0:T(8,128)(2,1)S(1)} collective-permute-done((bf16[768,384]{1,0:T(8,128)(2,1)S(1)}, bf16[768,384]{1,0:T(8,128)(2,1)S(1)}, u32[]{:S(2)}, u32[]{:S(2)}) %collective-permute-start.11) | collective-permute-done | bytes 589856 | tf_op jit(solution)/shard_map/ppermute | solution.py:33
  70.3 3.0 %collective-permute-start.12 = (bf16[384,384]{1,0:T(8,128)(2,1)S(1)}, bf16[384,384]{1,0:T(8,128)(2,1)S(1)}, u32[]{:S(2)}, u32[]{:S(2)}) collective-permute-start(bf16[384,384]{1,0:T(8,128)(2,1)S(1)} %slice.8), channel_id=1, source_target_pairs={{0,128},{128,0},{2,130},{130,2},{1,129},{129,1},{3,131},{131,3},{4... | collective-permute-start | bytes 884744 | tf_op jit(solution)/shard_map/ppermute | solution.py:33
  73.4 1.8 %collective-permute-start.13 = (bf16[384,384]{1,0:T(8,128)(2,1)S(1)}, bf16[384,384]{1,0:T(8,128)(2,1)S(1)}, u32[]{:S(2)}, u32[]{:S(2)}) collective-permute-start(bf16[384,384]{1,0:T(8,128)(2,1)S(1)} %slice.9), channel_id=1, source_target_pairs={{0,130},{128,2},{2,128},{130,0},{1,131},{129,3},{3,129},{131,1},{4... | collective-permute-start | bytes 884744 | tf_op jit(solution)/shard_map/ppermute | solution.py:33
  75.2 5.4 %collective-permute-done.6.refs_7_.refs_1_ = bf16[448,640]{1,0:T(8,128)(2,1)S(1)} collective-permute-done((bf16[448,640]{1,0:T(8,128)(2,1)S(1)}, bf16[448,640]{1,0:T(8,128)(2,1)S(1)}, u32[]{:S(2)}, u32[]{:S(2)}) %collective-permute-start.6) | collective-permute-done | bytes 573472 | tf_op jit(solution)/shard_map/ppermute | solution.py:47
  80.6 0.7 collective-permute-start.9
  81.3 4.5 %shard_map.101 = (bf16[448,384]{1,0:T(8,128)(2,1)}, bf16[448,384]{1,0:T(8,128)(2,1)}, bf16[448,384]{1,0:T(8,128)(2,1)}, bf16[448,384]{1,0:T(8,128)(2,1)S(1)}) custom-call(s32[4]{0:T(128)S(1)} %broadcast_select_fusion.refs_0_, bf16[896,1536]{1,0:T(8,128)(2,1)S(1)} %get-tuple-element.36.refs_1_, bf16[768,384]{1,0:T(8,128)(2,1)S(1)} %shard_map.99.refs_2_, ...), custom_call_target="tpu_custom_call" | custom-call | flops 2113929216 | bytes 8388608 | tf_op jit(solution)/shard_map/pallas_call | solution.py:189
  85.9 4.1 %collective-permute-start.14 = (bf16[448,384]{1,0:T(8,128)(2,1)}, bf16[448,384]{1,0:T(8,128)(2,1)S(1)}, u32[]{:S(2)}, u32[]{:S(2)}) collective-permute-start(bf16[448,384]{1,0:T(8,128)(2,1)} %get-tuple-element.46), channel_id=1, source_target_pairs={{0,65},{1,33},{32,64},{33,96},{64,1},{65,97},{96,0},{97,32},{2,67}... | collective-permute-start | bytes 1032200 | tf_op jit(solution)/shard_map/ppermute | solution.py:47
  90.0 2.0 %collective-permute-start.16 = (bf16[448,384]{1,0:T(8,128)(2,1)}, bf16[448,384]{1,0:T(8,128)(2,1)}, u32[]{:S(2)}, u32[]{:S(2)}) collective-permute-start(bf16[448,384]{1,0:T(8,128)(2,1)} %get-tuple-element.48), channel_id=1, source_target_pairs={{0,64},{1,32},{32,65},{33,97},{64,0},{65,96},{96,1},{97,33},{2,66}... | collective-permute-start | bytes 1032200 | tf_op jit(solution)/shard_map/ppermute | solution.py:47
  92.0 0.6 collective-permute-done.8.refs_3_
  92.6 1.4 collective-permute-start.17
  94.1 5.0 %collective-permute-done.14.refs_6_ = bf16[448,384]{1,0:T(8,128)(2,1)S(1)} collective-permute-done((bf16[448,384]{1,0:T(8,128)(2,1)}, bf16[448,384]{1,0:T(8,128)(2,1)S(1)}, u32[]{:S(2)}, u32[]{:S(2)}) %collective-permute-start.14) | collective-permute-done | bytes 344096 | tf_op jit(solution)/shard_map/ppermute | solution.py:47
  99.1 2.4 %collective-permute-done.15.refs_7_ = bf16[448,384]{1,0:T(8,128)(2,1)} collective-permute-done((bf16[448,384]{1,0:T(8,128)(2,1)}, bf16[448,384]{1,0:T(8,128)(2,1)}, u32[]{:S(2)}, u32[]{:S(2)}) %collective-permute-start.15) | collective-permute-done | bytes 344096 | tf_op jit(solution)/shard_map/ppermute | solution.py:47
  101.5 5.6 %collective-permute-done.16.refs_8_ = bf16[448,384]{1,0:T(8,128)(2,1)} collective-permute-done((bf16[448,384]{1,0:T(8,128)(2,1)}, bf16[448,384]{1,0:T(8,128)(2,1)}, u32[]{:S(2)}, u32[]{:S(2)}) %collective-permute-start.16) | collective-permute-done | bytes 344096 | tf_op jit(solution)/shard_map/ppermute | solution.py:47
  107.1 2.7 %shard_map.102 = (f32[8,56,128]{2,1,0:T(8,128)S(1)}, bf16[8,56,128]{2,1,0:T(8,128)(2,1)}, bf16[8,56,128]{2,1,0:T(8,128)(2,1)}, bf16[8,56,128]{2,1,0:T(8,128)(2,1...) custom-call(s32[2]{0:T(128)S(1)} %pad_add_fusion.refs_0_, ...), custom_call_target="tpu_custom_call" | custom-call | tf_op jit(solution)/shard_map/pallas_call | solution.py:237
  109.9 0.7 copy-done.2
  110.5 7.2 %collective-permute-start.18 = (bf16[8,56,128]{2,1,0:T(8,128)(2,1)S(1)}, bf16[8,56,128]{2,1,0:T(8,128)(2,1)S(1)}, u32[]{:S(2)}, u32[]{:S(2)}) collective-permute-start(bf16[8,56,128]{2,1,0:T(8,128)(2,1)S(1)} %get-tuple-element.51), channel_id=1, source_target_pairs={{0,16},{4,20},{8,24},{12,28},{16,0},{20,4},{24,8},{28,12},{1,17},{... | collective-permute-start | bytes 344072 | tf_op jit(solution)/shard_map/ppermute | solution.py:37
  117.8 1.9 %collective-permute-start.19 = (bf16[8,56,128]{2,1,0:T(8,128)(2,1)S(1)}, bf16[8,56,128]{2,1,0:T(8,128)(2,1)S(1)}, u32[]{:S(2)}, u32[]{:S(2)}) collective-permute-start(bf16[8,56,128]{2,1,0:T(8,128)(2,1)S(1)} %get-tuple-element.52), channel_id=1, source_target_pairs={{0,12},{4,16},{8,20},{12,24},{16,28},{20,0},{24,4},{28,8},{1,13},{... | collective-permute-start | bytes 344072 | tf_op jit(solution)/shard_map/ppermute | solution.py:37
  119.7 3.1 %collective-permute-start.20 = (bf16[8,56,128]{2,1,0:T(8,128)(2,1)}, bf16[8,56,128]{2,1,0:T(8,128)(2,1)S(1)}, u32[]{:S(2)}, u32[]{:S(2)}) collective-permute-start(bf16[8,56,128]{2,1,0:T(8,128)(2,1)} %get-tuple-element.53), channel_id=1, source_target_pairs={{0,20},{4,24},{8,28},{12,0},{16,4},{20,8},{24,12},{28,16},{1,21},{... | collective-permute-start | bytes 344072 | tf_op jit(solution)/shard_map/ppermute | solution.py:37
  122.8 1.4 collective-permute-start.21
  124.2 2.7 %collective-permute-start.22 = (bf16[8,56,128]{2,1,0:T(8,128)(2,1)}, bf16[8,56,128]{2,1,0:T(8,128)(2,1)S(1)}, u32[]{:S(2)}, u32[]{:S(2)}) collective-permute-start(bf16[8,56,128]{2,1,0:T(8,128)(2,1)} %get-tuple-element.55), channel_id=1, source_target_pairs={{0,24},{4,28},{8,0},{12,4},{16,8},{20,12},{24,16},{28,20},{1,25},{... | collective-permute-start | bytes 344072 | tf_op jit(solution)/shard_map/ppermute | solution.py:37
  126.9 1.0 collective-permute-start.23
  127.9 4.8 %collective-permute-done.19 = bf16[8,56,128]{2,1,0:T(8,128)(2,1)S(1)} collective-permute-done((bf16[8,56,128]{2,1,0:T(8,128)(2,1)S(1)}, bf16[8,56,128]{2,1,0:T(8,128)(2,1)S(1)}, u32[]{:S(2)}, u32[]{:S(2)}) %collective-permute-start.19) | collective-permute-done | bytes 114720 | tf_op jit(solution)/shard_map/ppermute | solution.py:37
  132.7 0.6 collective-permute-start.24
  133.3 0.8 collective-permute-done.21
  134.1 2.7 %collective-permute-done.22 = bf16[8,56,128]{2,1,0:T(8,128)(2,1)S(1)} collective-permute-done((bf16[8,56,128]{2,1,0:T(8,128)(2,1)}, bf16[8,56,128]{2,1,0:T(8,128)(2,1)S(1)}, u32[]{:S(2)}, u32[]{:S(2)}) %collective-permute-start.22) | collective-permute-done | bytes 114720 | tf_op jit(solution)/shard_map/ppermute | solution.py:37
  136.8 1.9 %collective-permute-done.23 = bf16[8,56,128]{2,1,0:T(8,128)(2,1)S(1)} collective-permute-done((bf16[8,56,128]{2,1,0:T(8,128)(2,1)}, bf16[8,56,128]{2,1,0:T(8,128)(2,1)S(1)}, u32[]{:S(2)}, u32[]{:S(2)}) %collective-permute-start.23) | collective-permute-done | bytes 114720 | tf_op jit(solution)/shard_map/ppermute | solution.py:37
  138.7 0.6 collective-permute-done.24
  139.4 1.7 fusion.3
  141.1 4.8 %all-to-all-start = ((f32[8,56,128]{2,1,0:T(8,128)}), f32[8,56,128]{2,1,0:T(8,128)S(1)}, u32[]{:S(2)}, u32[]{:S(2)}) async-start(f32[8,56,128]{2,1,0:T(8,128)} %get-tuple-element.59), calls=%async_computation | async-start | bytes 458752 | tf_op jit(solution)/shard_map/all_to_all | solution.py:380
  145.9 0.8 select_reduce_fusion
  146.8 0.7 collective-permute-start.29
  147.5 3.3 %collective-permute-start.30 = (bf16[8,56,128]{2,1,0:T(8,128)(2,1)S(1)}, bf16[8,56,128]{2,1,0:T(8,128)(2,1)S(1)}, u32[]{:S(2)}, u32[]{:S(2)}) collective-permute-start(bf16[8,56,128]{2,1,0:T(8,128)(2,1)S(1)} %get-tuple-element.58.refs_0_), channel_id=1, source_target_pairs={{0,64},{32,96},{64,0},{96,32},{1,65},{33,97},{65,1},{97,33},{2,66}... | collective-permute-start | bytes 344072 | tf_op jit(solution)/shard_map/ppermute | solution.py:37
  150.7 0.7 collective-permute-start.31
  152.0 2.9 %collective-permute-done.29.refs_1_ = bf16[8,56,128]{2,1,0:T(8,128)(2,1)S(1)} collective-permute-done((bf16[8,56,128]{2,1,0:T(8,128)(2,1)S(1)}, bf16[8,56,128]{2,1,0:T(8,128)(2,1)S(1)}, u32[]{:S(2)}, u32[]{:S(2)}) %collective-permute-start.29) | collective-permute-done | bytes 114720 | tf_op jit(solution)/shard_map/ppermute | solution.py:37
  155.6 0.6 copy-done.10
  156.3 2.2 %shard_map.104 = bf16[8,56,128]{2,1,0:T(8,128)(2,1)} custom-call(s32[8]{0:T(128)} %fusion.place, bf16[8,56,128]{2,1,0:T(8,128)(2,1)} %copy-done.7, bf16[8,56,128]{2,1,0:T(8,128)(2,1)} %copy-done.8, bf16[8,56,128]{2,1,0:T(8,128)(2,1)} %copy-done.9, bf16[8,56,128]{2,1,0:T(8,128)(2,1)} %copy-done.10), custom_call_target="tpu_custom_call" | custom-call | tf_op jit(solution)/shard_map/pallas_call | solution.py:260
  158.5 7.1 %all-to-all-start.1 = ((bf16[8,56,128]{2,1,0:T(8,128)(2,1)}), bf16[8,56,128]{2,1,0:T(8,128)(2,1)S(1)}, u32[]{:S(2)}, u32[]{:S(2)}) async-start(bf16[8,56,128]{2,1,0:T(8,128)(2,1)} %shard_map.104), calls=%async_computation.1 | async-start | bytes 229376 | tf_op jit(solution)/shard_map/all_to_all | solution.py:378
  166.3 1.2 collective-permute-done.25
  168.0 1.9 %collective-permute-start.27 = (f32[128,128]{1,0:T(8,128)S(1)}, f32[128,128]{1,0:T(8,128)S(1)}, u32[]{:S(2)}, u32[]{:S(2)}) collective-permute-start(f32[128,128]{1,0:T(8,128)S(1)} %add.84.refs_1_), channel_id=1, source_target_pairs={{0,128},{128,0},{2,130},{130,2},{1,129},{129,1},{3,131},{131,3},{4... | collective-permute-start | bytes 196616 | tf_op jit(solution)/shard_map/ppermute | solution.py:33
  169.9 1.8 %collective-permute-start.28 = (f32[128,128]{1,0:T(8,128)S(1)}, f32[128,128]{1,0:T(8,128)S(1)}, u32[]{:S(2)}, u32[]{:S(2)}) collective-permute-start(f32[128,128]{1,0:T(8,128)S(1)} %add.84.refs_1_), channel_id=1, source_target_pairs={{0,130},{128,2},{2,128},{130,0},{1,131},{129,3},{3,129},{131,1},{4... | collective-permute-start | bytes 196616 | tf_op jit(solution)/shard_map/ppermute | solution.py:33
  171.7 2.8 %all-to-all-done.1 = bf16[8,56,128]{2,1,0:T(8,128)(2,1)S(1)} async-done(((bf16[8,56,128]{2,1,0:T(8,128)(2,1)}), bf16[8,56,128]{2,1,0:T(8,128)(2,1)S(1)}, u32[]{:S(2)}, u32[]{:S(2)}) %all-to-all-start.1) | async-done | bytes 114720 | tf_op jit(solution)/shard_map/all_to_all | solution.py:378
  174.5 0.7 convert_bitcast_fusion
  175.2 2.2 %shard_map.103 = bf16[448,128]{1,0:T(8,128)(2,1)} custom-call(f32[448,128]{1,0:T(8,128)S(1)} %bitcast.24, f32[128,128]{1,0:T(8,128)S(1)} %add.84.refs_1_, f32[128,128]{1,0:T(8,128)S(1)} %collective-permute-done.26.refs_2_, f32[128,128]{1,0:T(8,128)S(1)} %collective-permute-done.27.refs_3_, f32[128,128]{1,0:T(8,128)S(1)} %collective-permute-done.28.refs_4_), custom_call_target="tpu_custom_call" | custom-call | tf_op jit(solution)/shard_map/pallas_call | solution.py:292
  (57 shorter events, 2.8 us)
Async XLA Ops:
  0.6 1.9 %copy-start = (bf16[1536,1024]{1,0:T(8,128)(2,1)S(1)}, bf16[1536,1024]{1,0:T(8,128)(2,1)}, u32[]{:S(2)}) copy-start(bf16[1536,1024]{1,0:T(8,128)(2,1)} %refs_1_.3) | copy-start | bytes 9437188
  2.5 0.7 copy-start.3
  3.2 6.8 %copy-start.11 = (f32[1536]{0:T(1024)S(1)}, f32[1536]{0:T(1024)}, u32[]{:S(2)}) copy-start(f32[1536]{0:T(1024)} %param.10) | copy-start | bytes 18436
  3.2 6.9 %copy-start.12 = (f32[1536]{0:T(1024)S(1)}, f32[1536]{0:T(1024)}, u32[]{:S(2)}) copy-start(f32[1536]{0:T(1024)} %param.11) | copy-start | bytes 18436
  3.2 6.9 %copy-start.13 = (f32[1536]{0:T(1024)S(1)}, f32[1536]{0:T(1024)}, u32[]{:S(2)}) copy-start(f32[1536]{0:T(1024)} %param.12) | copy-start | bytes 18436
  3.2 7.0 %copy-start.4 = (s32[1,768]{1,0:T(1,128)S(1)}, s32[1,768]{1,0:T(1,128)}, u32[]{:S(2)}) copy-start(s32[1,768]{1,0:T(1,128)} %refs_0_.3) | copy-start | bytes 9220
  3.2 7.0 %copy-start.5 = (bf16[1536,2,448]{0,2,1:T(8,128)(2,1)S(1)}, bf16[1536,2,448]{0,2,1:T(8,128)(2,1)}, u32[]{:S(2)}) copy-start(bf16[1536,2,448]{0,2,1:T(8,128)(2,1)} %param.9) | copy-start | bytes 8257540
  6.5 23.8 %collective-permute-start = (bf16[768,640]{1,0:T(8,128)(2,1)}, bf16[768,640]{1,0:T(8,128)(2,1)}, u32[]{:S(2)}, u32[]{:S(2)}) collective-permute-start(bf16[768,640]{1,0:T(8,128)(2,1)} %shard_map.95.refs_4_), channel_id=1, source_target_pairs={{0,128},{128,0},{2,130},{130,2},{1,129},{129,1},{3,131},{131,3},{4... | collective-permute-start | bytes 2949128 | tf_op jit(solution)/shard_map/ppermute | solution.py:33
  8.7 22.5 %collective-permute-start.1 = (bf16[768,640]{1,0:T(8,128)(2,1)}, bf16[768,640]{1,0:T(8,128)(2,1)}, u32[]{:S(2)}, u32[]{:S(2)}) collective-permute-start(bf16[768,640]{1,0:T(8,128)(2,1)} %shard_map.95.refs_4_), channel_id=1, source_target_pairs={{0,130},{128,2},{2,128},{130,0},{1,131},{129,3},{3,129},{131,1},{4... | collective-permute-start | bytes 2949128 | tf_op jit(solution)/shard_map/ppermute | solution.py:33
  10.1 2.9 %copy-start.6 = (bf16[1536,2,448]{0,2,1:T(8,128)(2,1)S(1)}, bf16[1536,2,448]{0,2,1:T(8,128)(2,1)}, u32[]{:S(2)}) copy-start(bf16[1536,2,448]{0,2,1:T(8,128)(2,1)} %param.9) | copy-start | bytes 8257540
  13.0 34.5 %copy-start.1 = (bf16[1536,1024]{1,0:T(8,128)(2,1)S(1)}, bf16[1536,1024]{1,0:T(8,128)(2,1)}, u32[]{:S(2)}) copy-start(bf16[1536,1024]{1,0:T(8,128)(2,1)} %refs_1_.3) | copy-start | bytes 9437188
  31.2 16.3 %collective-permute-start.2 = (bf16[448,768]{1,0:T(8,128)(2,1)S(1)}, bf16[448,768]{1,0:T(8,128)(2,1)}, u32[]{:S(2)}, u32[]{:S(2)}) collective-permute-start(bf16[448,768]{1,0:T(8,128)(2,1)S(1)} %shard_map.96), channel_id=1, source_target_pairs={{0,128},{128,0},{2,130},{130,2},{1,129},{129,1},{3,131},{131,3},{4... | collective-permute-start | bytes 2064392 | tf_op jit(solution)/shard_map/ppermute | solution.py:33
  33.3 22.2 %collective-permute-start.5 = (bf16[768,640]{1,0:T(8,128)(2,1)}, bf16[768,640]{1,0:T(8,128)(2,1)}, u32[]{:S(2)}, u32[]{:S(2)}) collective-permute-start(bf16[768,640]{1,0:T(8,128)(2,1)} %collective-permute-done.refs_5_), channel_id=1, source_target_pairs={{0,130},{128,2},{2,128},{130,0},{1,131},{129,3},{3,129},{131,1},{4... | collective-permute-start | bytes 2949128 | tf_op jit(solution)/shard_map/ppermute | solution.py:33
  34.9 14.3 %collective-permute-start.3 = (bf16[448,768]{1,0:T(8,128)(2,1)}, bf16[448,768]{1,0:T(8,128)(2,1)}, u32[]{:S(2)}, u32[]{:S(2)}) collective-permute-start(bf16[448,768]{1,0:T(8,128)(2,1)} %shard_map.97.refs_0_), channel_id=1, source_target_pairs={{0,1},{1,0},{2,3},{3,2},{4,5},{5,4},{6,7},{7,6},{8,9},{9,8},{10,11... | collective-permute-start | bytes 2064392 | tf_op jit(solution)/shard_map/ppermute | solution.py:37
  47.5 2.5 %collective-permute-start.4 = (bf16[448,768]{1,0:T(8,128)(2,1)}, bf16[448,768]{1,0:T(8,128)(2,1)}, u32[]{:S(2)}, u32[]{:S(2)}) collective-permute-start(bf16[448,768]{1,0:T(8,128)(2,1)} %collective-permute-done.2.refs_1_), channel_id=1, source_target_pairs={{0,1},{1,0},{2,3},{3,2},{4,5},{5,4},{6,7},{7,6},{8,9},{9,8},{10,11... | collective-permute-start | bytes 2064392 | tf_op jit(solution)/shard_map/ppermute | solution.py:37
  55.5 14.8 %collective-permute-start.11 = (bf16[768,384]{1,0:T(8,128)(2,1)S(1)}, bf16[768,384]{1,0:T(8,128)(2,1)S(1)}, u32[]{:S(2)}, u32[]{:S(2)}) collective-permute-start(bf16[768,384]{1,0:T(8,128)(2,1)S(1)} %shard_map.99.refs_2_), channel_id=1, source_target_pairs={{0,130},{128,2},{2,128},{130,0},{1,131},{129,3},{3,129},{131,1},{4... | collective-permute-start | bytes 1769480 | tf_op jit(solution)/shard_map/ppermute | solution.py:33
  57.2 16.1 %collective-permute-start.10 = (bf16[768,384]{1,0:T(8,128)(2,1)S(1)}, bf16[768,384]{1,0:T(8,128)(2,1)S(1)}, u32[]{:S(2)}, u32[]{:S(2)}) collective-permute-start(bf16[768,384]{1,0:T(8,128)(2,1)S(1)} %shard_map.99.refs_2_), channel_id=1, source_target_pairs={{0,128},{128,0},{2,130},{130,2},{1,129},{129,1},{3,131},{131,3},{4... | collective-permute-start | bytes 1769480 | tf_op jit(solution)/shard_map/ppermute | solution.py:33
  63.5 17.1 %collective-permute-start.6 = (bf16[448,640]{1,0:T(8,128)(2,1)S(1)}, bf16[448,640]{1,0:T(8,128)(2,1)S(1)}, u32[]{:S(2)}, u32[]{:S(2)}) collective-permute-start(bf16[448,640]{1,0:T(8,128)(2,1)S(1)} %get-tuple-element.41), channel_id=1, source_target_pairs={{0,65},{1,33},{32,64},{33,96},{64,1},{65,97},{96,0},{97,32},{2,67}... | collective-permute-start | bytes 1720328 | tf_op jit(solution)/shard_map/ppermute | solution.py:47
  65.4 24.6 %collective-permute-start.7 = (bf16[448,640]{1,0:T(8,128)(2,1)S(1)}, bf16[448,640]{1,0:T(8,128)(2,1)S(1)}, u32[]{:S(2)}, u32[]{:S(2)}) collective-permute-start(bf16[448,640]{1,0:T(8,128)(2,1)S(1)} %get-tuple-element.42), channel_id=1, source_target_pairs={{0,1},{1,97},{32,0},{33,32},{64,65},{65,33},{96,64},{97,96},{2,3},... | collective-permute-start | bytes 1720328 | tf_op jit(solution)/shard_map/ppermute | solution.py:47
  65.4 27.2 %collective-permute-start.8 = (bf16[448,640]{1,0:T(8,128)(2,1)S(1)}, bf16[448,640]{1,0:T(8,128)(2,1)S(1)}, u32[]{:S(2)}, u32[]{:S(2)}) collective-permute-start(bf16[448,640]{1,0:T(8,128)(2,1)S(1)} %get-tuple-element.43), channel_id=1, source_target_pairs={{0,64},{1,32},{32,65},{33,97},{64,0},{65,96},{96,1},{97,33},{2,66}... | collective-permute-start | bytes 1720328 | tf_op jit(solution)/shard_map/ppermute | solution.py:47
  70.3 11.0 %collective-permute-start.12 = (bf16[384,384]{1,0:T(8,128)(2,1)S(1)}, bf16[384,384]{1,0:T(8,128)(2,1)S(1)}, u32[]{:S(2)}, u32[]{:S(2)}) collective-permute-start(bf16[384,384]{1,0:T(8,128)(2,1)S(1)} %slice.8), channel_id=1, source_target_pairs={{0,128},{128,0},{2,130},{130,2},{1,129},{129,1},{3,131},{131,3},{4... | collective-permute-start | bytes 884744 | tf_op jit(solution)/shard_map/ppermute | solution.py:33
  73.4 8.0 %collective-permute-start.13 = (bf16[384,384]{1,0:T(8,128)(2,1)S(1)}, bf16[384,384]{1,0:T(8,128)(2,1)S(1)}, u32[]{:S(2)}, u32[]{:S(2)}) collective-permute-start(bf16[384,384]{1,0:T(8,128)(2,1)S(1)} %slice.9), channel_id=1, source_target_pairs={{0,130},{128,2},{2,128},{130,0},{1,131},{129,3},{3,129},{131,1},{4... | collective-permute-start | bytes 884744 | tf_op jit(solution)/shard_map/ppermute | solution.py:33
  80.6 13.5 %collective-permute-start.9 = (bf16[448,640]{1,0:T(8,128)(2,1)S(1)}, bf16[448,640]{1,0:T(8,128)(2,1)S(1)}, u32[]{:S(2)}, u32[]{:S(2)}) collective-permute-start(bf16[448,640]{1,0:T(8,128)(2,1)S(1)} %get-tuple-element.44.refs_5_), channel_id=1, source_target_pairs={{1,96},{32,1},{65,32},{96,65},{3,98},{34,3},{67,34},{98,67},{5,100... | collective-permute-start | bytes 1720328 | tf_op jit(solution)/shard_map/ppermute | solution.py:47
  85.9 13.2 %collective-permute-start.14 = (bf16[448,384]{1,0:T(8,128)(2,1)}, bf16[448,384]{1,0:T(8,128)(2,1)S(1)}, u32[]{:S(2)}, u32[]{:S(2)}) collective-permute-start(bf16[448,384]{1,0:T(8,128)(2,1)} %get-tuple-element.46), channel_id=1, source_target_pairs={{0,65},{1,33},{32,64},{33,96},{64,1},{65,97},{96,0},{97,32},{2,67}... | collective-permute-start | bytes 1032200 | tf_op jit(solution)/shard_map/ppermute | solution.py:47
  90.0 11.5 %collective-permute-start.15 = (bf16[448,384]{1,0:T(8,128)(2,1)}, bf16[448,384]{1,0:T(8,128)(2,1)}, u32[]{:S(2)}, u32[]{:S(2)}) collective-permute-start(bf16[448,384]{1,0:T(8,128)(2,1)} %get-tuple-element.47), channel_id=1, source_target_pairs={{0,1},{1,97},{32,0},{33,32},{64,65},{65,33},{96,64},{97,96},{2,3},... | collective-permute-start | bytes 1032200 | tf_op jit(solution)/shard_map/ppermute | solution.py:47
  90.0 17.1 %collective-permute-start.16 = (bf16[448,384]{1,0:T(8,128)(2,1)}, bf16[448,384]{1,0:T(8,128)(2,1)}, u32[]{:S(2)}, u32[]{:S(2)}) collective-permute-start(bf16[448,384]{1,0:T(8,128)(2,1)} %get-tuple-element.48), channel_id=1, source_target_pairs={{0,64},{1,32},{32,65},{33,97},{64,0},{65,96},{96,1},{97,33},{2,66}... | collective-permute-start | bytes 1032200 | tf_op jit(solution)/shard_map/ppermute | solution.py:47
  92.6 14.5 %collective-permute-start.17 = (bf16[448,384]{1,0:T(8,128)(2,1)S(1)}, bf16[448,384]{1,0:T(8,128)(2,1)}, u32[]{:S(2)}, u32[]{:S(2)}) collective-permute-start(bf16[448,384]{1,0:T(8,128)(2,1)S(1)} %get-tuple-element.49.refs_10_), channel_id=1, source_target_pairs={{1,96},{32,1},{65,32},{96,65},{3,98},{34,3},{67,34},{98,67},{5,100... | collective-permute-start | bytes 1032200 | tf_op jit(solution)/shard_map/ppermute | solution.py:47
  109.9 0.7 copy-start.2
  110.5 16.4 %collective-permute-start.18 = (bf16[8,56,128]{2,1,0:T(8,128)(2,1)S(1)}, bf16[8,56,128]{2,1,0:T(8,128)(2,1)S(1)}, u32[]{:S(2)}, u32[]{:S(2)}) collective-permute-start(bf16[8,56,128]{2,1,0:T(8,128)(2,1)S(1)} %get-tuple-element.51), channel_id=1, source_target_pairs={{0,16},{4,20},{8,24},{12,28},{16,0},{20,4},{24,8},{28,12},{1,17},{... | collective-permute-start | bytes 344072 | tf_op jit(solution)/shard_map/ppermute | solution.py:37
  117.8 14.9 %collective-permute-start.19 = (bf16[8,56,128]{2,1,0:T(8,128)(2,1)S(1)}, bf16[8,56,128]{2,1,0:T(8,128)(2,1)S(1)}, u32[]{:S(2)}, u32[]{:S(2)}) collective-permute-start(bf16[8,56,128]{2,1,0:T(8,128)(2,1)S(1)} %get-tuple-element.52), channel_id=1, source_target_pairs={{0,12},{4,16},{8,20},{12,24},{16,28},{20,0},{24,4},{28,8},{1,13},{... | collective-permute-start | bytes 344072 | tf_op jit(solution)/shard_map/ppermute | solution.py:37
  119.7 13.6 %collective-permute-start.20 = (bf16[8,56,128]{2,1,0:T(8,128)(2,1)}, bf16[8,56,128]{2,1,0:T(8,128)(2,1)S(1)}, u32[]{:S(2)}, u32[]{:S(2)}) collective-permute-start(bf16[8,56,128]{2,1,0:T(8,128)(2,1)} %get-tuple-element.53), channel_id=1, source_target_pairs={{0,20},{4,24},{8,28},{12,0},{16,4},{20,8},{24,12},{28,16},{1,21},{... | collective-permute-start | bytes 344072 | tf_op jit(solution)/shard_map/ppermute | solution.py:37
  122.8 11.3 %collective-permute-start.21 = (bf16[8,56,128]{2,1,0:T(8,128)(2,1)}, bf16[8,56,128]{2,1,0:T(8,128)(2,1)S(1)}, u32[]{:S(2)}, u32[]{:S(2)}) collective-permute-start(bf16[8,56,128]{2,1,0:T(8,128)(2,1)} %get-tuple-element.54), channel_id=1, source_target_pairs={{0,8},{4,12},{8,16},{12,20},{16,24},{20,28},{24,0},{28,4},{1,9},{5... | collective-permute-start | bytes 344072 | tf_op jit(solution)/shard_map/ppermute | solution.py:37
  124.2 12.6 %collective-permute-start.22 = (bf16[8,56,128]{2,1,0:T(8,128)(2,1)}, bf16[8,56,128]{2,1,0:T(8,128)(2,1)S(1)}, u32[]{:S(2)}, u32[]{:S(2)}) collective-permute-start(bf16[8,56,128]{2,1,0:T(8,128)(2,1)} %get-tuple-element.55), channel_id=1, source_target_pairs={{0,24},{4,28},{8,0},{12,4},{16,8},{20,12},{24,16},{28,20},{1,25},{... | collective-permute-start | bytes 344072 | tf_op jit(solution)/shard_map/ppermute | solution.py:37
  126.9 11.8 %collective-permute-start.23 = (bf16[8,56,128]{2,1,0:T(8,128)(2,1)}, bf16[8,56,128]{2,1,0:T(8,128)(2,1)S(1)}, u32[]{:S(2)}, u32[]{:S(2)}) collective-permute-start(bf16[8,56,128]{2,1,0:T(8,128)(2,1)} %get-tuple-element.56), channel_id=1, source_target_pairs={{0,4},{4,8},{8,12},{12,16},{16,20},{20,24},{24,28},{28,0},{1,5},{5... | collective-permute-start | bytes 344072 | tf_op jit(solution)/shard_map/ppermute | solution.py:37
  132.7 6.7 %collective-permute-start.24 = (bf16[8,56,128]{2,1,0:T(8,128)(2,1)}, bf16[8,56,128]{2,1,0:T(8,128)(2,1)S(1)}, u32[]{:S(2)}, u32[]{:S(2)}) collective-permute-start(bf16[8,56,128]{2,1,0:T(8,128)(2,1)} %get-tuple-element.57), channel_id=1, source_target_pairs={{0,28},{4,0},{8,4},{12,8},{16,12},{20,16},{24,20},{28,24},{1,29},{... | collective-permute-start | bytes 344072 | tf_op jit(solution)/shard_map/ppermute | solution.py:37
  141.1 14.4 %copy-start.7 = (bf16[8,56,128]{2,1,0:T(8,128)(2,1)}, bf16[8,56,128]{2,1,0:T(8,128)(2,1)S(1)}, u32[]{:S(2)}) copy-start(bf16[8,56,128]{2,1,0:T(8,128)(2,1)S(1)} %get-tuple-element.58.refs_0_) | copy-start | bytes 344068
  141.1 17.4 %all-to-all-start = ((f32[8,56,128]{2,1,0:T(8,128)}), f32[8,56,128]{2,1,0:T(8,128)S(1)}, u32[]{:S(2)}, u32[]{:S(2)}) async-start(f32[8,56,128]{2,1,0:T(8,128)} %get-tuple-element.59), calls=%async_computation | async-start | bytes 458752 | tf_op jit(solution)/shard_map/all_to_all | solution.py:380
  146.8 8.1 %collective-permute-start.29 = (bf16[8,56,128]{2,1,0:T(8,128)(2,1)S(1)}, bf16[8,56,128]{2,1,0:T(8,128)(2,1)S(1)}, u32[]{:S(2)}, u32[]{:S(2)}) collective-permute-start(bf16[8,56,128]{2,1,0:T(8,128)(2,1)S(1)} %get-tuple-element.58.refs_0_), channel_id=1, source_target_pairs={{0,32},{32,64},{64,96},{96,0},{1,33},{33,65},{65,97},{97,1},{2,34}... | collective-permute-start | bytes 344072 | tf_op jit(solution)/shard_map/ppermute | solution.py:37
  147.5 7.5 %collective-permute-start.30 = (bf16[8,56,128]{2,1,0:T(8,128)(2,1)S(1)}, bf16[8,56,128]{2,1,0:T(8,128)(2,1)S(1)}, u32[]{:S(2)}, u32[]{:S(2)}) collective-permute-start(bf16[8,56,128]{2,1,0:T(8,128)(2,1)S(1)} %get-tuple-element.58.refs_0_), channel_id=1, source_target_pairs={{0,64},{32,96},{64,0},{96,32},{1,65},{33,97},{65,1},{97,33},{2,66}... | collective-permute-start | bytes 344072 | tf_op jit(solution)/shard_map/ppermute | solution.py:37
  150.7 4.8 %collective-permute-start.31 = (bf16[8,56,128]{2,1,0:T(8,128)(2,1)S(1)}, bf16[8,56,128]{2,1,0:T(8,128)(2,1)S(1)}, u32[]{:S(2)}, u32[]{:S(2)}) collective-permute-start(bf16[8,56,128]{2,1,0:T(8,128)(2,1)S(1)} %get-tuple-element.58.refs_0_), channel_id=1, source_target_pairs={{0,96},{32,0},{64,32},{96,64},{1,97},{33,1},{65,33},{97,65},{2,98}... | collective-permute-start | bytes 344072 | tf_op jit(solution)/shard_map/ppermute | solution.py:37
  154.9 0.6 copy-start.8
  154.9 0.7 copy-start.9
  155.6 0.6 copy-start.10
  158.5 16.0 %all-to-all-start.1 = ((bf16[8,56,128]{2,1,0:T(8,128)(2,1)}), bf16[8,56,128]{2,1,0:T(8,128)(2,1)S(1)}, u32[]{:S(2)}, u32[]{:S(2)}) async-start(bf16[8,56,128]{2,1,0:T(8,128)(2,1)} %shard_map.104), calls=%async_computation.1 | async-start | bytes 229376 | tf_op jit(solution)/shard_map/all_to_all | solution.py:378
  166.2 1.3 collective-permute-start.25
  167.6 7.7 %collective-permute-start.26 = (f32[128,128]{1,0:T(8,128)S(1)}, f32[128,128]{1,0:T(8,128)S(1)}, u32[]{:S(2)}, u32[]{:S(2)}) collective-permute-start(f32[128,128]{1,0:T(8,128)S(1)} %add.84.refs_1_), channel_id=1, source_target_pairs={{0,2},{128,130},{2,0},{130,128},{1,3},{129,131},{3,1},{131,129},{4... | collective-permute-start | bytes 196616 | tf_op jit(solution)/shard_map/ppermute | solution.py:33
  168.0 7.2 %collective-permute-start.27 = (f32[128,128]{1,0:T(8,128)S(1)}, f32[128,128]{1,0:T(8,128)S(1)}, u32[]{:S(2)}, u32[]{:S(2)}) collective-permute-start(f32[128,128]{1,0:T(8,128)S(1)} %add.84.refs_1_), channel_id=1, source_target_pairs={{0,128},{128,0},{2,130},{130,2},{1,129},{129,1},{3,131},{131,3},{4... | collective-permute-start | bytes 196616 | tf_op jit(solution)/shard_map/ppermute | solution.py:33
  169.9 5.3 %collective-permute-start.28 = (f32[128,128]{1,0:T(8,128)S(1)}, f32[128,128]{1,0:T(8,128)S(1)}, u32[]{:S(2)}, u32[]{:S(2)}) collective-permute-start(f32[128,128]{1,0:T(8,128)S(1)} %add.84.refs_1_), channel_id=1, source_target_pairs={{0,130},{128,2},{2,128},{130,0},{1,131},{129,3},{3,129},{131,1},{4... | collective-permute-start | bytes 196616 | tf_op jit(solution)/shard_map/ppermute | solution.py:33

commit v6 on v5

--- a/solution.py
+++ b/solution.py
@@ -118,6 +118,16 @@
     )(jnp.stack([half, tally]).astype(jnp.int32), kept, benefit, present, behaviour, adjoint)
 
 
+def slots_of():
+    x, core, yh = lax.axis_index("x"), lax.axis_index("c"), lax.axis_index("yh")
+    odd = lax.rem(x + core, 2)
+    near = jnp.where(lax.div(lax.rem(x + odd, X), 2) == yh, 0, 2)
+    far = 2 - near
+    odd_slots = (near, far, near + 1, far + 1)
+    even_slots = (far + 1, near + 1, far, near)
+    return [jnp.where(odd == 1, a, b) for a, b in zip(odd_slots, even_slots)]
+
+
 def dots(s_all, groups):
     cap = s_all.shape[1] // len(groups)
     value = None
@@ -159,7 +169,7 @@
     )(*s_list, own, e1)
 
 
-def terms_kernel(counts, plan, s_all, *refs):
+def terms_kernel(counts, s_all, *refs):
     total, out_refs = refs[-1], refs[-5:-1]
     q = out_refs[0].shape[0]
     at = 0
@@ -176,11 +186,11 @@
     for chunk, value in enumerate(chunks):
         for side in range(2):
             total[2 * chunk + side] = value[side * q : (side + 1) * q]
-    for slot, out_ref in enumerate(out_refs):
-        out_ref[...] = total[plan[slot]]
-
-
-def terms_of(plan, s_all, near, far, after=()):
+    for slot, out_ref in zip(slots_of(), out_refs):
+        out_ref[...] = total[slot]
+
+
+def terms_of(s_all, near, far, after=()):
     q, cols = s_all.shape[0] // 2, far[0][0].shape[1]
     groups = (*near, *far)
     counts = (tuple(len(group) for group in near), tuple(len(group) for group in far))
@@ -188,8 +198,7 @@
     full = pl.BlockSpec(memory_space=pltpu.VMEM)
     return pl.pallas_call(
         lambda *refs: terms_kernel(counts, *refs),
-        in_specs=[pl.BlockSpec(memory_space=pltpu.SMEM)]
-        + [full] * (1 + len(values))
+        in_specs=[full] * (1 + len(values))
         + [pl.BlockSpec(memory_space=pl.ANY)] * len(after),
         out_specs=[full] * 4,
         scratch_shapes=[pltpu.VMEM((4, q, cols), jnp.bfloat16)],
@@ -200,10 +209,12 @@
             bytes_accessed=8 * 2**20,
             transcendentals=0,
         ),
-    )(plan, s_all, *values, *after)
-
-
-def rows_kernel(piece_count, plan, *refs):
+    )(s_all, *values, *after)
+
+
+def rows_kernel(piece_count, *refs):
+    odd = lax.rem(lax.axis_index("x") + lax.axis_index("c"), 2)
+    z = lax.axis_index("z")
     ins, outs, mine = refs[: 5 * piece_count], refs[5 * piece_count : -1], refs[-1]
     start = 0
     for piece in range(piece_count):
@@ -214,35 +225,35 @@
         for ref in got[1:]:
             total = total + ref[...].astype(jnp.float32)
 
-        @pl.when(plan[0] == 1)
+        @pl.when(odd == 1)
         def _(total=total, last=last, columns=columns):
             mine[:, columns] = total + last[...].astype(jnp.float32)
 
-        @pl.when(plan[0] == 0)
+        @pl.when(odd == 0)
         def _(total=total, kept=kept, columns=columns):
             mine[:, columns] = total + kept[...].astype(jnp.float32)
 
     for step, out in enumerate(outs):
         heads, rows, head = out.shape
-        at = pl.multiple_of(lax.rem(plan[1] + step, Z) * rows, 8)
+        at = pl.multiple_of(lax.rem(z + step, Z) * rows, 8)
         for j in range(heads):
             out[j] = mine[pl.ds(at, rows), j * head : (j + 1) * head].astype(out.dtype)
 
 
-def row_blocks(plan, inputs):
+def row_blocks(inputs):
     q = inputs[0].shape[0]
     cols = sum(t.shape[1] for t in inputs[::5])
     shape = (Z, q // Z, cols // Z)
     full = pl.BlockSpec(memory_space=pltpu.VMEM)
     return pl.pallas_call(
         lambda *refs: rows_kernel(len(inputs) // 5, *refs),
-        in_specs=[pl.BlockSpec(memory_space=pltpu.SMEM)] + [full] * len(inputs),
+        in_specs=[full] * len(inputs),
         out_specs=[full] * Z,
         out_shape=[jax.ShapeDtypeStruct(shape, jnp.float32)]
         + [jax.ShapeDtypeStruct(shape, jnp.bfloat16)] * (Z - 1),
         scratch_shapes=[pltpu.VMEM((q, cols), jnp.float32)],
         compiler_params=pltpu.CompilerParams(vmem_limit_bytes=16 * 2**20),
-    )(plan, *inputs)
+    )(*inputs)
 
 
 def choose_kernel(place, *refs):
@@ -324,15 +335,6 @@
     s_send = scaled_half(1 - yl, tallies[0], kept, *rows_of, adjoint)
     s_keep = scaled_half(yl, tallies[0], kept, *rows_of, adjoint)
 
-    odd = (x + core) % 2
-    near = jnp.where((x + odd) % X // 2 == yh, 0, 2)
-    far = 2 - near
-    plan = jnp.where(
-        odd == 1,
-        jnp.stack([near, far, near + 1, far + 1]),
-        jnp.stack([far + 1, near + 1, far, near]),
-    ).astype(jnp.int32)
-
     def over_x(terms):
         return [
             over_xc(terms[0], 1, 0, 2, 1),
@@ -351,17 +353,17 @@
     near_product, s_all = near_terms(s_list, own[0], e1)
     opposite, near_product, second = barrier((opposite, near_product, own[1]))
     f1, f3 = over_y(second, 1), over_y(second, 3)
-    first_terms = terms_of(plan, s_all, [[near_product]], [[opposite], [e3]])
+    first_terms = terms_of(s_all, [[near_product]], [[opposite], [e3]])
     first_sums = over_x(first_terms)
     cut = second.shape[0] // 2
     fa, fb = over_y(f3[:cut], 1), over_y(f1[cut:], 3)
     second_terms = terms_of(
-        plan, s_all, [[second], [f1]], [[fa, fb], [f3]], first_sums[:1]
+        s_all, [[second], [f1]], [[fa, fb], [f3]], first_sums[:1]
     )
     second_sums = over_x(second_terms)
 
     head = mixer_vectors.shape[1] // Z
-    parts = row_blocks(jnp.stack([odd, z]).astype(jnp.int32), first_sums + second_sums)
+    parts = row_blocks(first_sums + second_sums)
     exact = parts[0]
     for got in [shift(parts[d], "z", Z, d) for d in (4, 3, 5, 2, 6, 1, 7)]:
         exact = exact + got.astype(f32)

time: 178 us -> 173 us (0.972)
  Pallas kernels: 31.9 us -> 26.7 us
  waiting for transfers between devices: 69.7 us -> 73.1 us
  other arithmetic: 4.12 us -> 2.33 us
    pallas_call x1, Pallas kernels: 2.74 us -> 0.77 us  [row_blocks(): pl.pallas_call(lambda *refs: rows_kernel(len(inputs) // 5, *refs), in_spe...]
    unnamed x28 -> x26, local copies, waits for them, and re-layouts: 4.02 us -> 3.35 us
  transfers between devices with their start and end apart: 34 -> 34, of which waited for: 20 -> 19; matrix products, arithmetic and copies ran while one was open for 2% -> 1% of each run, Pallas kernels for 13% -> 12%
where the time goes in v6:
time: 173 us
  waiting for transfers between devices  73.1 us (42%)
  starting transfers between devices  64.9 us (38%)
  Pallas kernels  26.7 us (15%)
  local copies, waits for them, and re-layouts  3.43 us (2%)
  other arithmetic  2.33 us (1%)
    ppermute x11, waiting for transfers between devices, over_y(): return lax.ppermute(value, ('yl', 'yh'), ring_pairs(flip))  32.5 us
    ppermute x13, starting transfers between devices, shift(): lax.ppermute(value, axis, [(i, (i + step) % size) for i in range(size)])  22.3 us
    ppermute x8, waiting for transfers between devices, over_xc(): return lax.ppermute(value, ('x', 'c'), pairs)  19.7 us
    ppermute x11, starting transfers between devices, over_y(): return lax.ppermute(value, ('yl', 'yh'), ring_pairs(flip))  19.4 us
    ppermute x13, waiting for transfers between devices, shift(): lax.ppermute(value, axis, [(i, (i + step) % size) for i in range(size)])  18.1 us
    ppermute x8, starting transfers between devices, over_xc(): return lax.ppermute(value, ('x', 'c'), pairs)  11.9 us
    pallas_call x2, Pallas kernels, terms_of(): pl.pallas_call(lambda *refs: terms_kernel(counts, *refs), in_specs=[full]...  7.02 us
    all_to_all x1, starting transfers between devices, on_device(): arrived = lax.all_to_all(chosen, 'z', 0, 0, tiled=True).reshape(q, head)  6.92 us
  transfers between devices with their start and end apart: 34, of which 19 were waited for; matrix products, arithmetic and copies ran while one was open for 1% of the time, Pallas kernels for 12%

profile of v6, /device:TPU:8, one launch (start us, length us, event | category | flops | bytes accessed | tf_op | source)
XLA Modules:
  0.0 172.6 jit_solution(5447459369692393734)
XLA Ops:
  0.6 1.9 %copy-done = bf16[1536,1024]{1,0:T(8,128)(2,1)S(1)} copy-done((bf16[1536,1024]{1,0:T(8,128)(2,1)S(1)}, bf16[1536,1024]{1,0:T(8,128)(2,1)}, u32[]{:S(2)}) %copy-start) | copy-done | bytes 3145752
  2.5 0.7 copy-done.2
  3.2 3.3 %shard_map.95.refs_4_ = bf16[768,640]{1,0:T(8,128)(2,1)} custom-call(s32[1,768]{1,0:T(1,128)S(1)} %copy-done.2, bf16[1536,1024]{1,0:T(8,128)(2,1)S(1)} %copy-done), custom_call_target="tpu_custom_call" | custom-call | flops 1509949440 | bytes 2949120 | tf_op jit(solution)/shard_map/pallas_call | solution.py:64
  6.6 2.2 %collective-permute-start = (bf16[768,640]{1,0:T(8,128)(2,1)}, bf16[768,640]{1,0:T(8,128)(2,1)}, u32[]{:S(2)}, u32[]{:S(2)}) collective-permute-start(bf16[768,640]{1,0:T(8,128)(2,1)} %shard_map.95.refs_4_), channel_id=1, source_target_pairs={{0,128},{128,0},{2,130},{130,2},{1,129},{129,1},{3,131},{131,3},{4... | collective-permute-start | bytes 2949128 | tf_op jit(solution)/shard_map/ppermute | solution.py:33
  8.7 0.7 collective-permute-start.1
  10.2 2.8 %shard_map.96 = bf16[448,768]{1,0:T(8,128)(2,1)S(1)} custom-call(s32[2]{0:T(128)S(1)} %get-tuple-element.60.plan, s32[1,768]{1,0:T(1,128)S(1)} %copy-done.3, f32[1,1536]{1,0:T(1,128)S(1)} %broadcast_in_dim.33.benefit_ref, f32[1,1536]{1,0:T(1,128)S(1)} %broadcast_in_dim.34.present_ref, f32[1,1536]{1,0:T(1,128)S(1)} %broadcast_in_dim.35.behaviour_ref, ...), custom_call_target="tpu_custom_call" | custom-call | flops 1056964608 | bytes 2064384 | tf_op jit(solution)/shard_map/pallas_call | solution.py:99
  13.0 2.8 %shard_map.97.refs_0_ = bf16[448,768]{1,0:T(8,128)(2,1)S(1)} custom-call(s32[2]{0:T(128)S(1)} %get-tuple-element.61.plan, s32[1,768]{1,0:T(1,128)S(1)} %copy-done.3, f32[1,1536]{1,0:T(1,128)S(1)} %broadcast_in_dim.33.benefit_ref, f32[1,1536]{1,0:T(1,128)S(1)} %broadcast_in_dim.34.present_ref, f32[1,1536]{1,0:T(1,128)S(1)} %broadcast_in_dim.35.behaviour_ref, ...), custom_call_target="tpu_custom_call" | custom-call | flops 1056964608 | bytes 2064384 | tf_op jit(solution)/shard_map/pallas_call | solution.py:99
  15.8 14.5 %collective-permute-done.refs_5_ = bf16[768,640]{1,0:T(8,128)(2,1)} collective-permute-done((bf16[768,640]{1,0:T(8,128)(2,1)}, bf16[768,640]{1,0:T(8,128)(2,1)}, u32[]{:S(2)}, u32[]{:S(2)}) %collective-permute-start) | collective-permute-done | bytes 983072 | tf_op jit(solution)/shard_map/ppermute | solution.py:33
  30.4 0.9 collective-permute-done.1.refs_3_
  31.2 2.1 %collective-permute-start.2 = (bf16[448,768]{1,0:T(8,128)(2,1)S(1)}, bf16[448,768]{1,0:T(8,128)(2,1)S(1)}, u32[]{:S(2)}, u32[]{:S(2)}) collective-permute-start(bf16[448,768]{1,0:T(8,128)(2,1)S(1)} %shard_map.96), channel_id=1, source_target_pairs={{0,128},{128,0},{2,130},{130,2},{1,129},{129,1},{3,131},{131,3},{4... | collective-permute-start | bytes 2064392 | tf_op jit(solution)/shard_map/ppermute | solution.py:33
  33.3 1.6 collective-permute-start.5
  34.9 12.5 %collective-permute-done.2.refs_1_ = bf16[448,768]{1,0:T(8,128)(2,1)S(1)} collective-permute-done((bf16[448,768]{1,0:T(8,128)(2,1)S(1)}, bf16[448,768]{1,0:T(8,128)(2,1)S(1)}, u32[]{:S(2)}, u32[]{:S(2)}) %collective-permute-start.2) | collective-permute-done | bytes 688160 | tf_op jit(solution)/shard_map/ppermute | solution.py:33
  47.4 1.7 shard_map.99.refs_1_
  49.1 0.4 collective-permute-done.4.refs_3_
  49.5 3.8 %shard_map.98 = (bf16[896,640]{1,0:T(8,128)(2,1)S(1)}, bf16[896,1536]{1,0:T(8,128)(2,1)S(1)}) custom-call(bf16[448,768]{1,0:T(8,128)(2,1)S(1)} %shard_map.97.refs_0_, bf16[448,768]{1,0:T(8,128)(2,1)S(1)} %collective-permute-done.2.refs_1_, bf16[448,768]{1,0:T(8,128)(2,1)S(1)} %collective-permute-done.3.refs_2_, ...), custom_call_target="tpu_custom_call" | custom-call | flops 1761607680 | bytes 6291456 | tf_op jit(solution)/shard_map/pallas_call | solution.py:157
  53.3 2.0 %collective-permute-done.5.refs_2_ = bf16[768,640]{1,0:T(8,128)(2,1)S(1)} collective-permute-done((bf16[768,640]{1,0:T(8,128)(2,1)}, bf16[768,640]{1,0:T(8,128)(2,1)S(1)}, u32[]{:S(2)}, u32[]{:S(2)}) %collective-permute-start.5) | collective-permute-done | bytes 983072 | tf_op jit(solution)/shard_map/ppermute | solution.py:33
  55.4 1.7 %collective-permute-start.11 = (bf16[768,384]{1,0:T(8,128)(2,1)S(1)}, bf16[768,384]{1,0:T(8,128)(2,1)S(1)}, u32[]{:S(2)}, u32[]{:S(2)}) collective-permute-start(bf16[768,384]{1,0:T(8,128)(2,1)S(1)} %shard_map.99.refs_1_), channel_id=1, source_target_pairs={{0,130},{128,2},{2,128},{130,0},{1,131},{129,3},{3,129},{131,1},{4... | collective-permute-start | bytes 1769480 | tf_op jit(solution)/shard_map/ppermute | solution.py:33
  57.1 2.1 %collective-permute-start.10 = (bf16[768,384]{1,0:T(8,128)(2,1)S(1)}, bf16[768,384]{1,0:T(8,128)(2,1)S(1)}, u32[]{:S(2)}, u32[]{:S(2)}) collective-permute-start(bf16[768,384]{1,0:T(8,128)(2,1)S(1)} %shard_map.99.refs_1_), channel_id=1, source_target_pairs={{0,128},{128,0},{2,130},{130,2},{1,129},{129,1},{3,131},{131,3},{4... | collective-permute-start | bytes 1769480 | tf_op jit(solution)/shard_map/ppermute | solution.py:33
  59.2 3.9 %shard_map.100 = (bf16[448,640]{1,0:T(8,128)(2,1)S(1)}, bf16[448,640]{1,0:T(8,128)(2,1)S(1)}, bf16[448,640]{1,0:T(8,128)(2,1)S(1)}, bf16[448,640]{1,0:T(8,128)(2,1)S(1)}) custom-call(bf16[896,1536]{1,0:T(8,128)(2,1)S(1)} %get-tuple-element.36.refs_0_, bf16[896,640]{1,0:T(8,128)(2,1)S(1)} %get-tuple-element.38.refs_1_, ...), custom_call_target="tpu_custom_call" | custom-call | flops 2642411520 | bytes 8388608 | tf_op jit(solution)/shard_map/pallas_call | solution.py:199
  63.1 0.8 collective-permute-start.6
  63.9 2.5 %collective-permute-start.8 = (bf16[448,640]{1,0:T(8,128)(2,1)S(1)}, bf16[448,640]{1,0:T(8,128)(2,1)S(1)}, u32[]{:S(2)}, u32[]{:S(2)}) collective-permute-start(bf16[448,640]{1,0:T(8,128)(2,1)S(1)} %get-tuple-element.43), channel_id=1, source_target_pairs={{0,64},{1,32},{32,65},{33,97},{64,0},{65,96},{96,1},{97,33},{2,66}... | collective-permute-start | bytes 1720328 | tf_op jit(solution)/shard_map/ppermute | solution.py:47
  66.4 2.6 %collective-permute-done.11.refs_5_ = bf16[768,384]{1,0:T(8,128)(2,1)S(1)} collective-permute-done((bf16[768,384]{1,0:T(8,128)(2,1)S(1)}, bf16[768,384]{1,0:T(8,128)(2,1)S(1)}, u32[]{:S(2)}, u32[]{:S(2)}) %collective-permute-start.11) | collective-permute-done | bytes 589856 | tf_op jit(solution)/shard_map/ppermute | solution.py:33
  69.0 3.0 %collective-permute-start.12 = (bf16[384,384]{1,0:T(8,128)(2,1)S(1)}, bf16[384,384]{1,0:T(8,128)(2,1)S(1)}, u32[]{:S(2)}, u32[]{:S(2)}) collective-permute-start(bf16[384,384]{1,0:T(8,128)(2,1)S(1)} %slice.8), channel_id=1, source_target_pairs={{0,128},{128,0},{2,130},{130,2},{1,129},{129,1},{3,131},{131,3},{4... | collective-permute-start | bytes 884744 | tf_op jit(solution)/shard_map/ppermute | solution.py:33
  72.1 1.8 %collective-permute-start.13 = (bf16[384,384]{1,0:T(8,128)(2,1)S(1)}, bf16[384,384]{1,0:T(8,128)(2,1)S(1)}, u32[]{:S(2)}, u32[]{:S(2)}) collective-permute-start(bf16[384,384]{1,0:T(8,128)(2,1)S(1)} %slice.9), channel_id=1, source_target_pairs={{0,130},{128,2},{2,128},{130,0},{1,131},{129,3},{3,129},{131,1},{4... | collective-permute-start | bytes 884744 | tf_op jit(solution)/shard_map/ppermute | solution.py:33
  73.9 6.3 %collective-permute-done.6.refs_6_.refs_0_ = bf16[448,640]{1,0:T(8,128)(2,1)S(1)} collective-permute-done((bf16[448,640]{1,0:T(8,128)(2,1)S(1)}, bf16[448,640]{1,0:T(8,128)(2,1)S(1)}, u32[]{:S(2)}, u32[]{:S(2)}) %collective-permute-start.6) | collective-permute-done | bytes 573472 | tf_op jit(solution)/shard_map/ppermute | solution.py:47
  80.2 0.7 collective-permute-start.9
  81.0 3.1 %shard_map.101 = (bf16[448,384]{1,0:T(8,128)(2,1)S(1)}, bf16[448,384]{1,0:T(8,128)(2,1)S(1)}, bf16[448,384]{1,0:T(8,128)(2,1)S(1)}, bf16[448,384]{1,0:T(8,128)(2,1)S(1)}) custom-call(bf16[896,1536]{1,0:T(8,128)(2,1)S(1)} %get-tuple-element.36.refs_0_, bf16[768,384]{1,0:T(8,128)(2,1)S(1)} %shard_map.99.refs_1_, ...), custom_call_target="tpu_custom_call" | custom-call | flops 2113929216 | bytes 8388608 | tf_op jit(solution)/shard_map/pallas_call | solution.py:199
  84.1 4.2 %collective-permute-start.14 = (bf16[448,384]{1,0:T(8,128)(2,1)S(1)}, bf16[448,384]{1,0:T(8,128)(2,1)S(1)}, u32[]{:S(2)}, u32[]{:S(2)}) collective-permute-start(bf16[448,384]{1,0:T(8,128)(2,1)S(1)} %get-tuple-element.46), channel_id=1, source_target_pairs={{0,65},{1,33},{32,64},{33,96},{64,1},{65,97},{96,0},{97,32},{2,67}... | collective-permute-start | bytes 1032200 | tf_op jit(solution)/shard_map/ppermute | solution.py:47
  88.3 2.9 %collective-permute-start.16 = (bf16[448,384]{1,0:T(8,128)(2,1)S(1)}, bf16[448,384]{1,0:T(8,128)(2,1)S(1)}, u32[]{:S(2)}, u32[]{:S(2)}) collective-permute-start(bf16[448,384]{1,0:T(8,128)(2,1)S(1)} %get-tuple-element.48), channel_id=1, source_target_pairs={{0,64},{1,32},{32,65},{33,97},{64,0},{65,96},{96,1},{97,33},{2,66}... | collective-permute-start | bytes 1032200 | tf_op jit(solution)/shard_map/ppermute | solution.py:47
  91.2 0.3 collective-permute-done.8.refs_2_
  91.5 0.8 collective-permute-start.17
  92.4 7.1 %collective-permute-done.14.refs_5_ = bf16[448,384]{1,0:T(8,128)(2,1)S(1)} collective-permute-done((bf16[448,384]{1,0:T(8,128)(2,1)S(1)}, bf16[448,384]{1,0:T(8,128)(2,1)S(1)}, u32[]{:S(2)}, u32[]{:S(2)}) %collective-permute-start.14) | collective-permute-done | bytes 344096 | tf_op jit(solution)/shard_map/ppermute | solution.py:47
  99.5 2.7 %collective-permute-done.15.refs_6_ = bf16[448,384]{1,0:T(8,128)(2,1)S(1)} collective-permute-done((bf16[448,384]{1,0:T(8,128)(2,1)S(1)}, bf16[448,384]{1,0:T(8,128)(2,1)S(1)}, u32[]{:S(2)}, u32[]{:S(2)}) %collective-permute-start.15) | collective-permute-done | bytes 344096 | tf_op jit(solution)/shard_map/ppermute | solution.py:47
  102.2 3.2 %collective-permute-done.16.refs_7_ = bf16[448,384]{1,0:T(8,128)(2,1)S(1)} collective-permute-done((bf16[448,384]{1,0:T(8,128)(2,1)S(1)}, bf16[448,384]{1,0:T(8,128)(2,1)S(1)}, u32[]{:S(2)}, u32[]{:S(2)}) %collective-permute-start.16) | collective-permute-done | bytes 344096 | tf_op jit(solution)/shard_map/ppermute | solution.py:47
  105.4 0.8 shard_map.102
  106.2 7.5 %collective-permute-start.18 = (bf16[8,56,128]{2,1,0:T(8,128)(2,1)S(1)}, bf16[8,56,128]{2,1,0:T(8,128)(2,1)S(1)}, u32[]{:S(2)}, u32[]{:S(2)}) collective-permute-start(bf16[8,56,128]{2,1,0:T(8,128)(2,1)S(1)} %get-tuple-element.51), channel_id=1, source_target_pairs={{0,16},{4,20},{8,24},{12,28},{16,0},{20,4},{24,8},{28,12},{1,17},{... | collective-permute-start | bytes 344072 | tf_op jit(solution)/shard_map/ppermute | solution.py:37
  113.7 1.9 %collective-permute-start.19 = (bf16[8,56,128]{2,1,0:T(8,128)(2,1)S(1)}, bf16[8,56,128]{2,1,0:T(8,128)(2,1)S(1)}, u32[]{:S(2)}, u32[]{:S(2)}) collective-permute-start(bf16[8,56,128]{2,1,0:T(8,128)(2,1)S(1)} %get-tuple-element.52), channel_id=1, source_target_pairs={{0,12},{4,16},{8,20},{12,24},{16,28},{20,0},{24,4},{28,8},{1,13},{... | collective-permute-start | bytes 344072 | tf_op jit(solution)/shard_map/ppermute | solution.py:37
  115.6 3.1 %collective-permute-start.20 = (bf16[8,56,128]{2,1,0:T(8,128)(2,1)S(1)}, bf16[8,56,128]{2,1,0:T(8,128)(2,1)S(1)}, u32[]{:S(2)}, u32[]{:S(2)}) collective-permute-start(bf16[8,56,128]{2,1,0:T(8,128)(2,1)S(1)} %get-tuple-element.53), channel_id=1, source_target_pairs={{0,20},{4,24},{8,28},{12,0},{16,4},{20,8},{24,12},{28,16},{1,21},{... | collective-permute-start | bytes 344072 | tf_op jit(solution)/shard_map/ppermute | solution.py:37
  118.8 1.5 collective-permute-start.21
  120.3 2.6 %collective-permute-start.22 = (bf16[8,56,128]{2,1,0:T(8,128)(2,1)S(1)}, bf16[8,56,128]{2,1,0:T(8,128)(2,1)S(1)}, u32[]{:S(2)}, u32[]{:S(2)}) collective-permute-start(bf16[8,56,128]{2,1,0:T(8,128)(2,1)S(1)} %get-tuple-element.55), channel_id=1, source_target_pairs={{0,24},{4,28},{8,0},{12,4},{16,8},{20,12},{24,16},{28,20},{1,25},{... | collective-permute-start | bytes 344072 | tf_op jit(solution)/shard_map/ppermute | solution.py:37
  122.9 1.0 collective-permute-start.23
  123.9 6.0 %collective-permute-done.19 = bf16[8,56,128]{2,1,0:T(8,128)(2,1)S(1)} collective-permute-done((bf16[8,56,128]{2,1,0:T(8,128)(2,1)S(1)}, bf16[8,56,128]{2,1,0:T(8,128)(2,1)S(1)}, u32[]{:S(2)}, u32[]{:S(2)}) %collective-permute-start.19) | collective-permute-done | bytes 114720 | tf_op jit(solution)/shard_map/ppermute | solution.py:37
  130.0 3.5 %collective-permute-done.22 = bf16[8,56,128]{2,1,0:T(8,128)(2,1)S(1)} collective-permute-done((bf16[8,56,128]{2,1,0:T(8,128)(2,1)S(1)}, bf16[8,56,128]{2,1,0:T(8,128)(2,1)S(1)}, u32[]{:S(2)}, u32[]{:S(2)}) %collective-permute-start.22) | collective-permute-done | bytes 114720 | tf_op jit(solution)/shard_map/ppermute | solution.py:37
  133.5 1.5 collective-permute-done.23
  135.0 1.0 collective-permute-done.24
  136.1 0.8 fusion.3
  136.9 4.4 %all-to-all-start = ((f32[8,56,128]{2,1,0:T(8,128)}), f32[8,56,128]{2,1,0:T(8,128)S(1)}, u32[]{:S(2)}, u32[]{:S(2)}) async-start(f32[8,56,128]{2,1,0:T(8,128)} %get-tuple-element.59), calls=%async_computation | async-start | bytes 458752 | tf_op jit(solution)/shard_map/all_to_all | solution.py:382
  141.5 1.3 collective-permute-start.29
  142.8 2.4 %collective-permute-start.30 = (bf16[8,56,128]{2,1,0:T(8,128)(2,1)S(1)}, bf16[8,56,128]{2,1,0:T(8,128)(2,1)S(1)}, u32[]{:S(2)}, u32[]{:S(2)}) collective-permute-start(bf16[8,56,128]{2,1,0:T(8,128)(2,1)S(1)} %get-tuple-element.58.refs_0_), channel_id=1, source_target_pairs={{0,64},{32,96},{64,0},{96,32},{1,65},{33,97},{65,1},{97,33},{2,66}... | collective-permute-start | bytes 344072 | tf_op jit(solution)/shard_map/ppermute | solution.py:37
  145.2 0.8 collective-permute-start.31
  146.0 0.5 fusion.place
  146.6 3.7 %collective-permute-done.29.refs_1_ = bf16[8,56,128]{2,1,0:T(8,128)(2,1)S(1)} collective-permute-done((bf16[8,56,128]{2,1,0:T(8,128)(2,1)S(1)}, bf16[8,56,128]{2,1,0:T(8,128)(2,1)S(1)}, u32[]{:S(2)}, u32[]{:S(2)}) %collective-permute-start.29) | collective-permute-done | bytes 114720 | tf_op jit(solution)/shard_map/ppermute | solution.py:37
  150.3 0.6 collective-permute-done.31.refs_3_
  150.9 0.6 copy-done.8
  151.6 2.2 %shard_map.104 = bf16[8,56,128]{2,1,0:T(8,128)(2,1)} custom-call(s32[8]{0:T(128)} %fusion.place, bf16[8,56,128]{2,1,0:T(8,128)(2,1)} %copy-done.5, bf16[8,56,128]{2,1,0:T(8,128)(2,1)} %copy-done.6, bf16[8,56,128]{2,1,0:T(8,128)(2,1)} %copy-done.7, bf16[8,56,128]{2,1,0:T(8,128)(2,1)} %copy-done.8), custom_call_target="tpu_custom_call" | custom-call | tf_op jit(solution)/shard_map/pallas_call | solution.py:271
  153.8 6.9 %all-to-all-start.1 = ((bf16[8,56,128]{2,1,0:T(8,128)(2,1)}), bf16[8,56,128]{2,1,0:T(8,128)(2,1)S(1)}, u32[]{:S(2)}, u32[]{:S(2)}) async-start(bf16[8,56,128]{2,1,0:T(8,128)(2,1)} %shard_map.104), calls=%async_computation.1 | async-start | bytes 229376 | tf_op jit(solution)/shard_map/all_to_all | solution.py:380
  160.7 0.6 convolution_bitcast_fusion
  161.4 1.2 collective-permute-done.25
  162.7 0.2 collective-permute-start.26
  162.9 2.4 %collective-permute-start.27 = (f32[128,128]{1,0:T(8,128)S(1)}, f32[128,128]{1,0:T(8,128)S(1)}, u32[]{:S(2)}, u32[]{:S(2)}) collective-permute-start(f32[128,128]{1,0:T(8,128)S(1)} %add.55.refs_1_), channel_id=1, source_target_pairs={{0,128},{128,0},{2,130},{130,2},{1,129},{129,1},{3,131},{131,3},{4... | collective-permute-start | bytes 196616 | tf_op jit(solution)/shard_map/ppermute | solution.py:33
  165.2 1.6 collective-permute-start.28
  166.9 2.8 %all-to-all-done.1 = bf16[8,56,128]{2,1,0:T(8,128)(2,1)S(1)} async-done(((bf16[8,56,128]{2,1,0:T(8,128)(2,1)}), bf16[8,56,128]{2,1,0:T(8,128)(2,1)S(1)}, u32[]{:S(2)}, u32[]{:S(2)}) %all-to-all-start.1) | async-done | bytes 114720 | tf_op jit(solution)/shard_map/all_to_all | solution.py:380
  169.6 0.7 convert_bitcast_fusion
  170.3 2.2 %shard_map.103 = bf16[448,128]{1,0:T(8,128)(2,1)} custom-call(f32[448,128]{1,0:T(8,128)S(1)} %bitcast.18, f32[128,128]{1,0:T(8,128)S(1)} %add.55.refs_1_, f32[128,128]{1,0:T(8,128)S(1)} %collective-permute-done.26.refs_2_, f32[128,128]{1,0:T(8,128)S(1)} %collective-permute-done.27.refs_3_, f32[128,128]{1,0:T(8,128)S(1)} %collective-permute-done.28.refs_4_), custom_call_target="tpu_custom_call" | custom-call | tf_op jit(solution)/shard_map/pallas_call | solution.py:303
  (53 shorter events, 0.6 us)
Async XLA Ops:
  0.6 1.9 %copy-start = (bf16[1536,1024]{1,0:T(8,128)(2,1)S(1)}, bf16[1536,1024]{1,0:T(8,128)(2,1)}, u32[]{:S(2)}) copy-start(bf16[1536,1024]{1,0:T(8,128)(2,1)} %refs_1_.3) | copy-start | bytes 9437188
  2.5 0.7 copy-start.2
  3.2 6.9 %copy-start.9 = (f32[1536]{0:T(1024)S(1)}, f32[1536]{0:T(1024)}, u32[]{:S(2)}) copy-start(f32[1536]{0:T(1024)} %param.10) | copy-start | bytes 18436
  3.2 6.9 %copy-start.10 = (f32[1536]{0:T(1024)S(1)}, f32[1536]{0:T(1024)}, u32[]{:S(2)}) copy-start(f32[1536]{0:T(1024)} %param.11) | copy-start | bytes 18436
  3.2 6.9 %copy-start.11 = (f32[1536]{0:T(1024)S(1)}, f32[1536]{0:T(1024)}, u32[]{:S(2)}) copy-start(f32[1536]{0:T(1024)} %param.12) | copy-start | bytes 18436
  3.2 7.0 %copy-start.3 = (s32[1,768]{1,0:T(1,128)S(1)}, s32[1,768]{1,0:T(1,128)}, u32[]{:S(2)}) copy-start(s32[1,768]{1,0:T(1,128)} %refs_0_.3) | copy-start | bytes 9220
  3.2 7.0 %copy-start.4 = (bf16[1536,2,448]{0,2,1:T(8,128)(2,1)S(1)}, bf16[1536,2,448]{0,2,1:T(8,128)(2,1)}, u32[]{:S(2)}) copy-start(bf16[1536,2,448]{0,2,1:T(8,128)(2,1)} %param.9) | copy-start | bytes 8257540
  6.6 23.8 %collective-permute-start = (bf16[768,640]{1,0:T(8,128)(2,1)}, bf16[768,640]{1,0:T(8,128)(2,1)}, u32[]{:S(2)}, u32[]{:S(2)}) collective-permute-start(bf16[768,640]{1,0:T(8,128)(2,1)} %shard_map.95.refs_4_), channel_id=1, source_target_pairs={{0,128},{128,0},{2,130},{130,2},{1,129},{129,1},{3,131},{131,3},{4... | collective-permute-start | bytes 2949128 | tf_op jit(solution)/shard_map/ppermute | solution.py:33
  8.7 22.5 %collective-permute-start.1 = (bf16[768,640]{1,0:T(8,128)(2,1)}, bf16[768,640]{1,0:T(8,128)(2,1)}, u32[]{:S(2)}, u32[]{:S(2)}) collective-permute-start(bf16[768,640]{1,0:T(8,128)(2,1)} %shard_map.95.refs_4_), channel_id=1, source_target_pairs={{0,130},{128,2},{2,128},{130,0},{1,131},{129,3},{3,129},{131,1},{4... | collective-permute-start | bytes 2949128 | tf_op jit(solution)/shard_map/ppermute | solution.py:33
  13.0 34.4 %copy-start.1 = (bf16[1536,1024]{1,0:T(8,128)(2,1)S(1)}, bf16[1536,1024]{1,0:T(8,128)(2,1)}, u32[]{:S(2)}) copy-start(bf16[1536,1024]{1,0:T(8,128)(2,1)} %refs_1_.3) | copy-start | bytes 9437188
  31.2 16.2 %collective-permute-start.2 = (bf16[448,768]{1,0:T(8,128)(2,1)S(1)}, bf16[448,768]{1,0:T(8,128)(2,1)S(1)}, u32[]{:S(2)}, u32[]{:S(2)}) collective-permute-start(bf16[448,768]{1,0:T(8,128)(2,1)S(1)} %shard_map.96), channel_id=1, source_target_pairs={{0,128},{128,0},{2,130},{130,2},{1,129},{129,1},{3,131},{131,3},{4... | collective-permute-start | bytes 2064392 | tf_op jit(solution)/shard_map/ppermute | solution.py:33
  33.3 22.1 %collective-permute-start.5 = (bf16[768,640]{1,0:T(8,128)(2,1)}, bf16[768,640]{1,0:T(8,128)(2,1)S(1)}, u32[]{:S(2)}, u32[]{:S(2)}) collective-permute-start(bf16[768,640]{1,0:T(8,128)(2,1)} %collective-permute-done.refs_5_), channel_id=1, source_target_pairs={{0,130},{128,2},{2,128},{130,0},{1,131},{129,3},{3,129},{131,1},{4... | collective-permute-start | bytes 2949128 | tf_op jit(solution)/shard_map/ppermute | solution.py:33
  34.9 14.2 %collective-permute-start.3 = (bf16[448,768]{1,0:T(8,128)(2,1)S(1)}, bf16[448,768]{1,0:T(8,128)(2,1)S(1)}, u32[]{:S(2)}, u32[]{:S(2)}) collective-permute-start(bf16[448,768]{1,0:T(8,128)(2,1)S(1)} %shard_map.97.refs_0_), channel_id=1, source_target_pairs={{0,1},{1,0},{2,3},{3,2},{4,5},{5,4},{6,7},{7,6},{8,9},{9,8},{10,11... | collective-permute-start | bytes 2064392 | tf_op jit(solution)/shard_map/ppermute | solution.py:37
  47.4 2.1 %collective-permute-start.4 = (bf16[448,768]{1,0:T(8,128)(2,1)S(1)}, bf16[448,768]{1,0:T(8,128)(2,1)S(1)}, u32[]{:S(2)}, u32[]{:S(2)}) collective-permute-start(bf16[448,768]{1,0:T(8,128)(2,1)S(1)} %collective-permute-done.2.refs_1_), channel_id=1, source_target_pairs={{0,1},{1,0},{2,3},{3,2},{4,5},{5,4},{6,7},{7,6},{8,9},{9,8},{10,11... | collective-permute-start | bytes 2064392 | tf_op jit(solution)/shard_map/ppermute | solution.py:37
  55.4 13.6 %collective-permute-start.11 = (bf16[768,384]{1,0:T(8,128)(2,1)S(1)}, bf16[768,384]{1,0:T(8,128)(2,1)S(1)}, u32[]{:S(2)}, u32[]{:S(2)}) collective-permute-start(bf16[768,384]{1,0:T(8,128)(2,1)S(1)} %shard_map.99.refs_1_), channel_id=1, source_target_pairs={{0,130},{128,2},{2,128},{130,0},{1,131},{129,3},{3,129},{131,1},{4... | collective-permute-start | bytes 1769480 | tf_op jit(solution)/shard_map/ppermute | solution.py:33
  57.1 14.9 %collective-permute-start.10 = (bf16[768,384]{1,0:T(8,128)(2,1)S(1)}, bf16[768,384]{1,0:T(8,128)(2,1)S(1)}, u32[]{:S(2)}, u32[]{:S(2)}) collective-permute-start(bf16[768,384]{1,0:T(8,128)(2,1)S(1)} %shard_map.99.refs_1_), channel_id=1, source_target_pairs={{0,128},{128,0},{2,130},{130,2},{1,129},{129,1},{3,131},{131,3},{4... | collective-permute-start | bytes 1769480 | tf_op jit(solution)/shard_map/ppermute | solution.py:33
  63.1 17.1 %collective-permute-start.6 = (bf16[448,640]{1,0:T(8,128)(2,1)S(1)}, bf16[448,640]{1,0:T(8,128)(2,1)S(1)}, u32[]{:S(2)}, u32[]{:S(2)}) collective-permute-start(bf16[448,640]{1,0:T(8,128)(2,1)S(1)} %get-tuple-element.41), channel_id=1, source_target_pairs={{0,65},{1,33},{32,64},{33,96},{64,1},{65,97},{96,0},{97,32},{2,67}... | collective-permute-start | bytes 1720328 | tf_op jit(solution)/shard_map/ppermute | solution.py:47
  63.9 24.4 %collective-permute-start.7 = (bf16[448,640]{1,0:T(8,128)(2,1)S(1)}, bf16[448,640]{1,0:T(8,128)(2,1)S(1)}, u32[]{:S(2)}, u32[]{:S(2)}) collective-permute-start(bf16[448,640]{1,0:T(8,128)(2,1)S(1)} %get-tuple-element.42), channel_id=1, source_target_pairs={{0,1},{1,97},{32,0},{33,32},{64,65},{65,33},{96,64},{97,96},{2,3},... | collective-permute-start | bytes 1720328 | tf_op jit(solution)/shard_map/ppermute | solution.py:47
  63.9 27.6 %collective-permute-start.8 = (bf16[448,640]{1,0:T(8,128)(2,1)S(1)}, bf16[448,640]{1,0:T(8,128)(2,1)S(1)}, u32[]{:S(2)}, u32[]{:S(2)}) collective-permute-start(bf16[448,640]{1,0:T(8,128)(2,1)S(1)} %get-tuple-element.43), channel_id=1, source_target_pairs={{0,64},{1,32},{32,65},{33,97},{64,0},{65,96},{96,1},{97,33},{2,66}... | collective-permute-start | bytes 1720328 | tf_op jit(solution)/shard_map/ppermute | solution.py:47
  69.0 11.9 %collective-permute-start.12 = (bf16[384,384]{1,0:T(8,128)(2,1)S(1)}, bf16[384,384]{1,0:T(8,128)(2,1)S(1)}, u32[]{:S(2)}, u32[]{:S(2)}) collective-permute-start(bf16[384,384]{1,0:T(8,128)(2,1)S(1)} %slice.8), channel_id=1, source_target_pairs={{0,128},{128,0},{2,130},{130,2},{1,129},{129,1},{3,131},{131,3},{4... | collective-permute-start | bytes 884744 | tf_op jit(solution)/shard_map/ppermute | solution.py:33
  72.1 8.9 %collective-permute-start.13 = (bf16[384,384]{1,0:T(8,128)(2,1)S(1)}, bf16[384,384]{1,0:T(8,128)(2,1)S(1)}, u32[]{:S(2)}, u32[]{:S(2)}) collective-permute-start(bf16[384,384]{1,0:T(8,128)(2,1)S(1)} %slice.9), channel_id=1, source_target_pairs={{0,130},{128,2},{2,128},{130,0},{1,131},{129,3},{3,129},{131,1},{4... | collective-permute-start | bytes 884744 | tf_op jit(solution)/shard_map/ppermute | solution.py:33
  80.2 12.1 %collective-permute-start.9 = (bf16[448,640]{1,0:T(8,128)(2,1)S(1)}, bf16[448,640]{1,0:T(8,128)(2,1)S(1)}, u32[]{:S(2)}, u32[]{:S(2)}) collective-permute-start(bf16[448,640]{1,0:T(8,128)(2,1)S(1)} %get-tuple-element.44.refs_4_), channel_id=1, source_target_pairs={{1,96},{32,1},{65,32},{96,65},{3,98},{34,3},{67,34},{98,67},{5,100... | collective-permute-start | bytes 1720328 | tf_op jit(solution)/shard_map/ppermute | solution.py:47
  84.1 15.4 %collective-permute-start.14 = (bf16[448,384]{1,0:T(8,128)(2,1)S(1)}, bf16[448,384]{1,0:T(8,128)(2,1)S(1)}, u32[]{:S(2)}, u32[]{:S(2)}) collective-permute-start(bf16[448,384]{1,0:T(8,128)(2,1)S(1)} %get-tuple-element.46), channel_id=1, source_target_pairs={{0,65},{1,33},{32,64},{33,96},{64,1},{65,97},{96,0},{97,32},{2,67}... | collective-permute-start | bytes 1032200 | tf_op jit(solution)/shard_map/ppermute | solution.py:47
  88.3 13.9 %collective-permute-start.15 = (bf16[448,384]{1,0:T(8,128)(2,1)S(1)}, bf16[448,384]{1,0:T(8,128)(2,1)S(1)}, u32[]{:S(2)}, u32[]{:S(2)}) collective-permute-start(bf16[448,384]{1,0:T(8,128)(2,1)S(1)} %get-tuple-element.47), channel_id=1, source_target_pairs={{0,1},{1,97},{32,0},{33,32},{64,65},{65,33},{96,64},{97,96},{2,3},... | collective-permute-start | bytes 1032200 | tf_op jit(solution)/shard_map/ppermute | solution.py:47
  88.3 17.1 %collective-permute-start.16 = (bf16[448,384]{1,0:T(8,128)(2,1)S(1)}, bf16[448,384]{1,0:T(8,128)(2,1)S(1)}, u32[]{:S(2)}, u32[]{:S(2)}) collective-permute-start(bf16[448,384]{1,0:T(8,128)(2,1)S(1)} %get-tuple-element.48), channel_id=1, source_target_pairs={{0,64},{1,32},{32,65},{33,97},{64,0},{65,96},{96,1},{97,33},{2,66}... | collective-permute-start | bytes 1032200 | tf_op jit(solution)/shard_map/ppermute | solution.py:47
  91.5 49.8 %copy-start.12 = (s32[32]{0:T(128)S(1)}, s32[32]{0:T(128)}, u32[]{:S(2)}) copy-start(s32[32]{0:T(128)} %param.15) | copy-start | bytes 388
  91.5 13.9 %collective-permute-start.17 = (bf16[448,384]{1,0:T(8,128)(2,1)S(1)}, bf16[448,384]{1,0:T(8,128)(2,1)S(1)}, u32[]{:S(2)}, u32[]{:S(2)}) collective-permute-start(bf16[448,384]{1,0:T(8,128)(2,1)S(1)} %get-tuple-element.49.refs_9_), channel_id=1, source_target_pairs={{1,96},{32,1},{65,32},{96,65},{3,98},{34,3},{67,34},{98,67},{5,100... | collective-permute-start | bytes 1032200 | tf_op jit(solution)/shard_map/ppermute | solution.py:47
  106.2 16.7 %collective-permute-start.18 = (bf16[8,56,128]{2,1,0:T(8,128)(2,1)S(1)}, bf16[8,56,128]{2,1,0:T(8,128)(2,1)S(1)}, u32[]{:S(2)}, u32[]{:S(2)}) collective-permute-start(bf16[8,56,128]{2,1,0:T(8,128)(2,1)S(1)} %get-tuple-element.51), channel_id=1, source_target_pairs={{0,16},{4,20},{8,24},{12,28},{16,0},{20,4},{24,8},{28,12},{1,17},{... | collective-permute-start | bytes 344072 | tf_op jit(solution)/shard_map/ppermute | solution.py:37
  113.7 16.2 %collective-permute-start.19 = (bf16[8,56,128]{2,1,0:T(8,128)(2,1)S(1)}, bf16[8,56,128]{2,1,0:T(8,128)(2,1)S(1)}, u32[]{:S(2)}, u32[]{:S(2)}) collective-permute-start(bf16[8,56,128]{2,1,0:T(8,128)(2,1)S(1)} %get-tuple-element.52), channel_id=1, source_target_pairs={{0,12},{4,16},{8,20},{12,24},{16,28},{20,0},{24,4},{28,8},{1,13},{... | collective-permute-start | bytes 344072 | tf_op jit(solution)/shard_map/ppermute | solution.py:37
  115.6 14.3 %collective-permute-start.20 = (bf16[8,56,128]{2,1,0:T(8,128)(2,1)S(1)}, bf16[8,56,128]{2,1,0:T(8,128)(2,1)S(1)}, u32[]{:S(2)}, u32[]{:S(2)}) collective-permute-start(bf16[8,56,128]{2,1,0:T(8,128)(2,1)S(1)} %get-tuple-element.53), channel_id=1, source_target_pairs={{0,20},{4,24},{8,28},{12,0},{16,4},{20,8},{24,12},{28,16},{1,21},{... | collective-permute-start | bytes 344072 | tf_op jit(solution)/shard_map/ppermute | solution.py:37
  118.8 11.2 %collective-permute-start.21 = (bf16[8,56,128]{2,1,0:T(8,128)(2,1)S(1)}, bf16[8,56,128]{2,1,0:T(8,128)(2,1)S(1)}, u32[]{:S(2)}, u32[]{:S(2)}) collective-permute-start(bf16[8,56,128]{2,1,0:T(8,128)(2,1)S(1)} %get-tuple-element.54), channel_id=1, source_target_pairs={{0,8},{4,12},{8,16},{12,20},{16,24},{20,28},{24,0},{28,4},{1,9},{5... | collective-permute-start | bytes 344072 | tf_op jit(solution)/shard_map/ppermute | solution.py:37
  120.3 13.2 %collective-permute-start.22 = (bf16[8,56,128]{2,1,0:T(8,128)(2,1)S(1)}, bf16[8,56,128]{2,1,0:T(8,128)(2,1)S(1)}, u32[]{:S(2)}, u32[]{:S(2)}) collective-permute-start(bf16[8,56,128]{2,1,0:T(8,128)(2,1)S(1)} %get-tuple-element.55), channel_id=1, source_target_pairs={{0,24},{4,28},{8,0},{12,4},{16,8},{20,12},{24,16},{28,20},{1,25},{... | collective-permute-start | bytes 344072 | tf_op jit(solution)/shard_map/ppermute | solution.py:37
  122.9 12.1 %collective-permute-start.23 = (bf16[8,56,128]{2,1,0:T(8,128)(2,1)S(1)}, bf16[8,56,128]{2,1,0:T(8,128)(2,1)S(1)}, u32[]{:S(2)}, u32[]{:S(2)}) collective-permute-start(bf16[8,56,128]{2,1,0:T(8,128)(2,1)S(1)} %get-tuple-element.56), channel_id=1, source_target_pairs={{0,4},{4,8},{8,12},{12,16},{16,20},{20,24},{24,28},{28,0},{1,5},{5... | collective-permute-start | bytes 344072 | tf_op jit(solution)/shard_map/ppermute | solution.py:37
  129.9 6.1 %collective-permute-start.24 = (bf16[8,56,128]{2,1,0:T(8,128)(2,1)S(1)}, bf16[8,56,128]{2,1,0:T(8,128)(2,1)S(1)}, u32[]{:S(2)}, u32[]{:S(2)}) collective-permute-start(bf16[8,56,128]{2,1,0:T(8,128)(2,1)S(1)} %get-tuple-element.57), channel_id=1, source_target_pairs={{0,28},{4,0},{8,4},{12,8},{16,12},{20,16},{24,20},{28,24},{1,29},{... | collective-permute-start | bytes 344072 | tf_op jit(solution)/shard_map/ppermute | solution.py:37
  136.9 14.0 %copy-start.5 = (bf16[8,56,128]{2,1,0:T(8,128)(2,1)}, bf16[8,56,128]{2,1,0:T(8,128)(2,1)S(1)}, u32[]{:S(2)}) copy-start(bf16[8,56,128]{2,1,0:T(8,128)(2,1)S(1)} %get-tuple-element.58.refs_0_) | copy-start | bytes 344068
  136.9 16.9 %all-to-all-start = ((f32[8,56,128]{2,1,0:T(8,128)}), f32[8,56,128]{2,1,0:T(8,128)S(1)}, u32[]{:S(2)}, u32[]{:S(2)}) async-start(f32[8,56,128]{2,1,0:T(8,128)} %get-tuple-element.59), calls=%async_computation | async-start | bytes 458752 | tf_op jit(solution)/shard_map/all_to_all | solution.py:382
  141.5 8.7 %collective-permute-start.29 = (bf16[8,56,128]{2,1,0:T(8,128)(2,1)S(1)}, bf16[8,56,128]{2,1,0:T(8,128)(2,1)S(1)}, u32[]{:S(2)}, u32[]{:S(2)}) collective-permute-start(bf16[8,56,128]{2,1,0:T(8,128)(2,1)S(1)} %get-tuple-element.58.refs_0_), channel_id=1, source_target_pairs={{0,32},{32,64},{64,96},{96,0},{1,33},{33,65},{65,97},{97,1},{2,34}... | collective-permute-start | bytes 344072 | tf_op jit(solution)/shard_map/ppermute | solution.py:37
  142.8 7.5 %collective-permute-start.30 = (bf16[8,56,128]{2,1,0:T(8,128)(2,1)S(1)}, bf16[8,56,128]{2,1,0:T(8,128)(2,1)S(1)}, u32[]{:S(2)}, u32[]{:S(2)}) collective-permute-start(bf16[8,56,128]{2,1,0:T(8,128)(2,1)S(1)} %get-tuple-element.58.refs_0_), channel_id=1, source_target_pairs={{0,64},{32,96},{64,0},{96,32},{1,65},{33,97},{65,1},{97,33},{2,66}... | collective-permute-start | bytes 344072 | tf_op jit(solution)/shard_map/ppermute | solution.py:37
  145.2 5.6 %collective-permute-start.31 = (bf16[8,56,128]{2,1,0:T(8,128)(2,1)S(1)}, bf16[8,56,128]{2,1,0:T(8,128)(2,1)S(1)}, u32[]{:S(2)}, u32[]{:S(2)}) collective-permute-start(bf16[8,56,128]{2,1,0:T(8,128)(2,1)S(1)} %get-tuple-element.58.refs_0_), channel_id=1, source_target_pairs={{0,96},{32,0},{64,32},{96,64},{1,97},{33,1},{65,33},{97,65},{2,98}... | collective-permute-start | bytes 344072 | tf_op jit(solution)/shard_map/ppermute | solution.py:37
  150.2 0.6 copy-start.6
  150.3 0.7 copy-start.7
  150.9 0.6 copy-start.8
  153.8 15.8 %all-to-all-start.1 = ((bf16[8,56,128]{2,1,0:T(8,128)(2,1)}), bf16[8,56,128]{2,1,0:T(8,128)(2,1)S(1)}, u32[]{:S(2)}, u32[]{:S(2)}) async-start(bf16[8,56,128]{2,1,0:T(8,128)(2,1)} %shard_map.104), calls=%async_computation.1 | async-start | bytes 229376 | tf_op jit(solution)/shard_map/all_to_all | solution.py:380
  161.3 1.3 collective-permute-start.25
  162.7 7.7 %collective-permute-start.26 = (f32[128,128]{1,0:T(8,128)S(1)}, f32[128,128]{1,0:T(8,128)S(1)}, u32[]{:S(2)}, u32[]{:S(2)}) collective-permute-start(f32[128,128]{1,0:T(8,128)S(1)} %add.55.refs_1_), channel_id=1, source_target_pairs={{0,2},{128,130},{2,0},{130,128},{1,3},{129,131},{3,1},{131,129},{4... | collective-permute-start | bytes 196616 | tf_op jit(solution)/shard_map/ppermute | solution.py:33
  162.9 7.5 %collective-permute-start.27 = (f32[128,128]{1,0:T(8,128)S(1)}, f32[128,128]{1,0:T(8,128)S(1)}, u32[]{:S(2)}, u32[]{:S(2)}) collective-permute-start(f32[128,128]{1,0:T(8,128)S(1)} %add.55.refs_1_), channel_id=1, source_target_pairs={{0,128},{128,0},{2,130},{130,2},{1,129},{129,1},{3,131},{131,3},{4... | collective-permute-start | bytes 196616 | tf_op jit(solution)/shard_map/ppermute | solution.py:33
  165.2 5.1 %collective-permute-start.28 = (f32[128,128]{1,0:T(8,128)S(1)}, f32[128,128]{1,0:T(8,128)S(1)}, u32[]{:S(2)}, u32[]{:S(2)}) collective-permute-start(f32[128,128]{1,0:T(8,128)S(1)} %add.55.refs_1_), channel_id=1, source_target_pairs={{0,130},{128,2},{2,128},{130,0},{1,131},{129,3},{3,129},{131,1},{4... | collective-permute-start | bytes 196616 | tf_op jit(solution)/shard_map/ppermute | solution.py:33
